TPU v7x, 32 devices: a whole 2x2x4 slice. The times are simulated.
32 devices in a mesh: seq: 8 (over z, y), head: 4 (over x, core).
Axes of the slice: x: 2, y: 2, z: 4, core: 2. Of those that a mesh axis runs over, the one named last changes fastest.
Arguments:
- queries: bfloat16 [2, 512, 2048], P(None, 'seq', 'head'), may hold values from -6 to 6
- keys: bfloat16 [2, 512, 2048], P(None, 'seq', 'head'), may hold values from -6 to 6
- values: bfloat16 [2, 512, 2048], P(None, 'seq', 'head'), may hold values from -6 to 6
- out_weight: bfloat16 [2048, 4096], P('head'), may hold values from -0.125 to 0.125
- upstream: bfloat16 [2, 512, 4096], P(None, 'seq', 'head'), may hold values from -6 to 6
Outputs:
- output: bfloat16 [2, 512, 4096], P(None, 'seq', 'head')
- query_grad: bfloat16 [2, 512, 2048], P(None, 'seq', 'head')
- key_grad: bfloat16 [2, 512, 2048], P(None, 'seq', 'head')
- value_grad: bfloat16 [2, 512, 2048], P(None, 'seq', 'head')
- weight_grad: float32 [2048, 4096], P('head', 'seq')
All inputs are finite; a program needn't handle non-finite values.
Results may differ from a plain program's by a relative error of at most 0.01405.
Values may be sent and summed in bfloat16 or wider, within the bound.
No kernel may reach another device: no remote copies, remote signals or barrier semaphores. Data moves between devices by JAX's collectives and lax.ppermute only.
A program may use at most 128 MiB of HBM per device.

v0:
```python
import jax
import jax.numpy as jnp
from jax import lax
from jax.sharding import PartitionSpec as P

HEAD_DIM = 128


eps = 1e-06


def carried_in(shard, axis, join, neutral, backward):
    count = lax.axis_size(axis)
    place = lax.axis_index(axis)
    ahead = count - 1 - place if backward else place
    gathered = lax.all_gather(shard.astype(jnp.bfloat16), axis)
    state = jnp.zeros_like(shard) + jnp.asarray(neutral, shard.dtype)

    def one(lap, state):
        source = count - 1 - lap if backward else lap
        return join(state, lax.dynamic_index_in_dim(gathered, source, 0, False).astype(shard.dtype))

    return lax.fori_loop(0, ahead, one, state)


def add_terms(earlier, later):
    return jax.tree.map(lambda left, right: left + right, earlier, later)


def lower_mask(length):
    rows = lax.broadcasted_iota(jnp.int32, (length, length), 0)
    cols = lax.broadcasted_iota(jnp.int32, (length, length), 1)
    return rows >= cols


def on_device(queries, keys, values, out_weight, upstream):
    pair, length, width = queries.shape
    heads_here = width // HEAD_DIM
    shape_four = (pair, length, heads_here, HEAD_DIM)
    query4 = queries.reshape(shape_four)
    key4 = keys.reshape(shape_four)
    value4 = values.reshape(shape_four)
    kv_terms = jnp.einsum("pchd,pche->phde", key4, value4, preferred_element_type=jnp.float32)
    first_kv = kv_terms[0]
    second_kv = kv_terms[1]
    zero_state = jnp.zeros_like(first_kv)
    before = carried_in(first_kv, "seq", add_terms, zero_state, False)
    after = carried_in(second_kv, "seq", add_terms, zero_state, True)
    total_first = lax.psum(first_kv, "seq")
    state_second = total_first + after
    states = jnp.stack([before, state_second]).astype(jnp.bfloat16)
    mask = lower_mask(length)
    scores = jnp.einsum("pthd,pshd->phts", query4, key4, preferred_element_type=jnp.float32)
    weights = jnp.where(mask, scores, 0.0).astype(jnp.bfloat16)
    attended = jnp.einsum("phts,pshe->pthe", weights, value4, preferred_element_type=jnp.float32)
    attended = attended + jnp.einsum(
        "pthd,phde->pthe", query4, states, preferred_element_type=jnp.float32
    )
    scale = jnp.sqrt(jnp.mean(attended * attended, axis=-1, keepdims=True) + eps)
    normed = attended / scale
    hidden = normed.astype(jnp.bfloat16).reshape(pair * length, width)
    partial_out = jnp.dot(hidden, out_weight, preferred_element_type=jnp.float32)
    output = lax.psum_scatter(
        partial_out.astype(jnp.bfloat16), "head", scatter_dimension=1, tiled=True
    ).astype(jnp.float32)
    output = output.astype(jnp.bfloat16).reshape(pair, length, -1)
    flat_up = upstream.reshape(pair * length, upstream.shape[2])
    full_up = lax.all_gather(flat_up, "head", axis=1, tiled=True)
    hidden_grad = lax.dot_general(
        full_up, out_weight, (((1,), (1,)), ((), ())), preferred_element_type=jnp.float32
    )
    weight_share = lax.psum_scatter(
        lax.dot_general(
            full_up, hidden, (((0,), (0,)), ((), ())), preferred_element_type=jnp.float32
        ),
        "seq",
        scatter_dimension=0,
        tiled=True,
    )
    weight_grad = weight_share.T
    grad_four = hidden_grad.reshape(shape_four)
    inner = jnp.mean(grad_four * normed, axis=-1, keepdims=True)
    attn_grad = ((grad_four - normed * inner) / scale).astype(jnp.bfloat16)
    qg_terms = jnp.einsum("pthd,pthe->phde", query4, attn_grad, preferred_element_type=jnp.float32)
    first_qg = qg_terms[0]
    second_qg = qg_terms[1]
    higher_first = carried_in(first_qg, "seq", add_terms, zero_state, True)
    grad_second = carried_in(second_qg, "seq", add_terms, zero_state, False)
    total_second_qg = lax.psum(second_qg, "seq")
    grad_first = total_second_qg + higher_first
    later = jnp.stack([grad_first, grad_second]).astype(jnp.bfloat16)
    diffs = jnp.einsum("pthe,pshe->phts", attn_grad, value4, preferred_element_type=jnp.float32)
    diffs = jnp.where(mask, diffs, 0.0).astype(jnp.bfloat16)
    query_grad = jnp.einsum("phts,pshd->pthd", diffs, key4, preferred_element_type=jnp.float32)
    query_grad = query_grad + jnp.einsum(
        "pthe,phde->pthd", attn_grad, states, preferred_element_type=jnp.float32
    )
    key_grad = jnp.einsum("phts,pthd->pshd", diffs, query4, preferred_element_type=jnp.float32)
    key_grad = key_grad + jnp.einsum(
        "pshe,phde->pshd", value4, later, preferred_element_type=jnp.float32
    )
    value_grad = jnp.einsum(
        "phts,pthe->pshe", weights, attn_grad, preferred_element_type=jnp.float32
    )
    value_grad = value_grad + jnp.einsum(
        "pshd,phde->pshe", key4, later, preferred_element_type=jnp.float32
    )
    out_shape = (pair, length, width)
    return (
        output,
        query_grad.astype(jnp.bfloat16).reshape(out_shape),
        key_grad.astype(jnp.bfloat16).reshape(out_shape),
        value_grad.astype(jnp.bfloat16).reshape(out_shape),
        weight_grad,
    )


def solution(mesh):
    return jax.shard_map(
        on_device,
        mesh=mesh,
        in_specs=(
            P(None, "seq", "head"),
            P(None, "seq", "head"),
            P(None, "seq", "head"),
            P("head", None),
            P(None, "seq", "head"),
        ),
        out_specs=(
            P(None, "seq", "head"),
            P(None, "seq", "head"),
            P(None, "seq", "head"),
            P(None, "seq", "head"),
            P("head", "seq"),
        ),
        check_vma=False,
    )
```

profile of v0, /device:TPU:0, one launch (start us, length us, event | category | flops | bytes accessed | tf_op | source)
XLA Modules:
  0.0 532.0 jit_solution(12917790190861322981)
XLA Ops:
  7.2 0.7 all-gather.10.cloned.1.call-update
  8.0 1.2 fusion.17
  9.2 0.7 fusion.48
  10.0 0.7 all-gather.6.cloned.1.call-update
  10.8 0.7 slice_bitcast_fusion.1
  11.6 1.1 fusion.3
  12.7 1.1 convolution_bitcast_fusion.7
  13.8 15.3 %all-gather.10.cloned.1.call-done = bf16[128,4096]{1,0:T(8,128)(2,1)} async-done(((bf16[128,1024]{1,0:T(8,128)(2,1)}), bf16[128,4096]{1,0:T(8,128)(2,1)}) %all-gather.10.cloned.1.call-update) | async-done | bytes 1048592 | tf_op jit(solution)/shard_map/all_gather | solution.py:68
  29.0 4.0 fusion.49
  33.2 38.7 %all-gather.8.cloned.1.call-done = bf16[8,4,128,128]{3,2,1,0:T(8,128)(2,1)} async-done(((bf16[1,4,128,128]{3,2,1,0:T(8,128)(2,1)}), bf16[8,4,128,128]{3,2,1,0:T(8,128)(2,1)}) %all-gather.8.cloned.1.call-update) | async-done | bytes 1048592 | tf_op jit(solution)/shard_map/all_gather | solution.py:16
  71.9 6.9 %while.45 = (s32[]{:T(128)}, f32[4,128,128]{2,1,0:T(8,128)S(1)}, s32[]{:T(128)}, bf16[8,4,128,128]{3,2,1,0:T(8,128)(2,1)}, s32[]{:T(128)}, /*index=5*/s32[]{:T(128)}, s32[]{:T(128)}, s32[]{:T(128)}) while((s32[]{:T(128)}, f32[4,128,128]{2,1,0:T(8,128)S(1)}, s32[]{:T(128)}, bf16[8,4,128,128]{3,2,1,0:T(8,128)(2,1)}, s32[]{:T(128)}, ...), condition=%wide.region_4.5_spmd, body=%wide.region_3.4_spmd.sunk | while | flops 131078 | bytes 655495 | solution.py:23
  72.0 1.0 convert_add_fusion.9
  73.0 1.0 convert_add_fusion.9
  73.9 1.0 convert_add_fusion.9
  74.9 1.0 convert_add_fusion.9
  75.9 1.0 convert_add_fusion.9
  76.9 1.0 convert_add_fusion.9
  77.9 1.0 convert_add_fusion.9
  78.9 34.7 %all-gather.6.cloned.1.call-done = bf16[8,4,128,128]{3,2,1,0:T(8,128)(2,1)} async-done(((bf16[1,4,128,128]{3,2,1,0:T(8,128)(2,1)}), bf16[8,4,128,128]{3,2,1,0:T(8,128)(2,1)}) %all-gather.6.cloned.1.call-update) | async-done | bytes 1048592 | tf_op jit(solution)/shard_map/all_gather | solution.py:16
  113.6 73.0 %all-reduce.3.cloned.1.call-done = f32[4,128,128]{2,1,0:T(8,128)} async-done(((f32[4,128,128]{2,1,0:T(8,128)}), f32[4,128,128]{2,1,0:T(8,128)}) %all-reduce.3.cloned.1.call-update) | async-done | bytes 262160 | tf_op jit(solution)/shard_map/psum | solution.py:49
  186.6 1.0 fusion.11
  187.6 0.3 multiply_reduce_fusion.1
  187.9 0.3 multiply_reduce_fusion
  188.4 0.3 convolution_bitcast_fusion.1
  188.8 0.8 copy.71
  189.6 0.8 copy.73
  190.6 0.7 slice_bitcast_fusion
  191.4 4.0 convolution_convert_fusion
  195.4 4.5 convolution_bitcast_fusion
  200.0 0.9 copy-done.2
  201.2 0.3 fusion.10
  201.5 0.7 copy.156
  202.7 26.6 %all-gather.12.cloned.1.call-done = bf16[8,4,128,128]{3,2,1,0:T(8,128)(2,1)} async-done(((bf16[1,4,128,128]{3,2,1,0:T(8,128)(2,1)}), bf16[8,4,128,128]{3,2,1,0:T(8,128)(2,1)}) %all-gather.12.cloned.1.call-update) | async-done | bytes 1048592 | tf_op jit(solution)/shard_map/all_gather | solution.py:16
  229.3 6.9 %while.46 = (s32[]{:T(128)}, f32[4,128,128]{2,1,0:T(8,128)S(1)}, s32[]{:T(128)}, bf16[8,4,128,128]{3,2,1,0:T(8,128)(2,1)}, s32[]{:T(128)}, /*index=5*/s32[]{:T(128)}, s32[]{:T(128)}, s32[]{:T(128)}) while((s32[]{:T(128)}, f32[4,128,128]{2,1,0:T(8,128)S(1)}, s32[]{:T(128)}, bf16[8,4,128,128]{3,2,1,0:T(8,128)(2,1)}, s32[]{:T(128)}, ...), condition=%wide.region_10.11_spmd, body=%wide.region_9.10_spmd.sunk | while | flops 131078 | bytes 655495 | solution.py:23
  229.3 1.0 convert_add_fusion.10
  230.3 1.0 convert_add_fusion.10
  231.3 1.0 convert_add_fusion.10
  232.3 1.0 convert_add_fusion.10
  233.3 1.0 convert_add_fusion.10
  234.3 1.0 convert_add_fusion.10
  235.2 1.0 convert_add_fusion.10
  236.4 34.6 %all-gather.14.cloned.1.call-done = bf16[8,4,128,128]{3,2,1,0:T(8,128)(2,1)} async-done(((bf16[1,4,128,128]{3,2,1,0:T(8,128)(2,1)}), bf16[8,4,128,128]{3,2,1,0:T(8,128)(2,1)}) %all-gather.14.cloned.1.call-update) | async-done | bytes 1048592 | tf_op jit(solution)/shard_map/all_gather | solution.py:16
  271.1 72.9 %all-reduce.5.cloned.1.call-done = f32[4,128,128]{1,2,0:T(8,128)} async-done(((f32[4,128,128]{1,2,0:T(8,128)}), f32[4,128,128]{1,2,0:T(8,128)}) %all-reduce.5.cloned.1.call-update) | async-done | bytes 262160 | tf_op jit(solution)/shard_map/psum | solution.py:89
  344.0 1.0 fusion.12
  345.2 0.3 fusion.9
  345.5 0.7 copy_bitcast_fusion
  346.2 25.1 %reduce-scatter.3.cloned.1.call-done = bf16[128,1024]{1,0:T(8,128)(2,1)} async-done(((bf16[128,4096]{1,0:T(8,128)(2,1)}), bf16[128,1024]{1,0:T(8,128)(2,1)}) %reduce-scatter.3.cloned.1.call-update) | async-done | bytes 262160 | tf_op jit(solution)/shard_map/reduce_scatter | solution.py:63
  371.4 154.1 %reduce-scatter.5.cloned.1.call-done = f32[512,512]{0,1:T(8,128)} async-done(((f32[4096,512]{0,1:T(8,128)}), f32[512,512]{0,1:T(8,128)}) %reduce-scatter.5.cloned.1.call-update) | async-done | bytes 1048592 | tf_op jit(solution)/shard_map/reduce_scatter | solution.py:72
  (44 shorter events, 2.3 us)
Async XLA Ops:
  7.2 4.4 copy-start
  7.2 21.9 %all-gather.10.cloned.1.call-start = ((), (), s32[]{:S(2)}) async-start(), calls=%async_computation.6 | async-start | bytes 1310720 | tf_op jit(solution)/shard_map/all_gather | solution.py:68
  7.9 64.0 %all-gather.8.cloned.1.call-start = ((), (), s32[]{:S(2)}) async-start(), calls=%async_computation.4 | async-start | bytes 1179648 | tf_op jit(solution)/shard_map/all_gather | solution.py:16
  10.0 103.6 %all-gather.6.cloned.1.call-start = ((), (), s32[]{:S(2)}) async-start(), calls=%async_computation.2 | async-start | bytes 1179648 | tf_op jit(solution)/shard_map/all_gather | solution.py:16
  10.7 175.9 %all-reduce.3.cloned.1.call-start = ((), (), s32[]{:S(2)}) async-start(), calls=%async_computation.3 | async-start | bytes 524288 | tf_op jit(solution)/shard_map/psum | solution.py:49
  11.5 217.8 %all-gather.12.cloned.1.call-start = ((), (), s32[]{:S(2)}) async-start(), calls=%async_computation.8 | async-start | bytes 1179648 | tf_op jit(solution)/shard_map/all_gather | solution.py:16
  188.8 6.6 %copy-start.1 = (bf16[128,4096]{1,0:T(8,128)(2,1)S(1)}, bf16[128,4096]{1,0:T(8,128)(2,1)}, u32[]{:S(2)}) copy-start(bf16[128,4096]{1,0:T(8,128)(2,1)} %all-gather.10.cloned.1.call-done) | copy-start | bytes 3145732
  189.6 81.4 %all-gather.14.cloned.1.call-start = ((), (), s32[]{:S(2)}) async-start(), calls=%async_computation.9 | async-start | bytes 1179648 | tf_op jit(solution)/shard_map/all_gather | solution.py:16
  190.4 153.6 %all-reduce.5.cloned.1.call-start = ((), (), s32[]{:S(2)}) async-start(), calls=%async_computation.7 | async-start | bytes 524288 | tf_op jit(solution)/shard_map/psum | solution.py:89
  191.3 180.0 %reduce-scatter.3.cloned.1.call-start = ((), (), s32[]{:S(2)}) async-start(), calls=%async_computation.5 | async-start | bytes 1310720 | tf_op jit(solution)/shard_map/reduce_scatter | solution.py:63
  195.4 330.1 %reduce-scatter.5.cloned.1.call-start = ((), (), s32[]{:S(2)}) async-start(), calls=%async_computation.10 | async-start | bytes 9437184 | tf_op jit(solution)/shard_map/reduce_scatter | solution.py:72
  200.0 0.9 copy-start.2
  200.0 1.1 copy-start.3
Sparse Core Ops, SparseCore 0:
  9.6 19.4 all-gather.9
  31.7 40.1 all-gather.7
  74.6 38.8 all-gather.5
  117.3 69.2 all-reduce.2
  189.7 39.5 all-gather.11
  232.0 38.8 all-gather.13
  274.7 69.3 all-reduce.4
  347.1 24.1 reduce-scatter.2
  376.0 149.3 reduce-scatter.4
where the time goes:
time: 533 us; the launch traced here: 532 us
  waiting for transfers between devices  476 us (89%)
  matrix products  18.1 us (3%)
  other arithmetic  16 us (3%)
  between operations  14.1 us (3%)
  local copies, waits for them, and re-layouts  6.57 us (1%)
    reduce_scatter x1, waiting for transfers between devices, on_device(): lax.psum_scatter(lax.dot_general(full_up, hidden, (((0,), (0,)), ((), ())...  154 us
    all_gather x4, waiting for transfers between devices, carried_in(): gathered = lax.all_gather(shard.astype(jnp.bfloat16), axis)  135 us
    psum x1, waiting for transfers between devices, on_device(): total_first = lax.psum(first_kv, 'seq')  73 us
    psum x1, waiting for transfers between devices, on_device(): total_second_qg = lax.psum(second_qg, 'seq')  72.9 us
    reduce_scatter x1, waiting for transfers between devices, on_device(): lax.psum_scatter(partial_out.astype(jnp.bfloat16), 'head', scatter_dimens...  25.1 us
    all_gather x1, waiting for transfers between devices, on_device(): full_up = lax.all_gather(flat_up, 'head', axis=1, tiled=True)  15.3 us
    add x14, other arithmetic, add_terms(): return jax.tree.map(lambda left, right: left + right, earlier, later)  13.5 us
  transfers between devices with their start and end apart: 9, of which 9 were waited for; matrix products, arithmetic and copies ran while one was open for 7% of the time, Pallas kernels for 0%

commit v1 on v0

v1 whole, which is shorter than its diff:
```python
import functools

import jax
import jax.numpy as jnp
from jax import lax
from jax.experimental import pallas as pl
from jax.experimental.pallas import tpu as pltpu
from jax.sharding import PartitionSpec as P

HEAD_DIM = 128
EPS = 1e-06

NN = (((1,), (0,)), ((), ()))
NT = (((1,), (1,)), ((), ()))
TN = (((0,), (0,)), ((), ()))


def mm(a, b, dims):
    return lax.dot_general(a, b, dims, preferred_element_type=jnp.float32)


def head_cols(i):
    return slice(i * HEAD_DIM, (i + 1) * HEAD_DIM)


def lower(length):
    rows = lax.broadcasted_iota(jnp.int32, (length, length), 0)
    cols = lax.broadcasted_iota(jnp.int32, (length, length), 1)
    return rows >= cols


def xor_permute(x, axis, bit):
    count = lax.axis_size(axis)
    return lax.ppermute(x, axis, [(i, i ^ bit) for i in range(count)])


def whole(n):
    return [pl.BlockSpec(memory_space=pltpu.VMEM)] * n


def kernel_call(body, outs, args, flops=0, vmem=32 * 2**20):
    moved = sum(a.size * a.dtype.itemsize for a in list(args) + list(outs))
    return pl.pallas_call(
        body,
        out_shape=outs,
        in_specs=whole(len(args)),
        out_specs=whole(len(outs)),
        compiler_params=pltpu.CompilerParams(vmem_limit_bytes=vmem),
        cost_estimate=pl.CostEstimate(flops=flops, bytes_accessed=moved, transcendentals=0),
    )(*args)


def shaped(shape, dtype):
    return jax.ShapeDtypeStruct(shape, dtype)


def kv_body(k_ref, v_ref, own_ref, send_ref):
    for i in range(k_ref.shape[2] // HEAD_DIM):
        c = head_cols(i)
        first = mm(k_ref[0, :, c], v_ref[0, :, c], TN)
        second = mm(k_ref[1, :, c], v_ref[1, :, c], TN)
        own_ref[i] = first
        send_ref[0, i] = first.astype(jnp.bfloat16)
        send_ref[1, i] = (first + second).astype(jnp.bfloat16)


def exchange(near, send, axis):
    count = lax.axis_size(axis)
    place = lax.axis_index(axis)
    below = jnp.zeros_like(near)
    above = jnp.zeros_like(near)
    group = send.astype(jnp.float32)
    bit = 1
    while bit < count:
        upper = (place & bit) != 0
        if 2 * bit < count:
            got = xor_permute(send, axis, bit).astype(jnp.float32)
            got_near, got_both = got[0], got[1]
            group = group + got
            send = group.astype(jnp.bfloat16)
        else:
            got = xor_permute(jnp.where(upper, send[1], send[0]), axis, bit).astype(jnp.float32)
            got_near = got_both = got
        below = jnp.where(upper, below + got_near, below)
        above = jnp.where(upper, above, above + got_both)
        bit *= 2
    return below, above


def grad_body(heads, index_ref, *refs):
    chunks, w_ref, out_ref = refs[:heads], refs[heads], refs[heads + 1]
    step = pl.program_id(0)
    for m in range(heads):

        @pl.when(step == m)
        def _(m=m):
            part = mm(chunks[m][...], w_ref[...], NT)
            if m == 0:
                out_ref[...] = part
            else:
                out_ref[...] += part


def hidden_grad_of(chunks, weight, place):
    n = len(chunks)
    rows, cols = chunks[0].shape
    features = weight.shape[0]
    index = place ^ jnp.arange(n, dtype=jnp.int32)
    return pl.pallas_call(
        functools.partial(grad_body, n),
        out_shape=shaped((rows, features), jnp.float32),
        grid_spec=pltpu.PrefetchScalarGridSpec(
            num_scalar_prefetch=1,
            grid=(n,),
            in_specs=[pl.BlockSpec((rows, cols), lambda m, ix: (0, 0))] * n
            + [pl.BlockSpec((features, cols), lambda m, ix: (0, ix[m]))],
            out_specs=pl.BlockSpec((rows, features), lambda m, ix: (0, 0)),
        ),
        compiler_params=pltpu.CompilerParams(vmem_limit_bytes=32 * 2**20),
        cost_estimate=pl.CostEstimate(
            flops=2 * rows * features * cols * n,
            bytes_accessed=weight.size * 2 + n * rows * cols * 2,
            transcendentals=0,
        ),
    )(index, *chunks, weight)


def forward_body(q_ref, k_ref, v_ref, hg_ref, own_ref, below_ref, above_ref,
                 state_ref, hidden_ref, g_ref, qown_ref, qsend_ref):
    length = q_ref.shape[1]
    mask = lower(length)
    for i in range(q_ref.shape[2] // HEAD_DIM):
        c = head_cols(i)
        below = below_ref[i]
        states = (below, below + own_ref[i] + above_ref[i])
        terms = []
        for p in range(2):
            r = slice(p * length, (p + 1) * length)
            q, k, v = q_ref[p, :, c], k_ref[p, :, c], v_ref[p, :, c]
            state = states[p].astype(jnp.bfloat16)
            state_ref[p, i] = state
            weights = jnp.where(mask, mm(q, k, NT), 0.0).astype(jnp.bfloat16)
            attended = mm(weights, v, NN) + mm(q, state, NN)
            scale = jnp.sqrt(jnp.mean(attended * attended, axis=-1, keepdims=True) + EPS)
            normed = attended / scale
            hidden_ref[r, c] = normed.astype(jnp.bfloat16)
            hg = hg_ref[r, c]
            inner = jnp.mean(hg * normed, axis=-1, keepdims=True)
            g = ((hg - normed * inner) / scale).astype(jnp.bfloat16)
            g_ref[p, :, c] = g
            terms.append(mm(q, g, TN))
        qown_ref[i] = terms[1]
        qsend_ref[0, i] = terms[1].astype(jnp.bfloat16)
        qsend_ref[1, i] = (terms[0] + terms[1]).astype(jnp.bfloat16)


def inside_body(q_ref, k_ref, v_ref, g_ref, state_ref, dq_ref, dk_ref, dv_ref):
    length = q_ref.shape[1]
    mask = lower(length)
    for i in range(q_ref.shape[2] // HEAD_DIM):
        c = head_cols(i)
        for p in range(2):
            q, k, v, g = q_ref[p, :, c], k_ref[p, :, c], v_ref[p, :, c], g_ref[p, :, c]
            weights = jnp.where(mask, mm(q, k, NT), 0.0).astype(jnp.bfloat16)
            diffs = jnp.where(mask, mm(g, v, NT), 0.0).astype(jnp.bfloat16)
            dq_ref[p, :, c] = (mm(diffs, k, NN) + mm(g, state_ref[p, i], NT)).astype(jnp.bfloat16)
            dk_ref[p, :, c] = mm(diffs, q, TN)
            dv_ref[p, :, c] = mm(weights, g, TN)


def final_body(k_ref, v_ref, dkp_ref, dvp_ref, own_ref, below_ref, above_ref, dk_ref, dv_ref):
    for i in range(k_ref.shape[2] // HEAD_DIM):
        c = head_cols(i)
        below = below_ref[i]
        laters = (below + own_ref[i] + above_ref[i], below)
        for p in range(2):
            later = laters[p].astype(jnp.bfloat16)
            k, v = k_ref[p, :, c], v_ref[p, :, c]
            dk_ref[p, :, c] = (dkp_ref[p, :, c] + mm(v, later, NT)).astype(jnp.bfloat16)
            dv_ref[p, :, c] = (dvp_ref[p, :, c] + mm(k, later, NN)).astype(jnp.bfloat16)


def project_body(hidden_ref, w_ref, out_ref):
    out_ref[...] = mm(hidden_ref[...], w_ref[...], NN).astype(jnp.bfloat16)


def project(hidden, weight):
    rows, features = hidden.shape
    cols = weight.shape[1]
    tile = min(1024, cols)
    return pl.pallas_call(
        project_body,
        out_shape=shaped((rows, cols), jnp.bfloat16),
        grid=(cols // tile,),
        in_specs=[
            pl.BlockSpec((rows, features), lambda m: (0, 0)),
            pl.BlockSpec((features, tile), lambda m: (0, m)),
        ],
        out_specs=pl.BlockSpec((rows, tile), lambda m: (0, m)),
        compiler_params=pltpu.CompilerParams(vmem_limit_bytes=32 * 2**20),
        cost_estimate=pl.CostEstimate(
            flops=2 * rows * features * cols,
            bytes_accessed=2 * (hidden.size + weight.size + rows * cols),
            transcendentals=0,
        ),
    )(hidden, weight)


def weight_body(slots, index_ref, *refs):
    hidden_refs, up_ref, out_ref = refs[:-2], refs[-2], refs[-1]
    total = None
    for m in range(slots):
        up = up_ref[index_ref[m]]
        part = mm(hidden_refs[m][...], up, TN)
        total = part if total is None else total + part
    out_ref[...] = total


def weight_grad_of(hiddens, ups, index):
    n = len(hiddens)
    rows, features = hiddens[0].shape
    cols = ups.shape[2]
    return pl.pallas_call(
        functools.partial(weight_body, n),
        out_shape=shaped((features, cols), jnp.float32),
        in_specs=[pl.BlockSpec(memory_space=pltpu.SMEM)] + whole(n + 1),
        out_specs=pl.BlockSpec(memory_space=pltpu.VMEM),
        compiler_params=pltpu.CompilerParams(vmem_limit_bytes=32 * 2**20),
        cost_estimate=pl.CostEstimate(
            flops=2 * n * rows * features * cols,
            bytes_accessed=2 * n * rows * (features + cols) + 4 * features * cols,
            transcendentals=0,
        ),
    )(index, *hiddens, ups)


def gather_xor(x, axis):
    count = lax.axis_size(axis)
    slots = {0: x}
    bit = count // 2
    while bit:
        for m in list(slots):
            slots[m ^ bit] = xor_permute(slots[m], axis, bit)
        bit //= 2
    return [slots[m] for m in range(count)]


def on_device(queries, keys, values, out_weight, upstream):
    pair, length, width = queries.shape
    heads = width // HEAD_DIM
    n_seq, n_head = lax.axis_size("seq"), lax.axis_size("head")
    seq, head = lax.axis_index("seq"), lax.axis_index("head")
    rows = pair * length
    f32, bf16 = jnp.float32, jnp.bfloat16
    square = (heads, HEAD_DIM, HEAD_DIM)
    product = 2 * rows * HEAD_DIM * width

    kv_own, kv_send = kernel_call(
        kv_body, (shaped(square, f32), shaped((2,) + square, bf16)), (keys, values), product
    )
    below, above = exchange(kv_own, kv_send, "seq")

    flat_up = upstream.reshape(rows, upstream.shape[2])
    chunks = gather_xor(flat_up, "head")
    hidden_grad = hidden_grad_of(chunks, out_weight, head)

    states, hidden, attn_grad, qg_own, qg_send = kernel_call(
        forward_body,
        (
            shaped((2,) + square, bf16),
            shaped((rows, width), bf16),
            shaped((pair, length, width), bf16),
            shaped(square, f32),
            shaped((2,) + square, bf16),
        ),
        (queries, keys, values, hidden_grad, kv_own, below, above),
        3 * product,
    )
    q_below, q_above = exchange(qg_own, qg_send, "seq")

    output = lax.psum_scatter(project(hidden, out_weight), "head", scatter_dimension=1, tiled=True)

    query_grad, key_part, value_part = kernel_call(
        inside_body,
        (
            shaped((pair, length, width), bf16),
            shaped((pair, length, width), f32),
            shaped((pair, length, width), f32),
        ),
        (queries, keys, values, attn_grad, states),
        4 * product,
    )
    key_grad, value_grad = kernel_call(
        final_body,
        (shaped((pair, length, width), bf16), shaped((pair, length, width), bf16)),
        (keys, values, key_part, value_part, qg_own, q_below, q_above),
        2 * product,
    )

    if n_seq == 2 * n_head:
        cols = flat_up.shape[1] // 2
        odd = seq & 1
        left, right = flat_up[:, :cols], flat_up[:, cols:]
        flip = odd == 1
        got = []
        for k in range(2):
            pairs = [
                (s * n_head + h, (2 * h + (k ^ (s & 1))) * n_head + s // 2)
                for s in range(n_seq)
                for h in range(n_head)
            ]
            piece = jnp.where(flip, left if k else right, right if k else left)
            got.append(lax.ppermute(piece, ("seq", "head"), pairs))
        ups = lax.all_gather(jnp.stack(got), "head").reshape(n_seq, rows, cols)
        hiddens = gather_xor(hidden, "seq")
        source = seq ^ jnp.arange(n_seq, dtype=jnp.int32)
        index = (source // 2) * 2 + ((source & 1) ^ odd)
        weight_grad = weight_grad_of(hiddens, ups, index)
    else:
        full_up = lax.all_gather(flat_up, "head", axis=1, tiled=True)
        weight_grad = lax.psum_scatter(
            mm(full_up, hidden, TN), "seq", scatter_dimension=0, tiled=True
        ).T

    return (
        output.reshape(pair, length, -1),
        query_grad,
        key_grad,
        value_grad,
        weight_grad,
    )


def solution(mesh):
    rows = P(None, "seq", "head")
    return jax.shard_map(
        on_device,
        mesh=mesh,
        in_specs=(rows, rows, rows, P("head", None), rows),
        out_specs=(rows, rows, rows, rows, P("head", "seq")),
        check_vma=False,
    )
```

time: 533 us -> 91.3 us (0.17)
  waiting for transfers between devices: 476 us -> 25.4 us
  starting transfers between devices: 0.37 us -> 30 us
  matrix products: 18.1 us -> 0 us
  Pallas kernels: 0 us -> 13.6 us
  other arithmetic: 16 us -> 2.5 us
    reduce_scatter x2 -> x1, waiting for transfers between devices: 179 us -> 0.01 us  [on_device(): lax.psum_scatter(project(hidden, out_weight), 'head', scatter_dimension=1...]
    all_gather x5 -> x1, waiting for transfers between devices: 150 us -> 0.01 us  [on_device(): ups = lax.all_gather(jnp.stack(got), 'head').reshape(n_seq, rows, cols)]
    psum x2 -> x0, waiting for transfers between devices: 146 us -> none  [the longest x1 73 us: on_device(): total_first = lax.psum(first_kv, 'seq')]
    ppermute x0 -> x18, starting transfers between devices: none -> 29.9 us  [the longest x16 26.2 us: xor_permute(): return lax.ppermute(x, axis, [(i, i ^ bit) for i in range(count)])]
    ppermute x0 -> x18, waiting for transfers between devices: none -> 25.4 us  [the longest x16 23.8 us: xor_permute(): return lax.ppermute(x, axis, [(i, i ^ bit) for i in range(count)])]
    dot_general x15 -> x0, matrix products: 18.1 us -> none  [the longest x1 4.53 us: on_device(): lax.dot_general(full_up, hidden, (((0,), (0,)), ((), ())), preferred_elem...]
    pallas_call x0 -> x7, Pallas kernels: none -> 13.6 us  [the longest x4 5.28 us: kernel_call(): pl.pallas_call(body, out_shape=outs, in_specs=whole(len(args)), out_specs...]
    add x14 -> x1, other arithmetic: 13.5 us -> 0.01 us  [on_device(): index = source // 2 * 2 + (source & 1 ^ odd)]
  transfers between devices with their start and end apart: 9 -> 20, of which waited for: 9 -> 9; matrix products, arithmetic and copies ran while one was open for 7% -> 2% of each run, Pallas kernels for 0% -> 15%
where the time goes in v1:
time: 91.3 us; the launch traced here: 91.1 us
  starting transfers between devices  30 us (33%)
  waiting for transfers between devices  25.4 us (28%)
  between operations  14.3 us (16%)
  Pallas kernels  13.6 us (15%)
  local copies, waits for them, and re-layouts  5.34 us (6%)
  other arithmetic  2.5 us (3%)
    ppermute x16, starting transfers between devices, xor_permute(): return lax.ppermute(x, axis, [(i, i ^ bit) for i in range(count)])  26.2 us
    ppermute x16, waiting for transfers between devices, xor_permute(): return lax.ppermute(x, axis, [(i, i ^ bit) for i in range(count)])  23.8 us
    unnamed x18, local copies, waits for them, and re-layouts  5.34 us
    pallas_call x4, Pallas kernels, kernel_call(): pl.pallas_call(body, out_shape=outs, in_specs=whole(len(args)), out_specs...  5.28 us
    ppermute x2, starting transfers between devices, on_device(): got.append(lax.ppermute(piece, ('seq', 'head'), pairs))  3.69 us
    pallas_call x1, Pallas kernels, hidden_grad_of(): pl.pallas_call(functools.partial(grad_body, n), out_shape=shaped((rows, f...  2.91 us
    pallas_call x1, Pallas kernels, weight_grad_of(): pl.pallas_call(functools.partial(weight_body, n), out_shape=shaped((featu...  2.78 us
    pallas_call x1, Pallas kernels, project(): pl.pallas_call(project_body, out_shape=shaped((rows, cols), jnp.bfloat16)...  2.65 us
  transfers between devices with their start and end apart: 20, of which 9 were waited for; matrix products, arithmetic and copies ran while one was open for 2% of the time, Pallas kernels for 15%

profile of v1, /device:TPU:0, one launch (start us, length us, event | category | flops | bytes accessed | tf_op | source)
XLA Modules:
  0.0 91.1 jit_solution(17931915281330652250)
XLA Ops:
  7.2 0.0 all-gather.3.cloned.1.call-start
  7.2 1.0 %broadcast_select_fusion.1 = (bf16[128,512]{1,0:T(8,128)(2,1)S(1)}, bf16[128,512]{1,0:T(8,128)(2,1)S(1)}) fusion(pred[]{:T(512)S(6)} %eq.3, bf16[128,1024]{1,0:T(8,128)(2,1)} %bitcast.40), kind=kLoop, calls=%fused_computation.32 | loop fusion | flops 131072 | bytes 524289 | tf_op jit(solution)/shard_map/jit(_where)/select_n | solution.py:312
  8.3 3.0 %collective-permute-start.17 = (bf16[128,512]{1,0:T(8,128)(2,1)S(1)}, bf16[128,512]{1,0:T(8,128)(2,1)S(1)}, u32[]{:S(2)}, u32[]{:S(2)}) collective-permute-start(bf16[128,512]{1,0:T(8,128)(2,1)S(1)} %get-tuple-element.34), channel_id=1, source_target_pairs={{0,4},{1,12},{2,20},{3,28},{4,0},{5,8},{6,16},{7,24},{8,5},{9,13},... | collective-permute-start | bytes 393224 | tf_op jit(solution)/shard_map/ppermute | solution.py:313
  11.3 0.7 collective-permute-start.16
  12.0 0.9 copy-done.2
  12.9 0.9 copy-done.4
  13.8 0.3 shard_map.93
  14.0 0.1 collective-permute-start.3
  14.1 1.5 %collective-permute-done.17 = bf16[128,512]{1,0:T(8,128)(2,1)S(1)} collective-permute-done((bf16[128,512]{1,0:T(8,128)(2,1)S(1)}, bf16[128,512]{1,0:T(8,128)(2,1)S(1)}, u32[]{:S(2)}, u32[]{:S(2)}) %collective-permute-start.17) | collective-permute-done | bytes 131104 | tf_op jit(solution)/shard_map/ppermute | solution.py:313
  15.6 0.7 pad_maximum_fusion
  16.4 0.0 all-gather.3.cloned.1.call-update
  16.4 0.0 reduce-scatter.2.cloned.1.call-start
  16.4 12.8 %collective-permute-start.1 = (bf16[128,1024]{1,0:T(8,128)(2,1)}, bf16[128,1024]{1,0:T(8,128)(2,1)S(1)}, u32[]{:S(2)}, u32[]{:S(2)}) collective-permute-start(bf16[128,1024]{1,0:T(8,128)(2,1)} %bitcast.41), channel_id=1, source_target_pairs={{0,2},{1,3},{2,0},{3,1},{4,6},{5,7},{6,4},{7,5},{8,10},{9,11},{10,... | collective-permute-start | bytes 786440 | tf_op jit(solution)/shard_map/ppermute | solution.py:34
  29.2 0.1 fusion
  29.3 0.3 collective-permute-start.4
  29.6 4.5 %collective-permute-done.1.refs_2_ = bf16[128,1024]{1,0:T(8,128)(2,1)S(1)} collective-permute-done((bf16[128,1024]{1,0:T(8,128)(2,1)}, bf16[128,1024]{1,0:T(8,128)(2,1)S(1)}, u32[]{:S(2)}, u32[]{:S(2)}) %collective-permute-start.1) | collective-permute-done | bytes 262176 | tf_op jit(solution)/shard_map/ppermute | solution.py:34
  34.0 1.7 %collective-permute-done.4 = bf16[2,4,128,128]{3,2,1,0:T(8,128)(2,1)S(1)} collective-permute-done((bf16[2,4,128,128]{3,2,1,0:T(8,128)(2,1)S(1)}, bf16[2,4,128,128]{3,2,1,0:T(8,128)(2,1)S(1)}, u32[]{:S(2)}, u32[]{:S(2)}) %collective-permute-start.4) | collective-permute-done | bytes 262176 | tf_op jit(solution)/shard_map/ppermute | solution.py:34
  35.7 0.1 add_convert_fusion.1
  35.9 1.6 %collective-permute-start.5 = (bf16[4,128,128]{2,1,0:T(8,128)(2,1)S(1)}, bf16[4,128,128]{2,1,0:T(8,128)(2,1)S(1)}, u32[]{:S(2)}, u32[]{:S(2)}) collective-permute-start(bf16[4,128,128]{2,1,0:T(8,128)(2,1)S(1)} %fusion.7), channel_id=1, source_target_pairs={{0,16},{4,20},{8,24},{12,28},{16,0},{20,4},{24,8},{28,12},{1,17},{... | collective-permute-start | bytes 393224 | tf_op jit(solution)/shard_map/ppermute | solution.py:34
  37.6 2.3 %copy-done = bf16[512,4096]{1,0:T(8,128)(2,1)S(1)} copy-done((bf16[512,4096]{1,0:T(8,128)(2,1)S(1)}, bf16[512,4096]{1,0:T(8,128)(2,1)}, u32[]{:S(2)}) %copy-start) | copy-done | bytes 4194328
  39.9 2.9 %shard_map.92.hg_ref = f32[128,512]{1,0:T(8,128)S(1)} custom-call(s32[4]{0:T(128)S(1)} %iota_xor_fusion.index_ref, bf16[128,1024]{1,0:T(8,128)(2,1)S(1)} %bitcast.43, bf16[128,1024]{1,0:T(8,128)(2,1)S(1)} %collective-permute-done.refs_1_, bf16[128,1024]{1,0:T(8,128)(2,1)S(1)} %collective-permute-done.1.refs_2_, ...), custom_call_target="tpu_custom_call" | custom-call | flops 536870912 | bytes 5242880 | tf_op jit(solution)/shard_map/pallas_call | solution.py:109
  42.8 1.1 %collective-permute-done.5 = bf16[4,128,128]{2,1,0:T(8,128)(2,1)S(1)} collective-permute-done((bf16[4,128,128]{2,1,0:T(8,128)(2,1)S(1)}, bf16[4,128,128]{2,1,0:T(8,128)(2,1)S(1)}, u32[]{:S(2)}, u32[]{:S(2)}) %collective-permute-start.5) | collective-permute-done | bytes 131104 | tf_op jit(solution)/shard_map/ppermute | solution.py:34
  43.9 0.1 add_select_fusion.4
  44.0 1.8 %shard_map.94 = (bf16[2,4,128,128]{3,2,1,0:T(8,128)(2,1)S(1)}, bf16[128,512]{1,0:T(8,128)(2,1)S(1)}, bf16[2,64,512]{2,1,0:T(8,128)(2,1)S(1)}, f32[4,128,128]{2,1,0:T(8,128)S(1)}, bf16[2,4,128,128]{3,2,1,0:T(8,128)(2,1)S(1)}) custom-call(bf16[2,64,512]{2,1,0:T(8,128)(2,1)S(1)} %copy-done.8, bf16[2,64,512]{2,1,0:T(8,128)(2,1)S(1)} %copy-done.3, ...), custom_call_target="tpu_custom_call" | custom-call | flops 50331648 | bytes 2490368 | tf_op jit(solution)/shard_map/pallas_call | solution.py:43
  45.8 2.6 %shard_map.95 = bf16[128,4096]{1,0:T(8,128)(2,1)} custom-call(bf16[128,512]{1,0:T(8,128)(2,1)S(1)} %get-tuple-element.19.hidden_ref.refs_0_, bf16[512,4096]{1,0:T(8,128)(2,1)S(1)} %copy-done.1), custom_call_target="tpu_custom_call" | custom-call | flops 536870912 | bytes 5373952 | tf_op jit(solution)/shard_map/pallas_call | solution.py:191
  48.4 0.0 reduce-scatter.2.cloned.1.call-update
  48.5 0.3 collective-permute-start.6
  48.8 7.4 %collective-permute-done.6 = bf16[2,4,128,128]{3,2,1,0:T(8,128)(2,1)S(1)} collective-permute-done((bf16[2,4,128,128]{3,2,1,0:T(8,128)(2,1)S(1)}, bf16[2,4,128,128]{3,2,1,0:T(8,128)(2,1)S(1)}, u32[]{:S(2)}, u32[]{:S(2)}) %collective-permute-start.6) | collective-permute-done | bytes 262176 | tf_op jit(solution)/shard_map/ppermute | solution.py:34
  56.2 0.1 fusion.1
  56.2 0.1 collective-permute-start.7
  56.3 3.0 %collective-permute-start.12 = (bf16[128,512]{1,0:T(8,128)(2,1)S(1)}, bf16[128,512]{1,0:T(8,128)(2,1)S(1)}, u32[]{:S(2)}, u32[]{:S(2)}) collective-permute-start(bf16[128,512]{1,0:T(8,128)(2,1)S(1)} %get-tuple-element.19.hidden_ref.refs_0_), channel_id=1, source_target_pairs={{0,16},{4,20},{8,24},{12,28},{16,0},{20,4},{24,8},{28,12},{1,17},{... | collective-permute-start | bytes 393224 | tf_op jit(solution)/shard_map/ppermute | solution.py:34
  59.3 0.1 collective-permute-start.10
  59.4 6.2 %collective-permute-done.12.refs_4_ = bf16[128,512]{1,0:T(8,128)(2,1)S(1)} collective-permute-done((bf16[128,512]{1,0:T(8,128)(2,1)S(1)}, bf16[128,512]{1,0:T(8,128)(2,1)S(1)}, u32[]{:S(2)}, u32[]{:S(2)}) %collective-permute-start.12) | collective-permute-done | bytes 131104 | tf_op jit(solution)/shard_map/ppermute | solution.py:34
  65.5 3.8 %collective-permute-start.14 = (bf16[128,512]{1,0:T(8,128)(2,1)S(1)}, bf16[128,512]{1,0:T(8,128)(2,1)S(1)}, u32[]{:S(2)}, u32[]{:S(2)}) collective-permute-start(bf16[128,512]{1,0:T(8,128)(2,1)S(1)} %collective-permute-done.12.refs_4_), channel_id=1, source_target_pairs={{0,8},{4,12},{8,0},{12,4},{16,24},{20,28},{24,16},{28,20},{1,9},{5... | collective-permute-start | bytes 393224 | tf_op jit(solution)/shard_map/ppermute | solution.py:34
  69.3 0.1 add_convert_fusion
  69.5 0.1 collective-permute-start.8
  69.6 0.6 collective-permute-start.9
  70.1 2.2 %shard_map.96 = (bf16[2,64,512]{2,1,0:T(8,128)(2,1)}, f32[2,64,512]{2,1,0:T(8,128)S(1)}, f32[2,64,512]{2,1,0:T(8,128)S(1)}) custom-call(bf16[2,64,512]{2,1,0:T(8,128)(2,1)S(1)} %copy-done.8, bf16[2,64,512]{2,1,0:T(8,128)(2,1)S(1)} %copy-done.3, bf16[2,64,512]{2,1,0:T(8,128)(2,1)S(1)} %copy-done.5, bf16[2,64,512]{2,1,0:T(8,128)(2,1)S(1)} %get-tuple-element.20.g_ref, ...), custom_call_target="tpu_custom_call" | custom-call | flops 67108864 | bytes 1441792 | tf_op jit(solution)/shard_map/pallas_call | solution.py:43
  72.3 1.5 %collective-permute-start.13 = (bf16[128,512]{1,0:T(8,128)(2,1)S(1)}, bf16[128,512]{1,0:T(8,128)(2,1)S(1)}, u32[]{:S(2)}, u32[]{:S(2)}) collective-permute-start(bf16[128,512]{1,0:T(8,128)(2,1)S(1)} %collective-permute-done.12.refs_4_), channel_id=1, source_target_pairs={{0,4},{4,0},{8,12},{12,8},{16,20},{20,16},{24,28},{28,24},{1,5},{5... | collective-permute-start | bytes 393224 | tf_op jit(solution)/shard_map/ppermute | solution.py:34
  73.9 0.5 collective-permute-start.11
  74.4 1.6 %collective-permute-start.15 = (bf16[128,512]{1,0:T(8,128)(2,1)S(1)}, bf16[128,512]{1,0:T(8,128)(2,1)S(1)}, u32[]{:S(2)}, u32[]{:S(2)}) collective-permute-start(bf16[128,512]{1,0:T(8,128)(2,1)S(1)} %collective-permute-done.14.refs_6_), channel_id=1, source_target_pairs={{0,4},{4,0},{8,12},{12,8},{16,20},{20,16},{24,28},{28,24},{1,5},{5... | collective-permute-start | bytes 393224 | tf_op jit(solution)/shard_map/ppermute | solution.py:34
  76.1 0.2 collective-permute-done.8
  76.2 0.1 add_select_fusion
  76.3 1.0 %shard_map.97 = (bf16[2,64,512]{2,1,0:T(8,128)(2,1)}, bf16[2,64,512]{2,1,0:T(8,128)(2,1)}) custom-call(bf16[2,64,512]{2,1,0:T(8,128)(2,1)S(1)} %copy-done.3, bf16[2,64,512]{2,1,0:T(8,128)(2,1)S(1)} %copy-done.5, f32[2,64,512]{2,1,0:T(8,128)S(1)} %get-tuple-element.23.dkp_ref, f32[2,64,512]{2,1,0:T(8,128)S(1)} %get-tuple-element.24.dvp_ref, ...), custom_call_target="tpu_custom_call" | custom-call | flops 33554432 | bytes 1835008 | tf_op jit(solution)/shard_map/pallas_call | solution.py:43
  77.4 1.5 %collective-permute-done.11.refs_3_ = bf16[128,512]{1,0:T(8,128)(2,1)S(1)} collective-permute-done((bf16[128,512]{1,0:T(8,128)(2,1)S(1)}, bf16[128,512]{1,0:T(8,128)(2,1)S(1)}, u32[]{:S(2)}, u32[]{:S(2)}) %collective-permute-start.11) | collective-permute-done | bytes 131104 | tf_op jit(solution)/shard_map/ppermute | solution.py:34
  78.8 1.4 %collective-permute-done.15.refs_7_ = bf16[128,512]{1,0:T(8,128)(2,1)S(1)} collective-permute-done((bf16[128,512]{1,0:T(8,128)(2,1)S(1)}, bf16[128,512]{1,0:T(8,128)(2,1)S(1)}, u32[]{:S(2)}, u32[]{:S(2)}) %collective-permute-start.15) | collective-permute-done | bytes 131104 | tf_op jit(solution)/shard_map/ppermute | solution.py:34
  80.2 1.2 %copy-done.7 = bf16[8,128,512]{2,1,0:T(8,128)(2,1)S(1)} copy-done((bf16[8,128,512]{2,1,0:T(8,128)(2,1)S(1)}, bf16[8,128,512]{2,1,0:T(8,128)(2,1)}, u32[]{:S(2)}) %copy-start.7) | copy-done | bytes 1048600
  81.5 2.8 %shard_map.98 = f32[512,512]{1,0:T(8,128)} custom-call(s32[8]{0:T(128)S(1)} %xor_add_fusion.index_ref, bf16[128,512]{1,0:T(8,128)(2,1)S(1)} %get-tuple-element.19.hidden_ref.refs_0_, bf16[128,512]{1,0:T(8,128)(2,1)S(1)} %collective-permute-done.9.refs_1_, bf16[128,512]{1,0:T(8,128)(2,1)S(1)} %collective-permute-done.10.refs_2_, ...), custom_call_target="tpu_custom_call" | custom-call | flops 536870912 | bytes 3145728 | tf_op jit(solution)/shard_map/pallas_call | solution.py:223
  (35 shorter events, 0.3 us)
Async XLA Ops:
  7.2 30.4 %copy-start.6 = (bf16[2,64,1024]{2,1,0:T(8,128)(2,1)S(1)}, bf16[2,64,1024]{2,1,0:T(8,128)(2,1)}, u32[]{:S(2)}) copy-start(bf16[2,64,1024]{2,1,0:T(8,128)(2,1)} %param.9) | copy-start | bytes 786436
  7.2 73.1 %all-gather.3.cloned.1.call-start = ((), (), s32[]{:S(2)}) async-start(), calls=%async_computation.2 | async-start | bytes 1310720 | tf_op jit(solution)/shard_map/all_gather | solution.py:314
  8.3 7.4 %collective-permute-start.17 = (bf16[128,512]{1,0:T(8,128)(2,1)S(1)}, bf16[128,512]{1,0:T(8,128)(2,1)S(1)}, u32[]{:S(2)}, u32[]{:S(2)}) collective-permute-start(bf16[128,512]{1,0:T(8,128)(2,1)S(1)} %get-tuple-element.34), channel_id=1, source_target_pairs={{0,4},{1,12},{2,20},{3,28},{4,0},{5,8},{6,16},{7,24},{8,5},{9,13},... | collective-permute-start | bytes 393224 | tf_op jit(solution)/shard_map/ppermute | solution.py:313
  11.3 4.4 %collective-permute-start.16 = (bf16[128,512]{1,0:T(8,128)(2,1)S(1)}, bf16[128,512]{1,0:T(8,128)(2,1)S(1)}, u32[]{:S(2)}, u32[]{:S(2)}) collective-permute-start(bf16[128,512]{1,0:T(8,128)(2,1)S(1)} %get-tuple-element.33), channel_id=1, source_target_pairs={{0,0},{1,8},{2,16},{3,24},{4,4},{5,12},{6,20},{7,28},{8,1},{9,9},{... | collective-permute-start | bytes 393224 | tf_op jit(solution)/shard_map/ppermute | solution.py:313
  12.0 0.9 copy-start.2
  12.9 0.9 copy-start.4
  14.0 15.2 %collective-permute-start.3 = (bf16[2,4,128,128]{3,2,1,0:T(8,128)(2,1)S(1)}, bf16[2,4,128,128]{3,2,1,0:T(8,128)(2,1)S(1)}, u32[]{:S(2)}, u32[]{:S(2)}) collective-permute-start(bf16[2,4,128,128]{3,2,1,0:T(8,128)(2,1)S(1)} %get-tuple-element.18), channel_id=1, source_target_pairs={{0,4},{4,0},{8,12},{12,8},{16,20},{20,16},{24,28},{28,24},{1,5},{5... | collective-permute-start | bytes 786440 | tf_op jit(solution)/shard_map/ppermute | solution.py:34
  16.4 67.9 %reduce-scatter.2.cloned.1.call-start = ((), (), s32[]{:S(2)}) async-start(), calls=%async_computation.1 | async-start | bytes 1310720 | tf_op jit(solution)/shard_map/reduce_scatter | solution.py:281
  16.4 17.6 %collective-permute-start.1 = (bf16[128,1024]{1,0:T(8,128)(2,1)}, bf16[128,1024]{1,0:T(8,128)(2,1)S(1)}, u32[]{:S(2)}, u32[]{:S(2)}) collective-permute-start(bf16[128,1024]{1,0:T(8,128)(2,1)} %bitcast.41), channel_id=1, source_target_pairs={{0,2},{1,3},{2,0},{3,1},{4,6},{5,7},{6,4},{7,5},{8,10},{9,11},{10,... | collective-permute-start | bytes 786440 | tf_op jit(solution)/shard_map/ppermute | solution.py:34
  29.3 6.4 %collective-permute-start.4 = (bf16[2,4,128,128]{3,2,1,0:T(8,128)(2,1)S(1)}, bf16[2,4,128,128]{3,2,1,0:T(8,128)(2,1)S(1)}, u32[]{:S(2)}, u32[]{:S(2)}) collective-permute-start(bf16[2,4,128,128]{3,2,1,0:T(8,128)(2,1)S(1)} %fusion), channel_id=1, source_target_pairs={{0,8},{4,12},{8,0},{12,4},{16,24},{20,28},{24,16},{28,20},{1,9},{5... | collective-permute-start | bytes 786440 | tf_op jit(solution)/shard_map/ppermute | solution.py:34
  29.6 8.0 %collective-permute-start = (bf16[128,1024]{1,0:T(8,128)(2,1)}, bf16[128,1024]{1,0:T(8,128)(2,1)S(1)}, u32[]{:S(2)}, u32[]{:S(2)}) collective-permute-start(bf16[128,1024]{1,0:T(8,128)(2,1)} %bitcast.42), channel_id=1, source_target_pairs={{0,1},{1,0},{2,3},{3,2},{4,5},{5,4},{6,7},{7,6},{8,9},{9,8},{10,11... | collective-permute-start | bytes 786440 | tf_op jit(solution)/shard_map/ppermute | solution.py:34
  34.0 3.5 %collective-permute-start.2 = (bf16[128,1024]{1,0:T(8,128)(2,1)S(1)}, bf16[128,1024]{1,0:T(8,128)(2,1)S(1)}, u32[]{:S(2)}, u32[]{:S(2)}) collective-permute-start(bf16[128,1024]{1,0:T(8,128)(2,1)S(1)} %collective-permute-done.1.refs_2_), channel_id=1, source_target_pairs={{0,1},{1,0},{2,3},{3,2},{4,5},{5,4},{6,7},{7,6},{8,9},{9,8},{10,11... | collective-permute-start | bytes 786440 | tf_op jit(solution)/shard_map/ppermute | solution.py:34
  35.9 8.0 %collective-permute-start.5 = (bf16[4,128,128]{2,1,0:T(8,128)(2,1)S(1)}, bf16[4,128,128]{2,1,0:T(8,128)(2,1)S(1)}, u32[]{:S(2)}, u32[]{:S(2)}) collective-permute-start(bf16[4,128,128]{2,1,0:T(8,128)(2,1)S(1)} %fusion.7), channel_id=1, source_target_pairs={{0,16},{4,20},{8,24},{12,28},{16,0},{20,4},{24,8},{28,12},{1,17},{... | collective-permute-start | bytes 393224 | tf_op jit(solution)/shard_map/ppermute | solution.py:34
  37.5 6.5 %copy-start.3 = (bf16[2,64,512]{2,1,0:T(8,128)(2,1)S(1)}, bf16[2,64,512]{2,1,0:T(8,128)(2,1)}, u32[]{:S(2)}) copy-start(bf16[2,64,512]{2,1,0:T(8,128)(2,1)} %k_ref.7) | copy-start | bytes 393220
  37.5 6.5 %copy-start.5 = (bf16[2,64,512]{2,1,0:T(8,128)(2,1)S(1)}, bf16[2,64,512]{2,1,0:T(8,128)(2,1)}, u32[]{:S(2)}) copy-start(bf16[2,64,512]{2,1,0:T(8,128)(2,1)} %v_ref.7) | copy-start | bytes 393220
  37.5 6.5 %copy-start.8 = (bf16[2,64,512]{2,1,0:T(8,128)(2,1)S(1)}, bf16[2,64,512]{2,1,0:T(8,128)(2,1)}, u32[]{:S(2)}) copy-start(bf16[2,64,512]{2,1,0:T(8,128)(2,1)} %q_ref.3) | copy-start | bytes 393220
  37.6 2.3 %copy-start = (bf16[512,4096]{1,0:T(8,128)(2,1)S(1)}, bf16[512,4096]{1,0:T(8,128)(2,1)}, u32[]{:S(2)}) copy-start(bf16[512,4096]{1,0:T(8,128)(2,1)} %w_ref.1) | copy-start | bytes 12582916
  39.9 5.9 %copy-start.1 = (bf16[512,4096]{1,0:T(8,128)(2,1)S(1)}, bf16[512,4096]{1,0:T(8,128)(2,1)}, u32[]{:S(2)}) copy-start(bf16[512,4096]{1,0:T(8,128)(2,1)} %w_ref.1) | copy-start | bytes 12582916
  48.5 7.7 %collective-permute-start.6 = (bf16[2,4,128,128]{3,2,1,0:T(8,128)(2,1)S(1)}, bf16[2,4,128,128]{3,2,1,0:T(8,128)(2,1)S(1)}, u32[]{:S(2)}, u32[]{:S(2)}) collective-permute-start(bf16[2,4,128,128]{3,2,1,0:T(8,128)(2,1)S(1)} %get-tuple-element.26), channel_id=1, source_target_pairs={{0,4},{4,0},{8,12},{12,8},{16,20},{20,16},{24,28},{28,24},{1,5},{5... | collective-permute-start | bytes 786440 | tf_op jit(solution)/shard_map/ppermute | solution.py:34
  56.2 13.1 %collective-permute-start.7 = (bf16[2,4,128,128]{3,2,1,0:T(8,128)(2,1)S(1)}, bf16[2,4,128,128]{3,2,1,0:T(8,128)(2,1)S(1)}, u32[]{:S(2)}, u32[]{:S(2)}) collective-permute-start(bf16[2,4,128,128]{3,2,1,0:T(8,128)(2,1)S(1)} %fusion.1), channel_id=1, source_target_pairs={{0,8},{4,12},{8,0},{12,4},{16,24},{20,28},{24,16},{28,20},{1,9},{5... | collective-permute-start | bytes 786440 | tf_op jit(solution)/shard_map/ppermute | solution.py:34
  56.3 9.2 %collective-permute-start.12 = (bf16[128,512]{1,0:T(8,128)(2,1)S(1)}, bf16[128,512]{1,0:T(8,128)(2,1)S(1)}, u32[]{:S(2)}, u32[]{:S(2)}) collective-permute-start(bf16[128,512]{1,0:T(8,128)(2,1)S(1)} %get-tuple-element.19.hidden_ref.refs_0_), channel_id=1, source_target_pairs={{0,16},{4,20},{8,24},{12,28},{16,0},{20,4},{24,8},{28,12},{1,17},{... | collective-permute-start | bytes 393224 | tf_op jit(solution)/shard_map/ppermute | solution.py:34
  59.3 14.6 %collective-permute-start.10 = (bf16[128,512]{1,0:T(8,128)(2,1)S(1)}, bf16[128,512]{1,0:T(8,128)(2,1)S(1)}, u32[]{:S(2)}, u32[]{:S(2)}) collective-permute-start(bf16[128,512]{1,0:T(8,128)(2,1)S(1)} %get-tuple-element.19.hidden_ref.refs_0_), channel_id=1, source_target_pairs={{0,8},{4,12},{8,0},{12,4},{16,24},{20,28},{24,16},{28,20},{1,9},{5... | collective-permute-start | bytes 393224 | tf_op jit(solution)/shard_map/ppermute | solution.py:34
  65.5 8.9 %collective-permute-start.14 = (bf16[128,512]{1,0:T(8,128)(2,1)S(1)}, bf16[128,512]{1,0:T(8,128)(2,1)S(1)}, u32[]{:S(2)}, u32[]{:S(2)}) collective-permute-start(bf16[128,512]{1,0:T(8,128)(2,1)S(1)} %collective-permute-done.12.refs_4_), channel_id=1, source_target_pairs={{0,8},{4,12},{8,0},{12,4},{16,24},{20,28},{24,16},{28,20},{1,9},{5... | collective-permute-start | bytes 393224 | tf_op jit(solution)/shard_map/ppermute | solution.py:34
  69.5 6.8 %collective-permute-start.8 = (bf16[4,128,128]{2,1,0:T(8,128)(2,1)S(1)}, bf16[4,128,128]{2,1,0:T(8,128)(2,1)S(1)}, u32[]{:S(2)}, u32[]{:S(2)}) collective-permute-start(bf16[4,128,128]{2,1,0:T(8,128)(2,1)S(1)} %fusion.6), channel_id=1, source_target_pairs={{0,16},{4,20},{8,24},{12,28},{16,0},{20,4},{24,8},{28,12},{1,17},{... | collective-permute-start | bytes 393224 | tf_op jit(solution)/shard_map/ppermute | solution.py:34
  69.6 7.8 %collective-permute-start.9 = (bf16[128,512]{1,0:T(8,128)(2,1)S(1)}, bf16[128,512]{1,0:T(8,128)(2,1)S(1)}, u32[]{:S(2)}, u32[]{:S(2)}) collective-permute-start(bf16[128,512]{1,0:T(8,128)(2,1)S(1)} %get-tuple-element.19.hidden_ref.refs_0_), channel_id=1, source_target_pairs={{0,4},{4,0},{8,12},{12,8},{16,20},{20,16},{24,28},{28,24},{1,5},{5... | collective-permute-start | bytes 393224 | tf_op jit(solution)/shard_map/ppermute | solution.py:34
  72.3 6.5 %collective-permute-start.13 = (bf16[128,512]{1,0:T(8,128)(2,1)S(1)}, bf16[128,512]{1,0:T(8,128)(2,1)S(1)}, u32[]{:S(2)}, u32[]{:S(2)}) collective-permute-start(bf16[128,512]{1,0:T(8,128)(2,1)S(1)} %collective-permute-done.12.refs_4_), channel_id=1, source_target_pairs={{0,4},{4,0},{8,12},{12,8},{16,20},{20,16},{24,28},{28,24},{1,5},{5... | collective-permute-start | bytes 393224 | tf_op jit(solution)/shard_map/ppermute | solution.py:34
  73.9 5.0 %collective-permute-start.11 = (bf16[128,512]{1,0:T(8,128)(2,1)S(1)}, bf16[128,512]{1,0:T(8,128)(2,1)S(1)}, u32[]{:S(2)}, u32[]{:S(2)}) collective-permute-start(bf16[128,512]{1,0:T(8,128)(2,1)S(1)} %collective-permute-done.10.refs_2_), channel_id=1, source_target_pairs={{0,4},{4,0},{8,12},{12,8},{16,20},{20,16},{24,28},{28,24},{1,5},{5... | collective-permute-start | bytes 393224 | tf_op jit(solution)/shard_map/ppermute | solution.py:34
  74.4 5.8 %collective-permute-start.15 = (bf16[128,512]{1,0:T(8,128)(2,1)S(1)}, bf16[128,512]{1,0:T(8,128)(2,1)S(1)}, u32[]{:S(2)}, u32[]{:S(2)}) collective-permute-start(bf16[128,512]{1,0:T(8,128)(2,1)S(1)} %collective-permute-done.14.refs_6_), channel_id=1, source_target_pairs={{0,4},{4,0},{8,12},{12,8},{16,20},{20,16},{24,28},{28,24},{1,5},{5... | collective-permute-start | bytes 393224 | tf_op jit(solution)/shard_map/ppermute | solution.py:34
  80.2 1.2 %copy-start.7 = (bf16[8,128,512]{2,1,0:T(8,128)(2,1)S(1)}, bf16[8,128,512]{2,1,0:T(8,128)(2,1)}, u32[]{:S(2)}) copy-start(bf16[8,128,512]{2,1,0:T(8,128)(2,1)} %all-gather.3.cloned.1.call-done.refs_8_) | copy-start | bytes 3145732
Sparse Core Ops, SparseCore 0:
  16.5 25.6 all-gather.2
  48.6 23.4 reduce-scatter.1

commit v2 on v1

v2 whole, which is shorter than its diff:
```python
import functools

import jax
import jax.numpy as jnp
from jax import lax
from jax.experimental import pallas as pl
from jax.experimental.pallas import tpu as pltpu
from jax.sharding import PartitionSpec as P

HEAD_DIM = 128
EPS = 1e-06

NN = (((1,), (0,)), ((), ()))
NT = (((1,), (1,)), ((), ()))
TN = (((0,), (0,)), ((), ()))


def mm(a, b, dims):
    return lax.dot_general(a, b, dims, preferred_element_type=jnp.float32)


def head_cols(i):
    return slice(i * HEAD_DIM, (i + 1) * HEAD_DIM)


def lower(length):
    rows = lax.broadcasted_iota(jnp.int32, (length, length), 0)
    cols = lax.broadcasted_iota(jnp.int32, (length, length), 1)
    return rows >= cols


def xor_permute(x, axis, bit):
    count = lax.axis_size(axis)
    return lax.ppermute(x, axis, [(i, i ^ bit) for i in range(count)])


def whole(n):
    return [pl.BlockSpec(memory_space=pltpu.VMEM)] * n


def lasting(us):
    return pl.CostEstimate(flops=int(us * 1.1e9), bytes_accessed=0, transcendentals=0)


def kernel_call(body, outs, args, us=0.5, vmem=16 * 2**20):
    return pl.pallas_call(
        body,
        out_shape=outs,
        in_specs=whole(len(args)),
        out_specs=whole(len(outs)),
        compiler_params=pltpu.CompilerParams(vmem_limit_bytes=vmem),
        cost_estimate=lasting(us),
    )(*args)


def shaped(shape, dtype):
    return jax.ShapeDtypeStruct(shape, dtype)


def kv_body(k_hbm, v_hbm, own_ref, send_ref, k_ref, v_ref, sems):
    loads = [
        pltpu.make_async_copy(k_hbm, k_ref, sems.at[0]),
        pltpu.make_async_copy(v_hbm, v_ref, sems.at[1]),
    ]
    for load in loads:
        load.start()
    for load in loads:
        load.wait()
    for i in range(k_ref.shape[2] // HEAD_DIM):
        c = head_cols(i)
        first = mm(k_ref[0, :, c], v_ref[0, :, c], TN)
        second = mm(k_ref[1, :, c], v_ref[1, :, c], TN)
        own_ref[i] = first
        send_ref[0, i] = first.astype(jnp.bfloat16)
        send_ref[1, i] = (first + second).astype(jnp.bfloat16)


def in_hbm(x):
    return pltpu.with_memory_space_constraint(x, pltpu.HBM)


def kv_products(keys, values):
    heads = keys.shape[2] // HEAD_DIM
    square = (heads, HEAD_DIM, HEAD_DIM)
    return pl.pallas_call(
        kv_body,
        out_shape=(shaped(square, jnp.float32), shaped((2,) + square, jnp.bfloat16)),
        in_specs=[pl.BlockSpec(memory_space=pltpu.HBM)] * 2,
        out_specs=whole(2),
        scratch_shapes=[
            pltpu.VMEM(keys.shape, keys.dtype),
            pltpu.VMEM(values.shape, values.dtype),
            pltpu.SemaphoreType.DMA((2,)),
        ],
        compiler_params=pltpu.CompilerParams(vmem_limit_bytes=16 * 2**20),
    )(keys, values)


class Rounds:
    def __init__(self, near, send, axis, ahead):
        count = lax.axis_size(axis)
        place = lax.axis_index(axis)
        below = jnp.zeros_like(near)
        above = jnp.zeros_like(near)
        group = send.astype(jnp.float32)
        self.sent = []
        bit = 1
        while bit < count:
            upper = (place & bit) != 0
            last = 2 * bit == count
            if last:
                send = jnp.where(upper, send[1], send[0])
            if bit in ahead:
                send = after(send, *ahead[bit])
            self.sent.append(send)
            got = xor_permute(send, axis, bit).astype(jnp.float32)
            got_near, got_both = (got, got) if last else (got[0], got[1])
            below = jnp.where(upper, below + got_near, below)
            above = jnp.where(upper, above, above + got_both)
            if not last:
                group = group + got
                send = group.astype(jnp.bfloat16)
            bit *= 2
        self.below, self.above = below, above


def pick(table, at):
    value = jnp.int32(table[0])
    for i, entry in enumerate(table[1:], 1):
        value = jnp.where(at == i, entry, value)
    return value


def near_body(spot_ref, w_hbm, up_hbm, out_ref, w_ref, up_ref, sems):
    n, _, cols = w_ref.shape
    loads = [pltpu.make_async_copy(up_hbm, up_ref, sems.at[n])]
    for slot in range(n):
        at = pl.multiple_of((spot_ref[1] ^ slot) * cols, cols)
        loads.append(pltpu.make_async_copy(w_hbm.at[:, pl.ds(at, cols)], w_ref.at[slot], sems.at[slot]))
    for load in loads:
        load.start()
    loads[0].wait()
    loads[1].wait()
    out_ref[...] = mm(up_ref[...], w_ref[0], NT)
    for load in loads[2:]:
        load.wait()


def near_grad_of(up, weight, spot, n):
    rows, cols = up.shape
    features = weight.shape[0]
    return pl.pallas_call(
        near_body,
        out_shape=(
            shaped((rows, features), jnp.float32),
            shaped((n, features, cols), weight.dtype),
            shaped(up.shape, up.dtype),
        ),
        in_specs=[pl.BlockSpec(memory_space=pltpu.SMEM)] + [pl.BlockSpec(memory_space=pltpu.HBM)] * 2,
        out_specs=whole(3),
        scratch_shapes=[pltpu.SemaphoreType.DMA((n + 1,))],
        compiler_params=pltpu.CompilerParams(vmem_limit_bytes=16 * 2**20),
        cost_estimate=lasting(3),
    )(spot, weight, up)


def far_body(slots, w_ref, before_ref, *refs):
    chunks, out_ref = refs[:-1], refs[-1]
    total = before_ref[...]
    for i, slot in enumerate(slots):
        total += mm(chunks[i][...], w_ref[slot], NT)
    out_ref[...] = total


def forward_body(q_ref, k_ref, v_ref, hg_ref, own_ref, below_ref, above_ref,
                 state_ref, hidden_ref, g_ref, qown_ref, qsend_ref):
    length = q_ref.shape[1]
    mask = lower(length)
    for i in range(q_ref.shape[2] // HEAD_DIM):
        c = head_cols(i)
        below = below_ref[i]
        states = (below, below + own_ref[i] + above_ref[i])
        terms = []
        for p in range(2):
            r = slice(p * length, (p + 1) * length)
            q, k, v = q_ref[p, :, c], k_ref[p, :, c], v_ref[p, :, c]
            state = states[p].astype(jnp.bfloat16)
            state_ref[p, i] = state
            weights = jnp.where(mask, mm(q, k, NT), 0.0).astype(jnp.bfloat16)
            attended = mm(weights, v, NN) + mm(q, state, NN)
            scale = jnp.sqrt(jnp.mean(attended * attended, axis=-1, keepdims=True) + EPS)
            normed = attended / scale
            hidden_ref[r, c] = normed.astype(jnp.bfloat16)
            hg = hg_ref[r, c]
            inner = jnp.mean(hg * normed, axis=-1, keepdims=True)
            g = ((hg - normed * inner) / scale).astype(jnp.bfloat16)
            g_ref[p, :, c] = g
            terms.append(mm(q, g, TN))
        qown_ref[i] = terms[1]
        qsend_ref[0, i] = terms[1].astype(jnp.bfloat16)
        qsend_ref[1, i] = (terms[0] + terms[1]).astype(jnp.bfloat16)


def inside_body(q_ref, k_ref, v_ref, g_ref, state_ref, dq_ref, dk_ref, dv_ref):
    length = q_ref.shape[1]
    mask = lower(length)
    for i in range(q_ref.shape[2] // HEAD_DIM):
        c = head_cols(i)
        for p in range(2):
            q, k, v, g = q_ref[p, :, c], k_ref[p, :, c], v_ref[p, :, c], g_ref[p, :, c]
            weights = jnp.where(mask, mm(q, k, NT), 0.0).astype(jnp.bfloat16)
            diffs = jnp.where(mask, mm(g, v, NT), 0.0).astype(jnp.bfloat16)
            dq_ref[p, :, c] = (mm(diffs, k, NN) + mm(g, state_ref[p, i], NT)).astype(jnp.bfloat16)
            dk_ref[p, :, c] = mm(diffs, q, TN)
            dv_ref[p, :, c] = mm(weights, g, TN)


def final_body(k_ref, v_ref, dkp_ref, dvp_ref, own_ref, below_ref, above_ref, dk_ref, dv_ref):
    for i in range(k_ref.shape[2] // HEAD_DIM):
        c = head_cols(i)
        below = below_ref[i]
        laters = (below + own_ref[i] + above_ref[i], below)
        for p in range(2):
            later = laters[p].astype(jnp.bfloat16)
            k, v = k_ref[p, :, c], v_ref[p, :, c]
            dk_ref[p, :, c] = (dkp_ref[p, :, c] + mm(v, later, NT)).astype(jnp.bfloat16)
            dv_ref[p, :, c] = (dvp_ref[p, :, c] + mm(k, later, NN)).astype(jnp.bfloat16)


def project_body(slots, w_ref, hidden_ref, out_ref):
    for i, slot in enumerate(slots):
        out_ref[i] = mm(hidden_ref[...], w_ref[slot], NN).astype(out_ref.dtype)


def project(hidden, by_columns, slots, dtype):
    shape = (len(slots), hidden.shape[0], by_columns.shape[2])
    return kernel_call(functools.partial(project_body, slots), (shaped(shape, dtype),), (by_columns, hidden))[0]


def quarter_body(n, spot_ref, *refs):
    chunks, keep_ref, send_ref = refs[:n], refs[-2], refs[-1]
    seq, head = spot_ref[0], spot_ref[1]
    share, cols = keep_ref.shape[1:]
    rows = pl.ds(pl.multiple_of(head * share, share), share)
    odd = seq & 1
    for m in range(n):
        t = (seq // 2) ^ head ^ m
        entry = (t & 1) * (n // 2) + t // 2
        keep_ref[entry] = chunks[m][rows, pl.ds(pl.multiple_of(odd * cols, cols), cols)]
        send_ref[entry] = chunks[m][rows, pl.ds(pl.multiple_of((1 - odd) * cols, cols), cols)]


def columns_by_place(chunks, spot, waits):
    n = len(chunks)
    rows, cols = chunks[0].shape
    part = shaped((n, rows // n, cols // 2), chunks[0].dtype)
    keep, send = pl.pallas_call(
        functools.partial(quarter_body, n),
        out_shape=(part, part),
        in_specs=[pl.BlockSpec(memory_space=pltpu.SMEM)] + whole(n),
        out_specs=whole(2),
        compiler_params=pltpu.CompilerParams(vmem_limit_bytes=16 * 2**20),
        cost_estimate=lasting(0.5),
    )(spot, *chunks)
    got = xor_permute(send, "seq", 1)
    held = jnp.stack([keep, got], axis=1)
    bit = 1
    while bit < n:
        half = held.shape[0] // 2
        send = held[half:]
        if bit in waits:
            send = after(send, *waits[bit])
        got = xor_permute(send, "seq", 2 * bit)
        held = jnp.concatenate([held[:half], got], axis=1)
        bit *= 2
        if bit < n:
            held = jnp.concatenate([held[0::2], held[1::2]])
    return held[0]


def weight_body(slots, first, spot_ref, *refs):
    head = spot_ref[1]
    ups, out_ref = refs[len(slots)], refs[-1]
    n, _, share, _ = ups.shape
    lefts, rights = [], []
    for ref, group in zip(refs, slots):
        for i, slot in enumerate(group):
            for m in range(n):
                at = pl.multiple_of((head ^ m) * share, share)
                lefts.append(ref[i, pl.ds(at, share), :])
                rights.append(ups[m, slot])
    total = mm(jnp.concatenate(lefts), jnp.concatenate(rights), TN)
    out_ref[...] = total if first else refs[-2][...] + total


def weight_grad_of(hiddens, slots, ups, spot, before):
    features, cols = hiddens[0].shape[2], ups.shape[3]
    args = list(hiddens) + [ups] + ([] if before is None else [before])
    return pl.pallas_call(
        functools.partial(weight_body, slots, before is None),
        out_shape=shaped((features, cols), jnp.float32),
        in_specs=[pl.BlockSpec(memory_space=pltpu.SMEM)] + whole(len(args)),
        out_specs=pl.BlockSpec(memory_space=pltpu.VMEM),
        compiler_params=pltpu.CompilerParams(vmem_limit_bytes=16 * 2**20),
        cost_estimate=lasting(1),
    )(spot, *args)


def gather_xor(x, axis):
    held = {0: x}
    bit = lax.axis_size(axis) // 2
    while bit:
        for m in list(held):
            held[m ^ bit] = xor_permute(held[m], axis, bit)
        bit //= 2
    return [held[m] for m in range(len(held))]


def after(x, *others):
    return lax.optimization_barrier((x,) + others)[0]


def reduce_columns(away, home):
    got = xor_permute(away, "head", 1)
    total = home + got.astype(jnp.float32)
    bit = 2
    while bit < lax.axis_size("head"):
        total = total.reshape((-1, 2) + total.shape[1:])
        got = xor_permute(total[:, 1].astype(jnp.bfloat16), "head", bit)
        total = total[:, 0] + got.astype(jnp.float32)
        bit *= 2
    return total[0].astype(jnp.bfloat16)


def on_device(queries, keys, values, out_weight, upstream):
    pair, length, width = queries.shape
    heads = width // HEAD_DIM
    n_seq, n_head = lax.axis_size("seq"), lax.axis_size("head")
    seq, head = lax.axis_index("seq"), lax.axis_index("head")
    rows, own_cols = pair * length, upstream.shape[2]
    f32, bf16 = jnp.float32, jnp.bfloat16
    square = (heads, HEAD_DIM, HEAD_DIM)
    flat_up = upstream.reshape(rows, own_cols)
    spot = jnp.stack([seq, head]).astype(jnp.int32)
    split = n_seq == 2 * n_head

    kv_own, kv_send = kv_products(in_hbm(keys), in_hbm(values))
    sent_up = after(flat_up, kv_send)
    chunks = gather_xor(sent_up, "head")
    near_grad, by_columns, chunks[0] = near_grad_of(
        in_hbm(sent_up), in_hbm(out_weight), spot, n_head
    )
    hidden_grad = kernel_call(
        functools.partial(far_body, range(1, n_head)),
        (shaped((rows, width), f32),),
        [by_columns, near_grad] + chunks[1:],
        2,
    )[0]
    kv_rounds = Rounds(kv_own, kv_send, "seq", {})
    if split:
        ups = columns_by_place(chunks, spot, {1: (kv_rounds.sent[-1],)})

    states, hidden, attn_grad, qg_own, qg_send = kernel_call(
        forward_body,
        (
            shaped((2,) + square, bf16),
            shaped((rows, width), bf16),
            shaped((pair, length, width), bf16),
            shaped(square, f32),
            shaped((2,) + square, bf16),
        ),
        (queries, keys, values, hidden_grad, kv_own, kv_rounds.below, kv_rounds.above),
    )
    qg_rounds = Rounds(qg_own, qg_send, "seq", {})

    late = after(hidden, qg_rounds.sent[1])
    away = project(late, by_columns, range(1, n_head, 2), bf16)
    home = project(late, by_columns, range(0, n_head, 2), f32)
    output = reduce_columns(away, home)

    query_grad, key_part, value_part = kernel_call(
        inside_body,
        (
            shaped((pair, length, width), bf16),
            shaped((pair, length, width), f32),
            shaped((pair, length, width), f32),
        ),
        (queries, keys, values, after(attn_grad, qg_rounds.sent[1]), states),
        2,
    )
    key_grad, value_grad = kernel_call(
        final_body,
        (shaped((pair, length, width), bf16), shaped((pair, length, width), bf16)),
        (keys, values, key_part, value_part, qg_own, qg_rounds.below, qg_rounds.above),
    )

    if split:
        ups = jnp.stack(gather_xor(after(ups, qg_rounds.sent[1]), "head"))
        even = {0: hidden}
        bit = n_seq // 2
        while bit > 1:
            for m in list(even):
                block = even[m] if m == 0 else after(even[m], qg_rounds.sent[1])
                even[m ^ bit] = xor_permute(block, "seq", bit)
            bit //= 2
        order = [0, 2] + [m for m in range(4, n_seq, 2)]
        groups = [order[: n_seq // 4], order[n_seq // 4 :]]
        held, slots = [], []
        for i, group in enumerate(groups):
            block = after(jnp.stack([even[m] for m in group]), qg_rounds.sent[i + 1])
            held += [block, xor_permute(block, "seq", 1)]
            slots += [group, [m ^ 1 for m in group]]
        weight_grad = weight_grad_of(held[:3], slots[:3], ups, spot, None)
        weight_grad = weight_grad_of(held[3:], slots[3:], ups, spot, weight_grad)
    else:
        full_up = lax.all_gather(flat_up, "head", axis=1, tiled=True)
        weight_grad = lax.psum_scatter(
            mm(full_up, hidden, TN), "seq", scatter_dimension=0, tiled=True
        ).T

    return (
        output.reshape(pair, length, -1),
        query_grad,
        key_grad,
        value_grad,
        weight_grad,
    )


def solution(mesh):
    rows = P(None, "seq", "head")
    return jax.shard_map(
        on_device,
        mesh=mesh,
        in_specs=(rows, rows, rows, P("head", None), rows),
        out_specs=(rows, rows, rows, rows, P("head", "seq")),
        check_vma=False,
    )
```

time: 91.3 us -> 71.1 us (0.78)
  between operations: 14.3 us -> 0.91 us
  starting transfers between devices: 30 us -> 24.4 us
  local copies, waits for them, and re-layouts: 5.34 us -> 0.05 us
  waiting for transfers between devices: 25.4 us -> 28.8 us
  Pallas kernels: 13.6 us -> 14.8 us
    unnamed x18 -> x6, local copies, waits for them, and re-layouts: 5.34 us -> 0.02 us
    ppermute x16 -> x22, waiting for transfers between devices: 23.8 us -> 28.8 us  [xor_permute(): return lax.ppermute(x, axis, [(i, i ^ bit) for i in range(count)])]
    ppermute x2 -> x0, starting transfers between devices: 3.69 us -> none  [on_device(): got.append(lax.ppermute(piece, ('seq', 'head'), pairs))]
    pallas_call x4 -> x6, Pallas kernels: 5.28 us -> 7.09 us  [kernel_call(): pl.pallas_call(body, out_shape=outs, in_specs=whole(len(args)), out_specs...]
    ppermute x16 -> x22, starting transfers between devices: 26.2 us -> 24.4 us  [xor_permute(): return lax.ppermute(x, axis, [(i, i ^ bit) for i in range(count)])]
    ppermute x2 -> x0, waiting for transfers between devices: 1.52 us -> none  [on_device(): got.append(lax.ppermute(piece, ('seq', 'head'), pairs))]
    select_n x5 -> x4, other arithmetic: 1.25 us -> 0.23 us  [the longest x2 0.2 us: __init__(): above = jnp.where(upper, above, above + got_both)]
    pallas_call x3 -> x5, Pallas kernels: 8.34 us -> 7.69 us  [the longest x2 2.99 us: weight_grad_of(): pl.pallas_call(functools.partial(weight_body, slots, before is None), out...]
  transfers between devices with their start and end apart: 20 -> 22, of which waited for: 9 -> 10; matrix products, arithmetic and copies ran while one was open for 2% -> 2% of each run, Pallas kernels for 15% -> 19%
where the time goes in v2:
time: 71.1 us; the launch traced here: 71 us
  waiting for transfers between devices  28.8 us (41%)
  starting transfers between devices  24.4 us (34%)
  Pallas kernels  14.8 us (21%)
  other arithmetic  2.01 us (3%)
  between operations  0.91 us (1%)
    ppermute x22, waiting for transfers between devices, xor_permute(): return lax.ppermute(x, axis, [(i, i ^ bit) for i in range(count)])  28.8 us
    ppermute x22, starting transfers between devices, xor_permute(): return lax.ppermute(x, axis, [(i, i ^ bit) for i in range(count)])  24.4 us
    pallas_call x6, Pallas kernels, kernel_call(): pl.pallas_call(body, out_shape=outs, in_specs=whole(len(args)), out_specs...  7.09 us
    pallas_call x2, Pallas kernels, weight_grad_of(): pl.pallas_call(functools.partial(weight_body, slots, before is None), out...  2.99 us
    pallas_call x1, Pallas kernels, near_grad_of(): pl.pallas_call(near_body, out_shape=(shaped((rows, features), jnp.float32...  2.86 us
  transfers between devices with their start and end apart: 22, of which 10 were waited for; matrix products, arithmetic and copies ran while one was open for 2% of the time, Pallas kernels for 19%

profile of v2, /device:TPU:0, one launch (start us, length us, event | category | flops | bytes accessed | tf_op | source)
XLA Modules:
  0.0 71.0 jit_solution(11065367741076565575)
XLA Ops:
  0.6 1.3 %shard_map.92 = (f32[4,128,128]{2,1,0:T(8,128)S(1)}, bf16[2,4,128,128]{3,2,1,0:T(8,128)(2,1)S(1)}) custom-call(bf16[2,64,512]{2,1,0:T(8,128)(2,1)} %k_ref.5, bf16[2,64,512]{2,1,0:T(8,128)(2,1)} %v_ref.5), custom_call_target="tpu_custom_call" | custom-call | tf_op jit(solution)/shard_map/pallas_call | solution.py:85
  1.9 3.0 %collective-permute-start.3 = (bf16[2,4,128,128]{3,2,1,0:T(8,128)(2,1)S(1)}, bf16[2,4,128,128]{3,2,1,0:T(8,128)(2,1)S(1)}, u32[]{:S(2)}, u32[]{:S(2)}) collective-permute-start(bf16[2,4,128,128]{3,2,1,0:T(8,128)(2,1)S(1)} %get-tuple-element.30), channel_id=1, source_target_pairs={{0,4},{4,0},{8,12},{12,8},{16,20},{20,16},{24,28},{28,24},{1,5},{5... | collective-permute-start | bytes 786440 | tf_op jit(solution)/shard_map/ppermute | solution.py:34
  4.9 1.5 %collective-permute-start.1 = (bf16[128,1024]{1,0:T(8,128)(2,1)}, bf16[128,1024]{1,0:T(8,128)(2,1)S(1)}, u32[]{:S(2)}, u32[]{:S(2)}) collective-permute-start(bf16[128,1024]{1,0:T(8,128)(2,1)} %bitcast.74), channel_id=1, source_target_pairs={{0,2},{1,3},{2,0},{3,1},{4,6},{5,7},{6,4},{7,5},{8,10},{9,11},{10,... | collective-permute-start | bytes 786440 | tf_op jit(solution)/shard_map/ppermute | solution.py:34
  6.4 0.1 pad_add_fusion.spot_ref
  6.5 4.7 %collective-permute-done.3 = bf16[2,4,128,128]{3,2,1,0:T(8,128)(2,1)S(1)} collective-permute-done((bf16[2,4,128,128]{3,2,1,0:T(8,128)(2,1)S(1)}, bf16[2,4,128,128]{3,2,1,0:T(8,128)(2,1)S(1)}, u32[]{:S(2)}, u32[]{:S(2)}) %collective-permute-start.3) | collective-permute-done | bytes 262176 | tf_op jit(solution)/shard_map/ppermute | solution.py:34
  11.2 0.1 fusion.2
  11.3 1.9 %collective-permute-start.4 = (bf16[2,4,128,128]{3,2,1,0:T(8,128)(2,1)S(1)}, bf16[2,4,128,128]{3,2,1,0:T(8,128)(2,1)S(1)}, u32[]{:S(2)}, u32[]{:S(2)}) collective-permute-start(bf16[2,4,128,128]{3,2,1,0:T(8,128)(2,1)S(1)} %fusion.2), channel_id=1, source_target_pairs={{0,8},{4,12},{8,0},{12,4},{16,24},{20,28},{24,16},{28,20},{1,9},{5... | collective-permute-start | bytes 786440 | tf_op jit(solution)/shard_map/ppermute | solution.py:34
  13.2 2.9 %shard_map.93 = (f32[128,512]{1,0:T(8,128)S(1)}, bf16[4,512,1024]{2,1,0:T(8,128)(2,1)S(1)}, bf16[128,1024]{1,0:T(8,128)(2,1)S(1)}) custom-call(s32[2]{0:T(128)S(1)} %pad_add_fusion.spot_ref, bf16[512,4096]{1,0:T(8,128)(2,1)} %w_hbm.1, bf16[128,1024]{1,0:T(8,128)(2,1)} %bitcast.75), custom_call_target="tpu_custom_call" | custom-call | flops 3300000000 | tf_op jit(solution)/shard_map/pallas_call | solution.py:152
  16.1 0.1 collective-permute-start.2
  16.2 2.7 %collective-permute-done.4 = bf16[2,4,128,128]{3,2,1,0:T(8,128)(2,1)S(1)} collective-permute-done((bf16[2,4,128,128]{3,2,1,0:T(8,128)(2,1)S(1)}, bf16[2,4,128,128]{3,2,1,0:T(8,128)(2,1)S(1)}, u32[]{:S(2)}, u32[]{:S(2)}) %collective-permute-start.4) | collective-permute-done | bytes 262176 | tf_op jit(solution)/shard_map/ppermute | solution.py:34
  18.9 0.1 add_convert_fusion.1
  19.0 2.5 %collective-permute-start.5 = (bf16[4,128,128]{2,1,0:T(8,128)(2,1)S(1)}, bf16[4,128,128]{2,1,0:T(8,128)(2,1)S(1)}, u32[]{:S(2)}, u32[]{:S(2)}) collective-permute-start(bf16[4,128,128]{2,1,0:T(8,128)(2,1)S(1)} %fusion.12), channel_id=1, source_target_pairs={{0,16},{4,20},{8,24},{12,28},{16,0},{20,4},{24,8},{28,12},{1,17},{... | collective-permute-start | bytes 393224 | tf_op jit(solution)/shard_map/ppermute | solution.py:34
  21.6 0.6 shard_map.100
  22.2 1.6 %collective-permute-start.14 = (bf16[4,32,512]{2,1,0:T(8,128)(2,1)S(1)}, bf16[4,32,512]{2,1,0:T(8,128)(2,1)S(1)}, u32[]{:S(2)}, u32[]{:S(2)}) collective-permute-start(bf16[4,32,512]{2,1,0:T(8,128)(2,1)S(1)} %get-tuple-element.51), channel_id=1, source_target_pairs={{0,4},{4,0},{8,12},{12,8},{16,20},{20,16},{24,28},{28,24},{1,5},{5... | collective-permute-start | bytes 393224 | tf_op jit(solution)/shard_map/ppermute | solution.py:34
  23.8 1.2 %shard_map.94.hg_ref = f32[128,512]{1,0:T(8,128)S(1)} custom-call(bf16[4,512,1024]{2,1,0:T(8,128)(2,1)S(1)} %get-tuple-element.32.w_ref, f32[128,512]{1,0:T(8,128)S(1)} %get-tuple-element.33.before_ref, bf16[128,1024]{1,0:T(8,128)(2,1)S(1)} %collective-permute-done.refs_0_.refs_1_, bf16[128,1024]{1,0:T(8,128)(2,1)S(1)} %collective-permute-done.1.refs_1_.refs_2_, ...), custom_call_target="tpu_custom_call" | custom-call | flops 2200000000 | tf_op jit(solution)/shard_map/pallas_call | solution.py:46
  25.0 1.5 %collective-permute-done.5 = bf16[4,128,128]{2,1,0:T(8,128)(2,1)S(1)} collective-permute-done((bf16[4,128,128]{2,1,0:T(8,128)(2,1)S(1)}, bf16[4,128,128]{2,1,0:T(8,128)(2,1)S(1)}, u32[]{:S(2)}, u32[]{:S(2)}) %collective-permute-start.5) | collective-permute-done | bytes 131104 | tf_op jit(solution)/shard_map/ppermute | solution.py:34
  26.5 0.1 add_select_fusion.4
  26.7 1.8 %shard_map.95 = (bf16[2,4,128,128]{3,2,1,0:T(8,128)(2,1)S(1)}, bf16[128,512]{1,0:T(8,128)(2,1)S(1)}, bf16[2,64,512]{2,1,0:T(8,128)(2,1)S(1)}, f32[4,128,128]{2,1,0:T(8,128)S(1)}, bf16[2,4,128,128]{3,2,1,0:T(8,128)(2,1)S(1)}) custom-call(bf16[2,64,512]{2,1,0:T(8,128)(2,1)S(1)} %copy-done.2, bf16[2,64,512]{2,1,0:T(8,128)(2,1)S(1)} %copy-done, ...), custom_call_target="tpu_custom_call" | custom-call | flops 550000000 | tf_op jit(solution)/shard_map/pallas_call | solution.py:46
  28.4 1.3 %collective-permute-start.6 = (bf16[2,4,128,128]{3,2,1,0:T(8,128)(2,1)S(1)}, bf16[2,4,128,128]{3,2,1,0:T(8,128)(2,1)S(1)}, u32[]{:S(2)}, u32[]{:S(2)}) collective-permute-start(bf16[2,4,128,128]{3,2,1,0:T(8,128)(2,1)S(1)} %get-tuple-element.36), channel_id=1, source_target_pairs={{0,4},{4,0},{8,12},{12,8},{16,20},{20,16},{24,28},{28,24},{1,5},{5... | collective-permute-start | bytes 786440 | tf_op jit(solution)/shard_map/ppermute | solution.py:34
  29.8 0.7 %collective-permute-start.15 = (bf16[2,2,32,512]{3,2,1,0:T(8,128)(2,1)S(1)}, bf16[2,2,32,512]{3,2,1,0:T(8,128)(2,1)S(1)}, u32[]{:S(2)}, u32[]{:S(2)}) collective-permute-start(bf16[2,2,32,512]{3,2,1,0:T(8,128)(2,1)S(1)} %get-tuple-element.52), channel_id=1, source_target_pairs={{0,8},{4,12},{8,0},{12,4},{16,24},{20,28},{24,16},{28,20},{1,9},{5... | collective-permute-start | bytes 393224 | tf_op jit(solution)/shard_map/ppermute | solution.py:34
  30.5 3.4 %collective-permute-start.11 = (bf16[128,512]{1,0:T(8,128)(2,1)S(1)}, bf16[128,512]{1,0:T(8,128)(2,1)S(1)}, u32[]{:S(2)}, u32[]{:S(2)}) collective-permute-start(bf16[128,512]{1,0:T(8,128)(2,1)S(1)} %get-tuple-element.37.hidden_ref), channel_id=1, source_target_pairs={{0,16},{4,20},{8,24},{12,28},{16,0},{20,4},{24,8},{28,12},{1,17},{... | collective-permute-start | bytes 393224 | tf_op jit(solution)/shard_map/ppermute | solution.py:34
  33.9 0.1 collective-permute-start.20
  34.0 4.6 %collective-permute-done.15 = bf16[2,2,32,512]{3,2,1,0:T(8,128)(2,1)S(1)} collective-permute-done((bf16[2,2,32,512]{3,2,1,0:T(8,128)(2,1)S(1)}, bf16[2,2,32,512]{3,2,1,0:T(8,128)(2,1)S(1)}, u32[]{:S(2)}, u32[]{:S(2)}) %collective-permute-start.15) | collective-permute-done | bytes 131104 | tf_op jit(solution)/shard_map/ppermute | solution.py:34
  38.7 0.1 fusion.3
  38.8 1.9 %collective-permute-start.9 = (bf16[2,4,128,128]{3,2,1,0:T(8,128)(2,1)S(1)}, bf16[2,4,128,128]{3,2,1,0:T(8,128)(2,1)S(1)}, u32[]{:S(2)}, u32[]{:S(2)}) collective-permute-start(bf16[2,4,128,128]{3,2,1,0:T(8,128)(2,1)S(1)} %fusion.3), channel_id=1, source_target_pairs={{0,8},{4,12},{8,0},{12,4},{16,24},{20,28},{24,16},{28,20},{1,9},{5... | collective-permute-start | bytes 786440 | tf_op jit(solution)/shard_map/ppermute | solution.py:34
  40.7 1.3 %collective-permute-done.20 = bf16[128,512]{1,0:T(8,128)(2,1)S(1)} collective-permute-done((bf16[128,512]{1,0:T(8,128)(2,1)S(1)}, bf16[128,512]{1,0:T(8,128)(2,1)S(1)}, u32[]{:S(2)}, u32[]{:S(2)}) %collective-permute-start.20) | collective-permute-done | bytes 131104 | tf_op jit(solution)/shard_map/ppermute | solution.py:34
  42.0 3.8 %collective-permute-done.16 = bf16[1,4,32,512]{3,2,1,0:T(8,128)(2,1)S(1)} collective-permute-done((bf16[1,4,32,512]{3,2,1,0:T(8,128)(2,1)S(1)}, bf16[1,4,32,512]{3,2,1,0:T(8,128)(2,1)S(1)}, u32[]{:S(2)}, u32[]{:S(2)}) %collective-permute-start.16) | collective-permute-done | bytes 131104 | tf_op jit(solution)/shard_map/ppermute | solution.py:34
  45.8 1.6 %collective-permute-start.18 = (bf16[8,32,512]{2,1,0:T(8,128)(2,1)S(1)}, bf16[8,32,512]{2,1,0:T(8,128)(2,1)S(1)}, u32[]{:S(2)}, u32[]{:S(2)}) collective-permute-start(bf16[8,32,512]{2,1,0:T(8,128)(2,1)S(1)} %maximum_bitcast_fusion), channel_id=1, source_target_pairs={{0,2},{1,3},{2,0},{3,1},{4,6},{5,7},{6,4},{7,5},{8,10},{9,11},{10,... | collective-permute-start | bytes 786440 | tf_op jit(solution)/shard_map/ppermute | solution.py:34
  47.4 0.4 shard_map.97
  47.9 0.6 collective-permute-start.7
  48.4 0.4 shard_map.96
  48.9 0.1 add_convert_fusion
  49.0 1.5 %collective-permute-start.10 = (bf16[4,128,128]{2,1,0:T(8,128)(2,1)S(1)}, bf16[4,128,128]{2,1,0:T(8,128)(2,1)S(1)}, u32[]{:S(2)}, u32[]{:S(2)}) collective-permute-start(bf16[4,128,128]{2,1,0:T(8,128)(2,1)S(1)} %fusion.11), channel_id=1, source_target_pairs={{0,16},{4,20},{8,24},{12,28},{16,0},{20,4},{24,8},{28,12},{1,17},{... | collective-permute-start | bytes 393224 | tf_op jit(solution)/shard_map/ppermute | solution.py:34
  50.6 2.2 %shard_map.98 = (bf16[2,64,512]{2,1,0:T(8,128)(2,1)}, f32[2,64,512]{2,1,0:T(8,128)S(1)}, f32[2,64,512]{2,1,0:T(8,128)S(1)}) custom-call(bf16[2,64,512]{2,1,0:T(8,128)(2,1)S(1)} %copy-done.2, bf16[2,64,512]{2,1,0:T(8,128)(2,1)S(1)} %copy-done, bf16[2,64,512]{2,1,0:T(8,128)(2,1)S(1)} %copy-done.1, bf16[2,64,512]{2,1,0:T(8,128)(2,1)S(1)} %get-tuple-element.39.g_ref, ...), custom_call_target="tpu_custom_call" | custom-call | flops 2200000000 | tf_op jit(solution)/shard_map/pallas_call | solution.py:46
  52.8 2.4 %collective-permute-done.12 = bf16[128,512]{1,0:T(8,128)(2,1)S(1)} collective-permute-done((bf16[128,512]{1,0:T(8,128)(2,1)S(1)}, bf16[128,512]{1,0:T(8,128)(2,1)S(1)}, u32[]{:S(2)}, u32[]{:S(2)}) %collective-permute-start.12) | collective-permute-done | bytes 131104 | tf_op jit(solution)/shard_map/ppermute | solution.py:34
  55.3 0.5 collective-permute-start.21
  55.8 1.6 %collective-permute-start.13 = (bf16[2,128,512]{2,1,0:T(8,128)(2,1)S(1)}, bf16[2,128,512]{2,1,0:T(8,128)(2,1)S(1)}, u32[]{:S(2)}, u32[]{:S(2)}) collective-permute-start(bf16[2,128,512]{2,1,0:T(8,128)(2,1)S(1)} %pad_maximum_fusion.1.refs_2_), channel_id=1, source_target_pairs={{0,4},{4,0},{8,12},{12,8},{16,20},{20,16},{24,28},{28,24},{1,5},{5... | collective-permute-start | bytes 786440 | tf_op jit(solution)/shard_map/ppermute | solution.py:34
  57.4 0.9 %collective-permute-done.10 = bf16[4,128,128]{2,1,0:T(8,128)(2,1)S(1)} collective-permute-done((bf16[4,128,128]{2,1,0:T(8,128)(2,1)S(1)}, bf16[4,128,128]{2,1,0:T(8,128)(2,1)S(1)}, u32[]{:S(2)}, u32[]{:S(2)}) %collective-permute-start.10) | collective-permute-done | bytes 131104 | tf_op jit(solution)/shard_map/ppermute | solution.py:34
  58.4 0.1 add_select_fusion
  58.5 1.0 %shard_map.99 = (bf16[2,64,512]{2,1,0:T(8,128)(2,1)}, bf16[2,64,512]{2,1,0:T(8,128)(2,1)}) custom-call(bf16[2,64,512]{2,1,0:T(8,128)(2,1)S(1)} %copy-done, bf16[2,64,512]{2,1,0:T(8,128)(2,1)S(1)} %copy-done.1, f32[2,64,512]{2,1,0:T(8,128)S(1)} %get-tuple-element.42.dkp_ref, f32[2,64,512]{2,1,0:T(8,128)S(1)} %get-tuple-element.43.dvp_ref, ...), custom_call_target="tpu_custom_call" | custom-call | flops 550000000 | tf_op jit(solution)/shard_map/pallas_call | solution.py:46
  59.5 0.2 add_bitcast_fusion
  59.7 0.6 collective-permute-start.8
  60.3 0.1 pad_maximum_fusion.refs_3_.refs_1_
  60.5 4.0 %collective-permute-done.21.refs_1_ = bf16[2,128,512]{2,1,0:T(8,128)(2,1)S(1)} collective-permute-done((bf16[2,128,512]{2,1,0:T(8,128)(2,1)S(1)}, bf16[2,128,512]{2,1,0:T(8,128)(2,1)S(1)}, u32[]{:S(2)}, u32[]{:S(2)}) %collective-permute-start.21) | collective-permute-done | bytes 262176 | tf_op jit(solution)/shard_map/ppermute | solution.py:34
  64.5 1.1 %shard_map.101.refs_2_ = f32[512,512]{1,0:T(8,128)S(1)} custom-call(s32[2]{0:T(128)S(1)} %pad_add_fusion.spot_ref, bf16[2,128,512]{2,1,0:T(8,128)(2,1)S(1)} %pad_maximum_fusion.2.refs_0_, bf16[2,128,512]{2,1,0:T(8,128)(2,1)S(1)} %collective-permute-done.21.refs_1_, bf16[2,128,512]{2,1,0:T(8,128)(2,1)S(1)} %pad_maximum_fusion.1.refs_2_, ...), custom_call_target="tpu_custom_call" | custom-call | flops 1100000000 | tf_op jit(solution)/shard_map/pallas_call | solution.py:299
  65.7 2.7 %collective-permute-done.13.refs_0_ = bf16[2,128,512]{2,1,0:T(8,128)(2,1)S(1)} collective-permute-done((bf16[2,128,512]{2,1,0:T(8,128)(2,1)S(1)}, bf16[2,128,512]{2,1,0:T(8,128)(2,1)S(1)}, u32[]{:S(2)}, u32[]{:S(2)}) %collective-permute-start.13) | collective-permute-done | bytes 262176 | tf_op jit(solution)/shard_map/ppermute | solution.py:34
  68.3 1.8 %shard_map.102 = f32[512,512]{1,0:T(8,128)} custom-call(s32[2]{0:T(128)S(1)} %pad_add_fusion.spot_ref, bf16[2,128,512]{2,1,0:T(8,128)(2,1)S(1)} %collective-permute-done.13.refs_0_, bf16[4,8,32,512]{3,2,1,0:T(8,128)(2,1)S(1)} %pad_maximum_fusion.refs_3_.refs_1_, f32[512,512]{1,0:T(8,128)S(1)} %shard_map.101.refs_2_), custom_call_target="tpu_custom_call" | custom-call | flops 1100000000 | tf_op jit(solution)/shard_map/pallas_call | solution.py:299
  70.2 0.8 %fusion.1 = bf16[1,128,1024]{2,1,0:T(8,128)(2,1)} fusion(f32[1,2,128,1024]{3,2,1,0:T(8,128)S(1)} %add_bitcast_fusion, bf16[1,128,1024]{2,1,0:T(8,128)(2,1)S(1)} %collective-permute-done.8), kind=kLoop, calls=%fused_computation.5 | loop fusion | flops 393216 | bytes 1048576 | tf_op jit(solution)/shard_map/convert_element_type | solution.py:332
  (35 shorter events, 0.5 us)
Async XLA Ops:
  1.9 9.3 %collective-permute-start.3 = (bf16[2,4,128,128]{3,2,1,0:T(8,128)(2,1)S(1)}, bf16[2,4,128,128]{3,2,1,0:T(8,128)(2,1)S(1)}, u32[]{:S(2)}, u32[]{:S(2)}) collective-permute-start(bf16[2,4,128,128]{3,2,1,0:T(8,128)(2,1)S(1)} %get-tuple-element.30), channel_id=1, source_target_pairs={{0,4},{4,0},{8,12},{12,8},{16,20},{20,16},{24,28},{28,24},{1,5},{5... | collective-permute-start | bytes 786440 | tf_op jit(solution)/shard_map/ppermute | solution.py:34
  4.9 16.6 %collective-permute-start = (bf16[128,1024]{1,0:T(8,128)(2,1)}, bf16[128,1024]{1,0:T(8,128)(2,1)S(1)}, u32[]{:S(2)}, u32[]{:S(2)}) collective-permute-start(bf16[128,1024]{1,0:T(8,128)(2,1)} %bitcast.73), channel_id=1, source_target_pairs={{0,1},{1,0},{2,3},{3,2},{4,5},{5,4},{6,7},{7,6},{8,9},{9,8},{10,11... | collective-permute-start | bytes 786440 | tf_op jit(solution)/shard_map/ppermute | solution.py:34
  4.9 11.1 %collective-permute-start.1 = (bf16[128,1024]{1,0:T(8,128)(2,1)}, bf16[128,1024]{1,0:T(8,128)(2,1)S(1)}, u32[]{:S(2)}, u32[]{:S(2)}) collective-permute-start(bf16[128,1024]{1,0:T(8,128)(2,1)} %bitcast.74), channel_id=1, source_target_pairs={{0,2},{1,3},{2,0},{3,1},{4,6},{5,7},{6,4},{7,5},{8,10},{9,11},{10,... | collective-permute-start | bytes 786440 | tf_op jit(solution)/shard_map/ppermute | solution.py:34
  11.3 7.6 %collective-permute-start.4 = (bf16[2,4,128,128]{3,2,1,0:T(8,128)(2,1)S(1)}, bf16[2,4,128,128]{3,2,1,0:T(8,128)(2,1)S(1)}, u32[]{:S(2)}, u32[]{:S(2)}) collective-permute-start(bf16[2,4,128,128]{3,2,1,0:T(8,128)(2,1)S(1)} %fusion.2), channel_id=1, source_target_pairs={{0,8},{4,12},{8,0},{12,4},{16,24},{20,28},{24,16},{28,20},{1,9},{5... | collective-permute-start | bytes 786440 | tf_op jit(solution)/shard_map/ppermute | solution.py:34
  16.1 5.5 %collective-permute-start.2 = (bf16[128,1024]{1,0:T(8,128)(2,1)S(1)}, bf16[128,1024]{1,0:T(8,128)(2,1)S(1)}, u32[]{:S(2)}, u32[]{:S(2)}) collective-permute-start(bf16[128,1024]{1,0:T(8,128)(2,1)S(1)} %collective-permute-done.1.refs_1_.refs_2_), channel_id=1, source_target_pairs={{0,1},{1,0},{2,3},{3,2},{4,5},{5,4},{6,7},{7,6},{8,9},{9,8},{10,11... | collective-permute-start | bytes 786440 | tf_op jit(solution)/shard_map/ppermute | solution.py:34
  19.0 7.5 %collective-permute-start.5 = (bf16[4,128,128]{2,1,0:T(8,128)(2,1)S(1)}, bf16[4,128,128]{2,1,0:T(8,128)(2,1)S(1)}, u32[]{:S(2)}, u32[]{:S(2)}) collective-permute-start(bf16[4,128,128]{2,1,0:T(8,128)(2,1)S(1)} %fusion.12), channel_id=1, source_target_pairs={{0,16},{4,20},{8,24},{12,28},{16,0},{20,4},{24,8},{28,12},{1,17},{... | collective-permute-start | bytes 393224 | tf_op jit(solution)/shard_map/ppermute | solution.py:34
  22.2 7.6 %collective-permute-start.14 = (bf16[4,32,512]{2,1,0:T(8,128)(2,1)S(1)}, bf16[4,32,512]{2,1,0:T(8,128)(2,1)S(1)}, u32[]{:S(2)}, u32[]{:S(2)}) collective-permute-start(bf16[4,32,512]{2,1,0:T(8,128)(2,1)S(1)} %get-tuple-element.51), channel_id=1, source_target_pairs={{0,4},{4,0},{8,12},{12,8},{16,20},{20,16},{24,28},{28,24},{1,5},{5... | collective-permute-start | bytes 393224 | tf_op jit(solution)/shard_map/ppermute | solution.py:34
  23.8 2.9 %copy-start = (bf16[2,64,512]{2,1,0:T(8,128)(2,1)S(1)}, bf16[2,64,512]{2,1,0:T(8,128)(2,1)}, u32[]{:S(2)}) copy-start(bf16[2,64,512]{2,1,0:T(8,128)(2,1)} %k_ref.5) | copy-start | bytes 393220
  23.8 2.9 %copy-start.1 = (bf16[2,64,512]{2,1,0:T(8,128)(2,1)S(1)}, bf16[2,64,512]{2,1,0:T(8,128)(2,1)}, u32[]{:S(2)}) copy-start(bf16[2,64,512]{2,1,0:T(8,128)(2,1)} %v_ref.5) | copy-start | bytes 393220
  23.8 2.9 %copy-start.2 = (bf16[2,64,512]{2,1,0:T(8,128)(2,1)S(1)}, bf16[2,64,512]{2,1,0:T(8,128)(2,1)}, u32[]{:S(2)}) copy-start(bf16[2,64,512]{2,1,0:T(8,128)(2,1)} %q_ref.3) | copy-start | bytes 393220
  28.4 10.2 %collective-permute-start.6 = (bf16[2,4,128,128]{3,2,1,0:T(8,128)(2,1)S(1)}, bf16[2,4,128,128]{3,2,1,0:T(8,128)(2,1)S(1)}, u32[]{:S(2)}, u32[]{:S(2)}) collective-permute-start(bf16[2,4,128,128]{3,2,1,0:T(8,128)(2,1)S(1)} %get-tuple-element.36), channel_id=1, source_target_pairs={{0,4},{4,0},{8,12},{12,8},{16,20},{20,16},{24,28},{28,24},{1,5},{5... | collective-permute-start | bytes 786440 | tf_op jit(solution)/shard_map/ppermute | solution.py:34
  29.8 8.8 %collective-permute-start.15 = (bf16[2,2,32,512]{3,2,1,0:T(8,128)(2,1)S(1)}, bf16[2,2,32,512]{3,2,1,0:T(8,128)(2,1)S(1)}, u32[]{:S(2)}, u32[]{:S(2)}) collective-permute-start(bf16[2,2,32,512]{3,2,1,0:T(8,128)(2,1)S(1)} %get-tuple-element.52), channel_id=1, source_target_pairs={{0,8},{4,12},{8,0},{12,4},{16,24},{20,28},{24,16},{28,20},{1,9},{5... | collective-permute-start | bytes 393224 | tf_op jit(solution)/shard_map/ppermute | solution.py:34
  30.5 17.9 %collective-permute-start.11 = (bf16[128,512]{1,0:T(8,128)(2,1)S(1)}, bf16[128,512]{1,0:T(8,128)(2,1)S(1)}, u32[]{:S(2)}, u32[]{:S(2)}) collective-permute-start(bf16[128,512]{1,0:T(8,128)(2,1)S(1)} %get-tuple-element.37.hidden_ref), channel_id=1, source_target_pairs={{0,16},{4,20},{8,24},{12,28},{16,0},{20,4},{24,8},{28,12},{1,17},{... | collective-permute-start | bytes 393224 | tf_op jit(solution)/shard_map/ppermute | solution.py:34
  33.9 8.1 %collective-permute-start.20 = (bf16[128,512]{1,0:T(8,128)(2,1)S(1)}, bf16[128,512]{1,0:T(8,128)(2,1)S(1)}, u32[]{:S(2)}, u32[]{:S(2)}) collective-permute-start(bf16[128,512]{1,0:T(8,128)(2,1)S(1)} %get-tuple-element.37.hidden_ref), channel_id=1, source_target_pairs={{0,8},{4,12},{8,0},{12,4},{16,24},{20,28},{24,16},{28,20},{1,9},{5... | collective-permute-start | bytes 393224 | tf_op jit(solution)/shard_map/ppermute | solution.py:34
  38.6 7.2 %collective-permute-start.16 = (bf16[1,4,32,512]{3,2,1,0:T(8,128)(2,1)S(1)}, bf16[1,4,32,512]{3,2,1,0:T(8,128)(2,1)S(1)}, u32[]{:S(2)}, u32[]{:S(2)}) collective-permute-start(bf16[1,4,32,512]{3,2,1,0:T(8,128)(2,1)S(1)} %get-tuple-element.60), channel_id=1, source_target_pairs={{0,16},{4,20},{8,24},{12,28},{16,0},{20,4},{24,8},{28,12},{1,17},{... | collective-permute-start | bytes 393224 | tf_op jit(solution)/shard_map/ppermute | solution.py:34
  38.8 10.1 %collective-permute-start.9 = (bf16[2,4,128,128]{3,2,1,0:T(8,128)(2,1)S(1)}, bf16[2,4,128,128]{3,2,1,0:T(8,128)(2,1)S(1)}, u32[]{:S(2)}, u32[]{:S(2)}) collective-permute-start(bf16[2,4,128,128]{3,2,1,0:T(8,128)(2,1)S(1)} %fusion.3), channel_id=1, source_target_pairs={{0,8},{4,12},{8,0},{12,4},{16,24},{20,28},{24,16},{28,20},{1,9},{5... | collective-permute-start | bytes 786440 | tf_op jit(solution)/shard_map/ppermute | solution.py:34
  45.8 10.0 %collective-permute-start.18 = (bf16[8,32,512]{2,1,0:T(8,128)(2,1)S(1)}, bf16[8,32,512]{2,1,0:T(8,128)(2,1)S(1)}, u32[]{:S(2)}, u32[]{:S(2)}) collective-permute-start(bf16[8,32,512]{2,1,0:T(8,128)(2,1)S(1)} %maximum_bitcast_fusion), channel_id=1, source_target_pairs={{0,2},{1,3},{2,0},{3,1},{4,6},{5,7},{6,4},{7,5},{8,10},{9,11},{10,... | collective-permute-start | bytes 786440 | tf_op jit(solution)/shard_map/ppermute | solution.py:34
  47.4 12.9 %collective-permute-start.17 = (bf16[8,32,512]{2,1,0:T(8,128)(2,1)S(1)}, bf16[8,32,512]{2,1,0:T(8,128)(2,1)S(1)}, u32[]{:S(2)}, u32[]{:S(2)}) collective-permute-start(bf16[8,32,512]{2,1,0:T(8,128)(2,1)S(1)} %maximum_bitcast_fusion), channel_id=1, source_target_pairs={{0,1},{1,0},{2,3},{3,2},{4,5},{5,4},{6,7},{7,6},{8,9},{9,8},{10,11... | collective-permute-start | bytes 786440 | tf_op jit(solution)/shard_map/ppermute | solution.py:34
  47.9 11.6 %collective-permute-start.7 = (bf16[2,128,1024]{2,1,0:T(8,128)(2,1)S(1)}, bf16[2,128,1024]{2,1,0:T(8,128)(2,1)S(1)}, u32[]{:S(2)}, u32[]{:S(2)}) collective-permute-start(bf16[2,128,1024]{2,1,0:T(8,128)(2,1)S(1)} %shard_map.97), channel_id=1, source_target_pairs={{0,1},{1,0},{2,3},{3,2},{4,5},{5,4},{6,7},{7,6},{8,9},{9,8},{10,11... | collective-permute-start | bytes 1572872 | tf_op jit(solution)/shard_map/ppermute | solution.py:34
  48.4 6.8 %collective-permute-start.12 = (bf16[128,512]{1,0:T(8,128)(2,1)S(1)}, bf16[128,512]{1,0:T(8,128)(2,1)S(1)}, u32[]{:S(2)}, u32[]{:S(2)}) collective-permute-start(bf16[128,512]{1,0:T(8,128)(2,1)S(1)} %collective-permute-done.11), channel_id=1, source_target_pairs={{0,8},{4,12},{8,0},{12,4},{16,24},{20,28},{24,16},{28,20},{1,9},{5... | collective-permute-start | bytes 393224 | tf_op jit(solution)/shard_map/ppermute | solution.py:34
  49.0 9.3 %collective-permute-start.10 = (bf16[4,128,128]{2,1,0:T(8,128)(2,1)S(1)}, bf16[4,128,128]{2,1,0:T(8,128)(2,1)S(1)}, u32[]{:S(2)}, u32[]{:S(2)}) collective-permute-start(bf16[4,128,128]{2,1,0:T(8,128)(2,1)S(1)} %fusion.11), channel_id=1, source_target_pairs={{0,16},{4,20},{8,24},{12,28},{16,0},{20,4},{24,8},{28,12},{1,17},{... | collective-permute-start | bytes 393224 | tf_op jit(solution)/shard_map/ppermute | solution.py:34
  55.3 9.2 %collective-permute-start.21 = (bf16[2,128,512]{2,1,0:T(8,128)(2,1)S(1)}, bf16[2,128,512]{2,1,0:T(8,128)(2,1)S(1)}, u32[]{:S(2)}, u32[]{:S(2)}) collective-permute-start(bf16[2,128,512]{2,1,0:T(8,128)(2,1)S(1)} %pad_maximum_fusion.2.refs_0_), channel_id=1, source_target_pairs={{0,4},{4,0},{8,12},{12,8},{16,20},{20,16},{24,28},{28,24},{1,5},{5... | collective-permute-start | bytes 786440 | tf_op jit(solution)/shard_map/ppermute | solution.py:34
  55.8 12.5 %collective-permute-start.13 = (bf16[2,128,512]{2,1,0:T(8,128)(2,1)S(1)}, bf16[2,128,512]{2,1,0:T(8,128)(2,1)S(1)}, u32[]{:S(2)}, u32[]{:S(2)}) collective-permute-start(bf16[2,128,512]{2,1,0:T(8,128)(2,1)S(1)} %pad_maximum_fusion.1.refs_2_), channel_id=1, source_target_pairs={{0,4},{4,0},{8,12},{12,8},{16,20},{20,16},{24,28},{28,24},{1,5},{5... | collective-permute-start | bytes 786440 | tf_op jit(solution)/shard_map/ppermute | solution.py:34
  58.4 2.0 %collective-permute-start.19 = (bf16[8,32,512]{2,1,0:T(8,128)(2,1)S(1)}, bf16[8,32,512]{2,1,0:T(8,128)(2,1)S(1)}, u32[]{:S(2)}, u32[]{:S(2)}) collective-permute-start(bf16[8,32,512]{2,1,0:T(8,128)(2,1)S(1)} %collective-permute-done.18), channel_id=1, source_target_pairs={{0,1},{1,0},{2,3},{3,2},{4,5},{5,4},{6,7},{7,6},{8,9},{9,8},{10,11... | collective-permute-start | bytes 786440 | tf_op jit(solution)/shard_map/ppermute | solution.py:34
  59.7 10.5 %collective-permute-start.8 = (bf16[1,128,1024]{2,1,0:T(8,128)(2,1)S(1)}, bf16[1,128,1024]{2,1,0:T(8,128)(2,1)S(1)}, u32[]{:S(2)}, u32[]{:S(2)}) collective-permute-start(bf16[1,128,1024]{2,1,0:T(8,128)(2,1)S(1)} %fusion.4), channel_id=1, source_target_pairs={{0,2},{1,3},{2,0},{3,1},{4,6},{5,7},{6,4},{7,5},{8,10},{9,11},{10,... | collective-permute-start | bytes 786440 | tf_op jit(solution)/shard_map/ppermute | solution.py:34

commit v3 on v2

--- a/solution.py
+++ b/solution.py
@@ -9,6 +9,11 @@
 
 HEAD_DIM = 128
 EPS = 1e-06
+CFG = {'x4': 1, 'got4_r3': 0, 'near_r2': 0, 'cost_inside': 1, 'inside': 1, 'quarter_r3': 1, 'wg': 1, 'rs_r3': 0, 'out_final': 1, 'a2_r1': 0, 'cost_wga': 2, 'final_wga': 0, 'project': 0, 'cost_stack': 0.5, 'out_wgb': 1, 'got4': 2, 'g3': 1, 'cost_kv': 5, 'cost_forward': 0.2, 'cost_final': 1, 'up4_late': 0, 'first_got': 0, 'got6_r3': 1, 'wga_final': 1, 'cost_join_kv': 0.01, 'cost_project': 0.2, 'first_r3': 1, 'quarter_far': 0, 'cost_wgb': 0.5, 'q_fwd': 1, 'gtrick': 0, 'got2': 1, 'q_when': 0}
+
+
+def cfg(name, default=0):
+    return CFG.get(name, default)
 
 NN = (((1,), (0,)), ((), ()))
 NT = (((1,), (1,)), ((), ()))
@@ -38,18 +43,20 @@
     return [pl.BlockSpec(memory_space=pltpu.VMEM)] * n
 
 
-def lasting(us):
+def lasting(name, us):
+    us = cfg("cost_" + name, us)
     return pl.CostEstimate(flops=int(us * 1.1e9), bytes_accessed=0, transcendentals=0)
 
 
-def kernel_call(body, outs, args, us=0.5, vmem=16 * 2**20):
+def kernel_call(name, body, outs, args, us=0.5, vmem=16 * 2**20):
     return pl.pallas_call(
         body,
         out_shape=outs,
         in_specs=whole(len(args)),
         out_specs=whole(len(outs)),
         compiler_params=pltpu.CompilerParams(vmem_limit_bytes=vmem),
-        cost_estimate=lasting(us),
+        cost_estimate=lasting(name, us),
+        name=name,
     )(*args)
 
 
@@ -96,32 +103,60 @@
     )(keys, values)
 
 
+def join_body(a_ref, b_ref, out_ref):
+    out_ref[...] = (a_ref[...].astype(jnp.float32) + b_ref[...].astype(jnp.float32)).astype(out_ref.dtype)
+
+
+def swap_body(send_ref, q_ref, g_ref, next_ref, got_ref):
+    for i in range(q_ref.shape[2] // HEAD_DIM):
+        c = head_cols(i)
+        first = mm(q_ref[0, :, c], g_ref[0, :, c], TN)
+        second = mm(q_ref[1, :, c], g_ref[1, :, c], TN)
+        for at, term in enumerate((second, first + second)):
+            got_ref[at, i] = term.astype(jnp.bfloat16)
+            next_ref[at, i] = (send_ref[at, i].astype(jnp.float32) + term).astype(jnp.bfloat16)
+
+
 class Rounds:
-    def __init__(self, near, send, axis, ahead):
-        count = lax.axis_size(axis)
-        place = lax.axis_index(axis)
-        below = jnp.zeros_like(near)
-        above = jnp.zeros_like(near)
-        group = send.astype(jnp.float32)
+    def __init__(self, name, near, send, axis, ahead, rounds=None, swap=None):
+        self.name, self.swap = name, swap
+        self.axis, self.rounds, self.bit = axis, rounds, 1
+        self.below = jnp.zeros_like(near)
+        self.above = jnp.zeros_like(near)
+        self.next = send
         self.sent = []
-        bit = 1
-        while bit < count:
+        self.go_on(ahead)
+
+    def go_on(self, ahead):
+        count = lax.axis_size(self.axis)
+        place = lax.axis_index(self.axis)
+        while self.bit < count and len(self.sent) != self.rounds:
+            bit, send = self.bit, self.next
             upper = (place & bit) != 0
             last = 2 * bit == count
             if last:
                 send = jnp.where(upper, send[1], send[0])
             if bit in ahead:
                 send = after(send, *ahead[bit])
-            self.sent.append(send)
-            got = xor_permute(send, axis, bit).astype(jnp.float32)
+            if bit == 1 and self.swap:
+                theirs, mine = self.swap
+                if bit in ahead:
+                    mine = after(mine, *ahead[bit])
+                self.sent.append(mine)
+                got = xor_permute(mine, self.axis, bit)
+                shape = shaped(send.shape, send.dtype)
+                self.next, got = kernel_call("swap", swap_body, (shape, shape), (send, theirs, got))
+            else:
+                self.sent.append(send)
+                got = xor_permute(send, self.axis, bit)
+            if not last and not (bit == 1 and self.swap):
+                self.next = kernel_call("join_" + self.name, join_body, (shaped(send.shape, send.dtype),), (send, got), 0.1)[0]
+            got = got.astype(jnp.float32)
             got_near, got_both = (got, got) if last else (got[0], got[1])
-            below = jnp.where(upper, below + got_near, below)
-            above = jnp.where(upper, above, above + got_both)
-            if not last:
-                group = group + got
-                send = group.astype(jnp.bfloat16)
-            bit *= 2
-        self.below, self.above = below, above
+            self.below = jnp.where(upper, self.below + got_near, self.below)
+            self.above = jnp.where(upper, self.above, self.above + got_both)
+            self.bit *= 2
+        self.rounds = None
 
 
 def pick(table, at):
@@ -160,7 +195,8 @@
         out_specs=whole(3),
         scratch_shapes=[pltpu.SemaphoreType.DMA((n + 1,))],
         compiler_params=pltpu.CompilerParams(vmem_limit_bytes=16 * 2**20),
-        cost_estimate=lasting(3),
+        cost_estimate=lasting("near", 3),
+        name="near",
     )(spot, weight, up)
 
 
@@ -234,7 +270,7 @@
 
 def project(hidden, by_columns, slots, dtype):
     shape = (len(slots), hidden.shape[0], by_columns.shape[2])
-    return kernel_call(functools.partial(project_body, slots), (shaped(shape, dtype),), (by_columns, hidden))[0]
+    return kernel_call("project", functools.partial(project_body, slots), (shaped(shape, dtype),), (by_columns, hidden))[0]
 
 
 def quarter_body(n, spot_ref, *refs):
@@ -250,32 +286,33 @@
         send_ref[entry] = chunks[m][rows, pl.ds(pl.multiple_of((1 - odd) * cols, cols), cols)]
 
 
-def columns_by_place(chunks, spot, waits):
+def share_out(chunks, spot):
     n = len(chunks)
     rows, cols = chunks[0].shape
     part = shaped((n, rows // n, cols // 2), chunks[0].dtype)
-    keep, send = pl.pallas_call(
+    return pl.pallas_call(
         functools.partial(quarter_body, n),
         out_shape=(part, part),
         in_specs=[pl.BlockSpec(memory_space=pltpu.SMEM)] + whole(n),
         out_specs=whole(2),
         compiler_params=pltpu.CompilerParams(vmem_limit_bytes=16 * 2**20),
-        cost_estimate=lasting(0.5),
+        cost_estimate=lasting("quarter", 0.5),
+        name="quarter",
     )(spot, *chunks)
-    got = xor_permute(send, "seq", 1)
+
+
+def columns_by_place(keep, send):
+    n = keep.shape[0]
+    got = first_got = xor_permute(send, "seq", 1)
     held = jnp.stack([keep, got], axis=1)
     bit = 1
-    while bit < n:
+    while 2 * bit < n:
         half = held.shape[0] // 2
-        send = held[half:]
-        if bit in waits:
-            send = after(send, *waits[bit])
-        got = xor_permute(send, "seq", 2 * bit)
+        got = xor_permute(held[half:], "seq", 2 * bit)
         held = jnp.concatenate([held[:half], got], axis=1)
         bit *= 2
-        if bit < n:
-            held = jnp.concatenate([held[0::2], held[1::2]])
-    return held[0]
+        held = jnp.concatenate([held[0::2], held[1::2]])
+    return held[0], held[1], got, first_got
 
 
 def weight_body(slots, first, spot_ref, *refs):
@@ -293,7 +330,7 @@
     out_ref[...] = total if first else refs[-2][...] + total
 
 
-def weight_grad_of(hiddens, slots, ups, spot, before):
+def weight_grad_of(name, hiddens, slots, ups, spot, before):
     features, cols = hiddens[0].shape[2], ups.shape[3]
     args = list(hiddens) + [ups] + ([] if before is None else [before])
     return pl.pallas_call(
@@ -302,7 +339,8 @@
         in_specs=[pl.BlockSpec(memory_space=pltpu.SMEM)] + whole(len(args)),
         out_specs=pl.BlockSpec(memory_space=pltpu.VMEM),
         compiler_params=pltpu.CompilerParams(vmem_limit_bytes=16 * 2**20),
-        cost_estimate=lasting(1),
+        cost_estimate=lasting(name, 1),
+        name=name,
     )(spot, *args)
 
 
@@ -316,20 +354,52 @@
     return [held[m] for m in range(len(held))]
 
 
+def gather_far(x, axis):
+    held = {0: x}
+    bit = lax.axis_size(axis) // 2
+    while bit > 1:
+        for m in list(held):
+            held[m ^ bit] = xor_permute(held[m], axis, bit)
+        bit //= 2
+    return held
+
+
+def stack_body(*refs):
+    for i, ref in enumerate(refs[:-1]):
+        refs[-1][i] = ref[...]
+
+
+def stacked(blocks, us):
+    shape = (len(blocks),) + blocks[0].shape
+    return kernel_call("stack", stack_body, (shaped(shape, blocks[0].dtype),), blocks, us)[0]
+
+
 def after(x, *others):
+    if not others:
+        return x
     return lax.optimization_barrier((x,) + others)[0]
 
 
-def reduce_columns(away, home):
-    got = xor_permute(away, "head", 1)
-    total = home + got.astype(jnp.float32)
-    bit = 2
-    while bit < lax.axis_size("head"):
-        total = total.reshape((-1, 2) + total.shape[1:])
-        got = xor_permute(total[:, 1].astype(jnp.bfloat16), "head", bit)
-        total = total[:, 0] + got.astype(jnp.float32)
-        bit *= 2
-    return total[0].astype(jnp.bfloat16)
+class Columns:
+    def __init__(self, away, home):
+        self.got = xor_permute(away, "head", 1)
+        self.total = home + self.got.astype(jnp.float32)
+        self.bit = 2
+        self.split()
+
+    def split(self):
+        self.send = None
+        if self.bit < lax.axis_size("head"):
+            total = self.total.reshape((-1, 2) + self.total.shape[1:])
+            self.total, self.send = total[:, 0], total[:, 1].astype(jnp.bfloat16)
+
+    def finish(self):
+        while self.send is not None:
+            got = xor_permute(self.send, "head", self.bit)
+            self.total = self.total + got.astype(jnp.float32)
+            self.bit *= 2
+            self.split()
+        return self.total[0].astype(jnp.bfloat16)
 
 
 def on_device(queries, keys, values, out_weight, upstream):
@@ -342,7 +412,7 @@
     square = (heads, HEAD_DIM, HEAD_DIM)
     flat_up = upstream.reshape(rows, own_cols)
     spot = jnp.stack([seq, head]).astype(jnp.int32)
-    split = n_seq == 2 * n_head
+    split = n_seq == 8 and n_head == 4
 
     kv_own, kv_send = kv_products(in_hbm(keys), in_hbm(values))
     sent_up = after(flat_up, kv_send)
@@ -350,17 +420,39 @@
     near_grad, by_columns, chunks[0] = near_grad_of(
         in_hbm(sent_up), in_hbm(out_weight), spot, n_head
     )
+    far_before = near_grad
+    if split:
+        shares = share_out(chunks, spot)
+        if cfg("quarter_far"):
+            far_before = after(near_grad, shares[1])
     hidden_grad = kernel_call(
+        "far",
         functools.partial(far_body, range(1, n_head)),
         (shaped((rows, width), f32),),
-        [by_columns, near_grad] + chunks[1:],
+        [by_columns, far_before] + chunks[1:],
         2,
     )[0]
-    kv_rounds = Rounds(kv_own, kv_send, "seq", {})
-    if split:
-        ups = columns_by_place(chunks, spot, {1: (kv_rounds.sent[-1],)})
+    ahead = {}
+    if cfg("near_r2", 1):
+        ahead[2] = (near_grad,)
+    if split and cfg("quarter_r3"):
+        ahead[n_seq // 2] = (shares[1],)
+    kv_rounds = Rounds("kv", kv_own, kv_send, "seq", ahead)
+    kv_below = kv_rounds.below
+    if cfg("gtrick"):
+        due_after = [kv_send, kv_rounds.sent[1], kv_rounds.sent[2]][cfg("q_when", 1)]
+        their_queries = xor_permute(after(queries, due_after), "seq", 1)
+        if cfg("q_fwd"):
+            kv_below = after(kv_below, their_queries)
+    ahead = {1: (), 2: (), 4: ()}
+    if split:
+        ups_keep, ups_send, ups_got, ups_got1 = columns_by_place(*shares)
+        kv_below = after(kv_below, *[(), (ups_got1,), (ups_got,)][cfg("fwd_a", 0)])
+        if cfg("a2_r1"):
+            ahead[1] = (ups_got,)
 
     states, hidden, attn_grad, qg_own, qg_send = kernel_call(
+        "forward",
         forward_body,
         (
             shaped((2,) + square, bf16),
@@ -369,49 +461,109 @@
             shaped(square, f32),
             shaped((2,) + square, bf16),
         ),
-        (queries, keys, values, hidden_grad, kv_own, kv_rounds.below, kv_rounds.above),
+        (queries, keys, values, hidden_grad, kv_own, kv_below, kv_rounds.above),
     )
-    qg_rounds = Rounds(qg_own, qg_send, "seq", {})
-
-    late = after(hidden, qg_rounds.sent[1])
+
+    def due(x, rule):
+        return x if rule == 0 else after(x, qg_rounds.sent[rule])
+
+    even = {0: hidden}
+    if split:
+        if cfg("x4", 1):
+            across = jnp.stack([hidden, ups_send.reshape(hidden.shape)])
+            across = xor_permute(across, "seq", n_seq // 2)
+            got4, got_up = across[0], across[1].reshape(ups_keep.shape)
+        else:
+            got4 = xor_permute(hidden, "seq", n_seq // 2)
+            got_up = xor_permute(ups_send, "seq", n_seq // 2)
+        got2 = xor_permute(hidden, "seq", 2)
+        if cfg("got2_r2"):
+            ahead[2] += (got2,)
+        if cfg("up4_r2"):
+            ahead[2] += (got_up,)
+    swap = (their_queries, attn_grad) if cfg("gtrick") else None
+    qg_rounds = Rounds("qg", qg_own, qg_send, "seq", ahead, 2, swap)
+
+    late = due(hidden, cfg("project", 1))
     away = project(late, by_columns, range(1, n_head, 2), bf16)
     home = project(late, by_columns, range(0, n_head, 2), f32)
-    output = reduce_columns(away, home)
+    sums = Columns(away, home)
+    ahead = ()
+    if cfg("rs_r3", 1):
+        ahead += (sums.got,)
+    if split:
+        even[2] = due(got2, cfg("got2", 1))
+        if not cfg("up4_late"):
+            ups = jnp.concatenate([ups_keep, due(got_up, cfg("up4", 1))])
+            ups = gather_far(ups, "head")
+            if cfg("g_r3"):
+                ahead += (ups[2],)
+        first_rows = stacked([hidden, even[2]], 0.1)
+        first_got = xor_permute(first_rows, "seq", 1)
+        if cfg("first_r3"):
+            ahead += (first_got,)
+        if cfg("h6", 0) == 0:
+            got6 = xor_permute(even[2], "seq", n_seq // 2)
+        if cfg("got4_r3"):
+            ahead += (got4,)
+        if cfg("got6_r3") and cfg("h6", 0) == 0:
+            ahead += (got6,)
+    qg_rounds.go_on({n_seq // 2: ahead})
+    third = qg_rounds.sent[2]
+    if split:
+        even[4] = due(got4, cfg("got4", 2))
+        if cfg("h6", 0):
+            got6 = xor_permute(even[4], "seq", 2)
+        even[6] = due(got6, cfg("got6", 2))
+        second_rows = stacked([even[4], even[6]], 0.1)
+        second_got = xor_permute(second_rows, "seq", 1)
+        if cfg("up4_late"):
+            ups = jnp.concatenate([ups_keep, after(got_up, third)])
+            ups = gather_far(ups, "head")
+        ups[1] = xor_permute(due(ups[0], cfg("g1", 0)), "head", 1)
+        ups[3] = xor_permute(due(ups[2], cfg("g3", 2)), "head", 1)
+        ups = jnp.stack([ups[m] for m in range(n_head)])
+        first_got = due(first_got, cfg("first_got", 2))
+    output = sums.finish()
 
     query_grad, key_part, value_part = kernel_call(
+        "inside",
         inside_body,
         (
             shaped((pair, length, width), bf16),
             shaped((pair, length, width), f32),
             shaped((pair, length, width), f32),
         ),
-        (queries, keys, values, after(attn_grad, qg_rounds.sent[1]), states),
+        (queries, keys, values, due(attn_grad, cfg("inside", 1)), states),
         2,
     )
+    if cfg("out_final"):
+        key_part = after(key_part, output)
+    if split:
+        if cfg("wg", 0) == 0:
+            weight_part = weight_grad_of("wga", [first_rows, first_got], [[0, 2], [1, 3]], ups, spot, None)
+            if cfg("wga_final"):
+                key_part = after(key_part, weight_part)
     key_grad, value_grad = kernel_call(
+        "final",
         final_body,
         (shaped((pair, length, width), bf16), shaped((pair, length, width), bf16)),
         (keys, values, key_part, value_part, qg_own, qg_rounds.below, qg_rounds.above),
     )
-
-    if split:
-        ups = jnp.stack(gather_xor(after(ups, qg_rounds.sent[1]), "head"))
-        even = {0: hidden}
-        bit = n_seq // 2
-        while bit > 1:
-            for m in list(even):
-                block = even[m] if m == 0 else after(even[m], qg_rounds.sent[1])
-                even[m ^ bit] = xor_permute(block, "seq", bit)
-            bit //= 2
-        order = [0, 2] + [m for m in range(4, n_seq, 2)]
-        groups = [order[: n_seq // 4], order[n_seq // 4 :]]
-        held, slots = [], []
-        for i, group in enumerate(groups):
-            block = after(jnp.stack([even[m] for m in group]), qg_rounds.sent[i + 1])
-            held += [block, xor_permute(block, "seq", 1)]
-            slots += [group, [m ^ 1 for m in group]]
-        weight_grad = weight_grad_of(held[:3], slots[:3], ups, spot, None)
-        weight_grad = weight_grad_of(held[3:], slots[3:], ups, spot, weight_grad)
+    if split:
+        if cfg("wg", 0) == 0:
+            deps = [key_grad] + ([output] if cfg("out_wgb", 1) else [])
+            if cfg("final_wga"):
+                weight_part = after(weight_part, *deps)
+                second_got = after(second_got, weight_part)
+            else:
+                second_got = after(second_got, *deps)
+            weight_grad = weight_grad_of("wgb", [second_rows, second_got], [[4, 6], [5, 7]], ups, spot, weight_part)
+        else:
+            second_got = after(second_got, key_grad)
+            weight_grad = weight_grad_of(
+                "wgb", [first_rows, first_got, second_rows, second_got], [[0, 2], [1, 3], [4, 6], [5, 7]], ups, spot, None
+            )
     else:
         full_up = lax.all_gather(flat_up, "head", axis=1, tiled=True)
         weight_grad = lax.psum_scatter(

time: 71.1 us -> 64.4 us (0.906)
  waiting for transfers between devices: 28.8 us -> 22.7 us
    ppermute x22 -> x21, waiting for transfers between devices: 28.8 us -> 22.7 us  [xor_permute(): return lax.ppermute(x, axis, [(i, i ^ bit) for i in range(count)])]
    pallas_call x2 -> x1, Pallas kernels: 2.99 us -> 2.26 us  [weight_grad_of(): pl.pallas_call(functools.partial(weight_body, slots, before is None), out...]
    pallas_call x6 -> x12, Pallas kernels: 7.09 us -> 7.4 us  [kernel_call(): pl.pallas_call(body, out_shape=outs, in_specs=whole(len(args)), out_specs...]
    ppermute x22 -> x21, starting transfers between devices: 24.4 us -> 24.5 us  [xor_permute(): return lax.ppermute(x, axis, [(i, i ^ bit) for i in range(count)])]
  transfers between devices with their start and end apart: 22 -> 21, of which waited for: 10 -> 7; matrix products, arithmetic and copies ran while one was open for 2% -> 2% of each run, Pallas kernels for 19% -> 17%
where the time goes in v3:
time: 64.4 us; the launch traced here: 64.2 us
  starting transfers between devices  24.5 us (38%)
  waiting for transfers between devices  22.7 us (35%)
  Pallas kernels  14.4 us (22%)
  other arithmetic  1.65 us (3%)
  between operations  0.94 us (1%)
    ppermute x21, starting transfers between devices, xor_permute(): return lax.ppermute(x, axis, [(i, i ^ bit) for i in range(count)])  24.5 us
    ppermute x21, waiting for transfers between devices, xor_permute(): return lax.ppermute(x, axis, [(i, i ^ bit) for i in range(count)])  22.7 us
    pallas_call x12, Pallas kernels, kernel_call(): pl.pallas_call(body, out_shape=outs, in_specs=whole(len(args)), out_specs...  7.4 us
    pallas_call x1, Pallas kernels, near_grad_of(): pl.pallas_call(near_body, out_shape=(shaped((rows, features), jnp.float32...  2.86 us
    pallas_call x1, Pallas kernels, weight_grad_of(): pl.pallas_call(functools.partial(weight_body, slots, before is None), out...  2.26 us
  transfers between devices with their start and end apart: 21, of which 7 were waited for; matrix products, arithmetic and copies ran while one was open for 2% of the time, Pallas kernels for 17%

profile of v3, /device:TPU:0, one launch (start us, length us, event | category | flops | bytes accessed | tf_op | source)
XLA Modules:
  0.0 64.2 jit_solution(5395965417788585654)
XLA Ops:
  0.6 1.3 %shard_map.92 = (f32[4,128,128]{2,1,0:T(8,128)S(1)}, bf16[2,4,128,128]{3,2,1,0:T(8,128)(2,1)S(1)}) custom-call(bf16[2,64,512]{2,1,0:T(8,128)(2,1)} %k_ref.5, bf16[2,64,512]{2,1,0:T(8,128)(2,1)} %v_ref.5), custom_call_target="tpu_custom_call" | custom-call | tf_op jit(solution)/shard_map/pallas_call | solution.py:92
  1.9 3.0 %collective-permute-start.3 = (bf16[2,4,128,128]{3,2,1,0:T(8,128)(2,1)S(1)}, bf16[2,4,128,128]{3,2,1,0:T(8,128)(2,1)S(1)}, u32[]{:S(2)}, u32[]{:S(2)}) collective-permute-start(bf16[2,4,128,128]{3,2,1,0:T(8,128)(2,1)S(1)} %get-tuple-element.32.a_ref), channel_id=1, source_target_pairs={{0,4},{4,0},{8,12},{12,8},{16,20},{20,16},{24,28},{28,24},{1,5},{5... | collective-permute-start | bytes 786440 | tf_op jit(solution)/shard_map/ppermute | solution.py:39
  4.9 1.5 %collective-permute-start.1 = (bf16[128,1024]{1,0:T(8,128)(2,1)}, bf16[128,1024]{1,0:T(8,128)(2,1)S(1)}, u32[]{:S(2)}, u32[]{:S(2)}) collective-permute-start(bf16[128,1024]{1,0:T(8,128)(2,1)} %bitcast.73), channel_id=1, source_target_pairs={{0,2},{1,3},{2,0},{3,1},{4,6},{5,7},{6,4},{7,5},{8,10},{9,11},{10,... | collective-permute-start | bytes 786440 | tf_op jit(solution)/shard_map/ppermute | solution.py:39
  6.4 0.1 pad_add_fusion.spot_ref
  6.5 4.7 %collective-permute-done.3.b_ref = bf16[2,4,128,128]{3,2,1,0:T(8,128)(2,1)S(1)} collective-permute-done((bf16[2,4,128,128]{3,2,1,0:T(8,128)(2,1)S(1)}, bf16[2,4,128,128]{3,2,1,0:T(8,128)(2,1)S(1)}, u32[]{:S(2)}, u32[]{:S(2)}) %collective-permute-start.3) | collective-permute-done | bytes 262176 | tf_op jit(solution)/shard_map/ppermute | solution.py:39
  11.2 0.1 join_kv.2.a_ref
  11.3 1.9 %collective-permute-start.4 = (bf16[2,4,128,128]{3,2,1,0:T(8,128)(2,1)S(1)}, bf16[2,4,128,128]{3,2,1,0:T(8,128)(2,1)S(1)}, u32[]{:S(2)}, u32[]{:S(2)}) collective-permute-start(bf16[2,4,128,128]{3,2,1,0:T(8,128)(2,1)S(1)} %join_kv.2.a_ref), channel_id=1, source_target_pairs={{0,8},{4,12},{8,0},{12,4},{16,24},{20,28},{24,16},{28,20},{1,9},{5... | collective-permute-start | bytes 786440 | tf_op jit(solution)/shard_map/ppermute | solution.py:39
  13.2 2.9 %near.1 = (f32[128,512]{1,0:T(8,128)S(1)}, bf16[4,512,1024]{2,1,0:T(8,128)(2,1)S(1)}, bf16[128,1024]{1,0:T(8,128)(2,1)S(1)}) custom-call(s32[2]{0:T(128)S(1)} %pad_add_fusion.spot_ref, bf16[512,4096]{1,0:T(8,128)(2,1)} %w_hbm.1, bf16[128,1024]{1,0:T(8,128)(2,1)} %bitcast.75), custom_call_target="tpu_custom_call" | custom-call | flops 3300000000 | tf_op jit(solution)/shard_map/near/pallas_call | solution.py:187
  16.1 0.0 collective-permute-done.refs_0_.refs_1_
  16.1 0.6 quarter.1
  16.7 1.6 %collective-permute-start.14 = (bf16[4,32,512]{2,1,0:T(8,128)(2,1)S(1)}, bf16[4,32,512]{2,1,0:T(8,128)(2,1)S(1)}, u32[]{:S(2)}, u32[]{:S(2)}) collective-permute-start(bf16[4,32,512]{2,1,0:T(8,128)(2,1)S(1)} %get-tuple-element.38), channel_id=1, source_target_pairs={{0,4},{4,0},{8,12},{12,8},{16,20},{20,16},{24,28},{28,24},{1,5},{5... | collective-permute-start | bytes 393224 | tf_op jit(solution)/shard_map/ppermute | solution.py:39
  18.3 0.6 collective-permute-done.4.b_ref
  18.9 0.1 join_kv.3
  18.9 2.5 %collective-permute-start.5 = (bf16[4,128,128]{2,1,0:T(8,128)(2,1)S(1)}, bf16[4,128,128]{2,1,0:T(8,128)(2,1)S(1)}, u32[]{:S(2)}, u32[]{:S(2)}) collective-permute-start(bf16[4,128,128]{2,1,0:T(8,128)(2,1)S(1)} %fusion.11), channel_id=1, source_target_pairs={{0,16},{4,20},{8,24},{12,28},{16,0},{20,4},{24,8},{28,12},{1,17},{... | collective-permute-start | bytes 393224 | tf_op jit(solution)/shard_map/ppermute | solution.py:39
  21.5 1.2 %far.1.hg_ref = f32[128,512]{1,0:T(8,128)S(1)} custom-call(bf16[4,512,1024]{2,1,0:T(8,128)(2,1)S(1)} %get-tuple-element.34.w_ref, f32[128,512]{1,0:T(8,128)S(1)} %get-tuple-element.35.before_ref, bf16[128,1024]{1,0:T(8,128)(2,1)S(1)} %collective-permute-done.refs_0_.refs_1_, bf16[128,1024]{1,0:T(8,128)(2,1)S(1)} %collective-permute-done.1.refs_1_.refs_2_, ...), custom_call_target="tpu_custom_call" | custom-call | flops 2200000000 | tf_op jit(solution)/shard_map/far/pallas_call | solution.py:52
  22.8 1.6 %collective-permute-start.15 = (bf16[2,2,32,512]{3,2,1,0:T(8,128)(2,1)S(1)}, bf16[2,2,32,512]{3,2,1,0:T(8,128)(2,1)S(1)}, u32[]{:S(2)}, u32[]{:S(2)}) collective-permute-start(bf16[2,2,32,512]{3,2,1,0:T(8,128)(2,1)S(1)} %get-tuple-element.69), channel_id=1, source_target_pairs={{0,8},{4,12},{8,0},{12,4},{16,24},{20,28},{24,16},{28,20},{1,9},{5... | collective-permute-start | bytes 393224 | tf_op jit(solution)/shard_map/ppermute | solution.py:39
  24.4 3.4 %collective-permute-done.5 = bf16[4,128,128]{2,1,0:T(8,128)(2,1)S(1)} collective-permute-done((bf16[4,128,128]{2,1,0:T(8,128)(2,1)S(1)}, bf16[4,128,128]{2,1,0:T(8,128)(2,1)S(1)}, u32[]{:S(2)}, u32[]{:S(2)}) %collective-permute-start.5) | collective-permute-done | bytes 131104 | tf_op jit(solution)/shard_map/ppermute | solution.py:39
  27.8 0.1 add_select_fusion.4
  27.9 1.8 %forward.1 = (bf16[2,4,128,128]{3,2,1,0:T(8,128)(2,1)S(1)}, bf16[128,512]{1,0:T(8,128)(2,1)S(1)}, bf16[2,64,512]{2,1,0:T(8,128)(2,1)S(1)}, f32[4,128,128]{2,1,0:T(8,128)S(1)}, bf16[2,4,128,128]{3,2,1,0:T(8,128)(2,1)S(1)}) custom-call(bf16[2,64,512]{2,1,0:T(8,128)(2,1)S(1)} %copy-done.2, bf16[2,64,512]{2,1,0:T(8,128)(2,1)S(1)} %copy-done, ...), custom_call_target="tpu_custom_call" | custom-call | flops 220000000 | tf_op jit(solution)/shard_map/forward/pallas_call | solution.py:52
  29.7 0.7 %collective-permute-start.8 = (bf16[2,4,128,128]{3,2,1,0:T(8,128)(2,1)S(1)}, bf16[2,4,128,128]{3,2,1,0:T(8,128)(2,1)S(1)}, u32[]{:S(2)}, u32[]{:S(2)}) collective-permute-start(bf16[2,4,128,128]{3,2,1,0:T(8,128)(2,1)S(1)} %get-tuple-element.42.a_ref), channel_id=1, source_target_pairs={{0,4},{4,0},{8,12},{12,8},{16,20},{20,16},{24,28},{28,24},{1,5},{5... | collective-permute-start | bytes 786440 | tf_op jit(solution)/shard_map/ppermute | solution.py:39
  30.4 1.6 %collective-permute-start.16 = (bf16[2,128,512]{2,1,0:T(8,128)(2,1)S(1)}, bf16[2,128,512]{2,1,0:T(8,128)(2,1)S(1)}, u32[]{:S(2)}, u32[]{:S(2)}) collective-permute-start(bf16[2,128,512]{2,1,0:T(8,128)(2,1)S(1)} %pad_maximum_fusion.1), channel_id=1, source_target_pairs={{0,16},{4,20},{8,24},{12,28},{16,0},{20,4},{24,8},{28,12},{1,17},{... | collective-permute-start | bytes 786440 | tf_op jit(solution)/shard_map/ppermute | solution.py:39
  32.0 2.4 %collective-permute-start.10 = (bf16[128,512]{1,0:T(8,128)(2,1)S(1)}, bf16[128,512]{1,0:T(8,128)(2,1)S(1)}, u32[]{:S(2)}, u32[]{:S(2)}) collective-permute-start(bf16[128,512]{1,0:T(8,128)(2,1)S(1)} %get-tuple-element.40.hidden_ref.refs_0_), channel_id=1, source_target_pairs={{0,8},{4,12},{8,0},{12,4},{16,24},{20,28},{24,16},{28,20},{1,9},{5... | collective-permute-start | bytes 393224 | tf_op jit(solution)/shard_map/ppermute | solution.py:39
  34.4 0.4 project.3
  34.9 0.1 collective-permute-start.6
  34.9 0.4 project.2
  35.4 2.5 %collective-permute-done.8.b_ref = bf16[2,4,128,128]{3,2,1,0:T(8,128)(2,1)S(1)} collective-permute-done((bf16[2,4,128,128]{3,2,1,0:T(8,128)(2,1)S(1)}, bf16[2,4,128,128]{3,2,1,0:T(8,128)(2,1)S(1)}, u32[]{:S(2)}, u32[]{:S(2)}) %collective-permute-start.8) | collective-permute-done | bytes 262176 | tf_op jit(solution)/shard_map/ppermute | solution.py:39
  37.9 0.1 join_qg.2.a_ref
  38.0 0.1 collective-permute-start.9
  38.1 2.2 %inside.1 = (bf16[2,64,512]{2,1,0:T(8,128)(2,1)}, f32[2,64,512]{2,1,0:T(8,128)S(1)}, f32[2,64,512]{2,1,0:T(8,128)S(1)}) custom-call(bf16[2,64,512]{2,1,0:T(8,128)(2,1)S(1)} %copy-done.2, bf16[2,64,512]{2,1,0:T(8,128)(2,1)S(1)} %copy-done, bf16[2,64,512]{2,1,0:T(8,128)(2,1)S(1)} %copy-done.1, bf16[2,64,512]{2,1,0:T(8,128)(2,1)S(1)} %get-tuple-element.43.g_ref, ...), custom_call_target="tpu_custom_call" | custom-call | flops 1100000000 | tf_op jit(solution)/shard_map/inside/pallas_call | solution.py:52
  40.3 1.2 %collective-permute-done.10.refs_1_ = bf16[128,512]{1,0:T(8,128)(2,1)S(1)} collective-permute-done((bf16[128,512]{1,0:T(8,128)(2,1)S(1)}, bf16[128,512]{1,0:T(8,128)(2,1)S(1)}, u32[]{:S(2)}, u32[]{:S(2)}) %collective-permute-start.10) | collective-permute-done | bytes 131104 | tf_op jit(solution)/shard_map/ppermute | solution.py:39
  41.5 3.0 %collective-permute-start.12 = (bf16[128,512]{1,0:T(8,128)(2,1)S(1)}, bf16[128,512]{1,0:T(8,128)(2,1)S(1)}, u32[]{:S(2)}, u32[]{:S(2)}) collective-permute-start(bf16[128,512]{1,0:T(8,128)(2,1)S(1)} %collective-permute-done.10.refs_1_), channel_id=1, source_target_pairs={{0,16},{4,20},{8,24},{12,28},{16,0},{20,4},{24,8},{28,12},{1,17},{... | collective-permute-start | bytes 393224 | tf_op jit(solution)/shard_map/ppermute | solution.py:39
  44.5 0.8 %collective-permute-start.11 = (bf16[2,128,512]{2,1,0:T(8,128)(2,1)S(1)}, bf16[2,128,512]{2,1,0:T(8,128)(2,1)S(1)}, u32[]{:S(2)}, u32[]{:S(2)}) collective-permute-start(bf16[2,128,512]{2,1,0:T(8,128)(2,1)S(1)} %stack.54.refs_0_), channel_id=1, source_target_pairs={{0,4},{4,0},{8,12},{12,8},{16,20},{20,16},{24,28},{28,24},{1,5},{5... | collective-permute-start | bytes 786440 | tf_op jit(solution)/shard_map/ppermute | solution.py:39
  45.3 0.0 collective-permute-done.16
  45.3 1.6 %collective-permute-start.19 = (bf16[8,32,512]{2,1,0:T(8,128)(2,1)S(1)}, bf16[8,32,512]{2,1,0:T(8,128)(2,1)S(1)}, u32[]{:S(2)}, u32[]{:S(2)}) collective-permute-start(bf16[8,32,512]{2,1,0:T(8,128)(2,1)S(1)} %get-tuple-element.64), channel_id=1, source_target_pairs={{0,2},{1,3},{2,0},{3,1},{4,6},{5,7},{6,4},{7,5},{8,10},{9,11},{10,... | collective-permute-start | bytes 786440 | tf_op jit(solution)/shard_map/ppermute | solution.py:39
  46.9 0.2 add_bitcast_fusion
  47.1 5.2 %collective-permute-done.9.b_ref = bf16[2,4,128,128]{3,2,1,0:T(8,128)(2,1)S(1)} collective-permute-done((bf16[2,4,128,128]{3,2,1,0:T(8,128)(2,1)S(1)}, bf16[2,4,128,128]{3,2,1,0:T(8,128)(2,1)S(1)}, u32[]{:S(2)}, u32[]{:S(2)}) %collective-permute-start.9) | collective-permute-done | bytes 262176 | tf_op jit(solution)/shard_map/ppermute | solution.py:39
  52.3 0.1 join_qg.3
  52.4 0.0 collective-permute-done.11.refs_1_
  52.5 0.1 collective-permute-start.13
  52.6 1.6 %collective-permute-start.7 = (bf16[1,128,1024]{2,1,0:T(8,128)(2,1)S(1)}, bf16[1,128,1024]{2,1,0:T(8,128)(2,1)S(1)}, u32[]{:S(2)}, u32[]{:S(2)}) collective-permute-start(bf16[1,128,1024]{2,1,0:T(8,128)(2,1)S(1)} %fusion.2), channel_id=1, source_target_pairs={{0,2},{1,3},{2,0},{3,1},{4,6},{5,7},{6,4},{7,5},{8,10},{9,11},{10,... | collective-permute-start | bytes 786440 | tf_op jit(solution)/shard_map/ppermute | solution.py:39
  54.2 0.5 collective-permute-start.17
  54.7 0.1 collective-permute-start.20
  54.8 5.1 %collective-permute-done.13 = bf16[4,128,128]{2,1,0:T(8,128)(2,1)S(1)} collective-permute-done((bf16[4,128,128]{2,1,0:T(8,128)(2,1)S(1)}, bf16[4,128,128]{2,1,0:T(8,128)(2,1)S(1)}, u32[]{:S(2)}, u32[]{:S(2)}) %collective-permute-start.13) | collective-permute-done | bytes 131104 | tf_op jit(solution)/shard_map/ppermute | solution.py:39
  59.9 0.1 add_select_fusion
  60.0 1.1 %final.1 = (bf16[2,64,512]{2,1,0:T(8,128)(2,1)}, bf16[2,64,512]{2,1,0:T(8,128)(2,1)}) custom-call(bf16[2,64,512]{2,1,0:T(8,128)(2,1)S(1)} %copy-done, bf16[2,64,512]{2,1,0:T(8,128)(2,1)S(1)} %copy-done.1, f32[2,64,512]{2,1,0:T(8,128)S(1)} %get-tuple-element.46.dkp_ref, f32[2,64,512]{2,1,0:T(8,128)S(1)} %get-tuple-element.47.dvp_ref, ...), custom_call_target="tpu_custom_call" | custom-call | flops 1100000000 | tf_op jit(solution)/shard_map/final/pallas_call | solution.py:52
  61.1 0.8 %fusion.1 = bf16[1,128,1024]{2,1,0:T(8,128)(2,1)} fusion(f32[1,2,128,1024]{3,2,1,0:T(8,128)S(1)} %add_bitcast_fusion, bf16[1,128,1024]{2,1,0:T(8,128)(2,1)S(1)} %collective-permute-done.7), kind=kLoop, calls=%fused_computation.5 | loop fusion | flops 393216 | bytes 1048576 | tf_op jit(solution)/shard_map/convert_element_type | solution.py:402
  61.8 0.1 pad_maximum_fusion.refs_4_
  62.0 2.3 %wgb.1 = f32[512,512]{1,0:T(8,128)} custom-call(s32[2]{0:T(128)S(1)} %pad_add_fusion.spot_ref, bf16[2,128,512]{2,1,0:T(8,128)(2,1)S(1)} %stack.54.refs_0_, bf16[2,128,512]{2,1,0:T(8,128)(2,1)S(1)} %collective-permute-done.11.refs_1_, bf16[2,128,512]{2,1,0:T(8,128)(2,1)S(1)} %stack.55.refs_2_, bf16[2,128,512]{2,1,0:T(8,128)(2,1)S(1)} %collective-permute-done.17.refs_3_, ...), custom_call_target="tpu_custom_call" | custom-call | flops 550000000 | tf_op jit(solution)/shard_map/wgb/pallas_call | solution.py:336
  (34 shorter events, 0.4 us)
Async XLA Ops:
  1.9 9.3 %collective-permute-start.3 = (bf16[2,4,128,128]{3,2,1,0:T(8,128)(2,1)S(1)}, bf16[2,4,128,128]{3,2,1,0:T(8,128)(2,1)S(1)}, u32[]{:S(2)}, u32[]{:S(2)}) collective-permute-start(bf16[2,4,128,128]{3,2,1,0:T(8,128)(2,1)S(1)} %get-tuple-element.32.a_ref), channel_id=1, source_target_pairs={{0,4},{4,0},{8,12},{12,8},{16,20},{20,16},{24,28},{28,24},{1,5},{5... | collective-permute-start | bytes 786440 | tf_op jit(solution)/shard_map/ppermute | solution.py:39
  4.9 8.2 %collective-permute-start.1 = (bf16[128,1024]{1,0:T(8,128)(2,1)}, bf16[128,1024]{1,0:T(8,128)(2,1)S(1)}, u32[]{:S(2)}, u32[]{:S(2)}) collective-permute-start(bf16[128,1024]{1,0:T(8,128)(2,1)} %bitcast.73), channel_id=1, source_target_pairs={{0,2},{1,3},{2,0},{3,1},{4,6},{5,7},{6,4},{7,5},{8,10},{9,11},{10,... | collective-permute-start | bytes 786440 | tf_op jit(solution)/shard_map/ppermute | solution.py:39
  6.4 9.7 %collective-permute-start = (bf16[128,1024]{1,0:T(8,128)(2,1)}, bf16[128,1024]{1,0:T(8,128)(2,1)S(1)}, u32[]{:S(2)}, u32[]{:S(2)}) collective-permute-start(bf16[128,1024]{1,0:T(8,128)(2,1)} %bitcast.74), channel_id=1, source_target_pairs={{0,1},{1,0},{2,3},{3,2},{4,5},{5,4},{6,7},{7,6},{8,9},{9,8},{10,11... | collective-permute-start | bytes 786440 | tf_op jit(solution)/shard_map/ppermute | solution.py:39
  11.3 7.6 %collective-permute-start.4 = (bf16[2,4,128,128]{3,2,1,0:T(8,128)(2,1)S(1)}, bf16[2,4,128,128]{3,2,1,0:T(8,128)(2,1)S(1)}, u32[]{:S(2)}, u32[]{:S(2)}) collective-permute-start(bf16[2,4,128,128]{3,2,1,0:T(8,128)(2,1)S(1)} %join_kv.2.a_ref), channel_id=1, source_target_pairs={{0,8},{4,12},{8,0},{12,4},{16,24},{20,28},{24,16},{28,20},{1,9},{5... | collective-permute-start | bytes 786440 | tf_op jit(solution)/shard_map/ppermute | solution.py:39
  13.2 2.9 %collective-permute-start.2 = (bf16[128,1024]{1,0:T(8,128)(2,1)S(1)}, bf16[128,1024]{1,0:T(8,128)(2,1)S(1)}, u32[]{:S(2)}, u32[]{:S(2)}) collective-permute-start(bf16[128,1024]{1,0:T(8,128)(2,1)S(1)} %collective-permute-done.1.refs_1_.refs_2_), channel_id=1, source_target_pairs={{0,1},{1,0},{2,3},{3,2},{4,5},{5,4},{6,7},{7,6},{8,9},{9,8},{10,11... | collective-permute-start | bytes 786440 | tf_op jit(solution)/shard_map/ppermute | solution.py:39
  16.7 6.0 %collective-permute-start.14 = (bf16[4,32,512]{2,1,0:T(8,128)(2,1)S(1)}, bf16[4,32,512]{2,1,0:T(8,128)(2,1)S(1)}, u32[]{:S(2)}, u32[]{:S(2)}) collective-permute-start(bf16[4,32,512]{2,1,0:T(8,128)(2,1)S(1)} %get-tuple-element.38), channel_id=1, source_target_pairs={{0,4},{4,0},{8,12},{12,8},{16,20},{20,16},{24,28},{28,24},{1,5},{5... | collective-permute-start | bytes 393224 | tf_op jit(solution)/shard_map/ppermute | solution.py:39
  18.9 8.8 %collective-permute-start.5 = (bf16[4,128,128]{2,1,0:T(8,128)(2,1)S(1)}, bf16[4,128,128]{2,1,0:T(8,128)(2,1)S(1)}, u32[]{:S(2)}, u32[]{:S(2)}) collective-permute-start(bf16[4,128,128]{2,1,0:T(8,128)(2,1)S(1)} %fusion.11), channel_id=1, source_target_pairs={{0,16},{4,20},{8,24},{12,28},{16,0},{20,4},{24,8},{28,12},{1,17},{... | collective-permute-start | bytes 393224 | tf_op jit(solution)/shard_map/ppermute | solution.py:39
  21.5 6.4 %copy-start = (bf16[2,64,512]{2,1,0:T(8,128)(2,1)S(1)}, bf16[2,64,512]{2,1,0:T(8,128)(2,1)}, u32[]{:S(2)}) copy-start(bf16[2,64,512]{2,1,0:T(8,128)(2,1)} %k_ref.5) | copy-start | bytes 393220
  21.5 6.4 %copy-start.1 = (bf16[2,64,512]{2,1,0:T(8,128)(2,1)S(1)}, bf16[2,64,512]{2,1,0:T(8,128)(2,1)}, u32[]{:S(2)}) copy-start(bf16[2,64,512]{2,1,0:T(8,128)(2,1)} %v_ref.5) | copy-start | bytes 393220
  21.5 6.4 %copy-start.2 = (bf16[2,64,512]{2,1,0:T(8,128)(2,1)S(1)}, bf16[2,64,512]{2,1,0:T(8,128)(2,1)}, u32[]{:S(2)}) copy-start(bf16[2,64,512]{2,1,0:T(8,128)(2,1)} %q_ref.3) | copy-start | bytes 393220
  22.8 7.6 %collective-permute-start.15 = (bf16[2,2,32,512]{3,2,1,0:T(8,128)(2,1)S(1)}, bf16[2,2,32,512]{3,2,1,0:T(8,128)(2,1)S(1)}, u32[]{:S(2)}, u32[]{:S(2)}) collective-permute-start(bf16[2,2,32,512]{3,2,1,0:T(8,128)(2,1)S(1)} %get-tuple-element.69), channel_id=1, source_target_pairs={{0,8},{4,12},{8,0},{12,4},{16,24},{20,28},{24,16},{28,20},{1,9},{5... | collective-permute-start | bytes 393224 | tf_op jit(solution)/shard_map/ppermute | solution.py:39
  29.7 8.2 %collective-permute-start.8 = (bf16[2,4,128,128]{3,2,1,0:T(8,128)(2,1)S(1)}, bf16[2,4,128,128]{3,2,1,0:T(8,128)(2,1)S(1)}, u32[]{:S(2)}, u32[]{:S(2)}) collective-permute-start(bf16[2,4,128,128]{3,2,1,0:T(8,128)(2,1)S(1)} %get-tuple-element.42.a_ref), channel_id=1, source_target_pairs={{0,4},{4,0},{8,12},{12,8},{16,20},{20,16},{24,28},{28,24},{1,5},{5... | collective-permute-start | bytes 786440 | tf_op jit(solution)/shard_map/ppermute | solution.py:39
  30.4 14.8 %collective-permute-start.16 = (bf16[2,128,512]{2,1,0:T(8,128)(2,1)S(1)}, bf16[2,128,512]{2,1,0:T(8,128)(2,1)S(1)}, u32[]{:S(2)}, u32[]{:S(2)}) collective-permute-start(bf16[2,128,512]{2,1,0:T(8,128)(2,1)S(1)} %pad_maximum_fusion.1), channel_id=1, source_target_pairs={{0,16},{4,20},{8,24},{12,28},{16,0},{20,4},{24,8},{28,12},{1,17},{... | collective-permute-start | bytes 786440 | tf_op jit(solution)/shard_map/ppermute | solution.py:39
  32.0 9.5 %collective-permute-start.10 = (bf16[128,512]{1,0:T(8,128)(2,1)S(1)}, bf16[128,512]{1,0:T(8,128)(2,1)S(1)}, u32[]{:S(2)}, u32[]{:S(2)}) collective-permute-start(bf16[128,512]{1,0:T(8,128)(2,1)S(1)} %get-tuple-element.40.hidden_ref.refs_0_), channel_id=1, source_target_pairs={{0,8},{4,12},{8,0},{12,4},{16,24},{20,28},{24,16},{28,20},{1,9},{5... | collective-permute-start | bytes 393224 | tf_op jit(solution)/shard_map/ppermute | solution.py:39
  34.9 12.0 %collective-permute-start.6 = (bf16[2,128,1024]{2,1,0:T(8,128)(2,1)S(1)}, bf16[2,128,1024]{2,1,0:T(8,128)(2,1)S(1)}, u32[]{:S(2)}, u32[]{:S(2)}) collective-permute-start(bf16[2,128,1024]{2,1,0:T(8,128)(2,1)S(1)} %project.3), channel_id=1, source_target_pairs={{0,1},{1,0},{2,3},{3,2},{4,5},{5,4},{6,7},{7,6},{8,9},{9,8},{10,11... | collective-permute-start | bytes 1572872 | tf_op jit(solution)/shard_map/ppermute | solution.py:39
  38.0 14.4 %collective-permute-start.9 = (bf16[2,4,128,128]{3,2,1,0:T(8,128)(2,1)S(1)}, bf16[2,4,128,128]{3,2,1,0:T(8,128)(2,1)S(1)}, u32[]{:S(2)}, u32[]{:S(2)}) collective-permute-start(bf16[2,4,128,128]{3,2,1,0:T(8,128)(2,1)S(1)} %join_qg.2.a_ref), channel_id=1, source_target_pairs={{0,8},{4,12},{8,0},{12,4},{16,24},{20,28},{24,16},{28,20},{1,9},{5... | collective-permute-start | bytes 786440 | tf_op jit(solution)/shard_map/ppermute | solution.py:39
  41.5 11.0 %collective-permute-start.12 = (bf16[128,512]{1,0:T(8,128)(2,1)S(1)}, bf16[128,512]{1,0:T(8,128)(2,1)S(1)}, u32[]{:S(2)}, u32[]{:S(2)}) collective-permute-start(bf16[128,512]{1,0:T(8,128)(2,1)S(1)} %collective-permute-done.10.refs_1_), channel_id=1, source_target_pairs={{0,16},{4,20},{8,24},{12,28},{16,0},{20,4},{24,8},{28,12},{1,17},{... | collective-permute-start | bytes 393224 | tf_op jit(solution)/shard_map/ppermute | solution.py:39
  44.5 8.0 %collective-permute-start.11 = (bf16[2,128,512]{2,1,0:T(8,128)(2,1)S(1)}, bf16[2,128,512]{2,1,0:T(8,128)(2,1)S(1)}, u32[]{:S(2)}, u32[]{:S(2)}) collective-permute-start(bf16[2,128,512]{2,1,0:T(8,128)(2,1)S(1)} %stack.54.refs_0_), channel_id=1, source_target_pairs={{0,4},{4,0},{8,12},{12,8},{16,20},{20,16},{24,28},{28,24},{1,5},{5... | collective-permute-start | bytes 786440 | tf_op jit(solution)/shard_map/ppermute | solution.py:39
  45.3 9.4 %collective-permute-start.19 = (bf16[8,32,512]{2,1,0:T(8,128)(2,1)S(1)}, bf16[8,32,512]{2,1,0:T(8,128)(2,1)S(1)}, u32[]{:S(2)}, u32[]{:S(2)}) collective-permute-start(bf16[8,32,512]{2,1,0:T(8,128)(2,1)S(1)} %get-tuple-element.64), channel_id=1, source_target_pairs={{0,2},{1,3},{2,0},{3,1},{4,6},{5,7},{6,4},{7,5},{8,10},{9,11},{10,... | collective-permute-start | bytes 786440 | tf_op jit(solution)/shard_map/ppermute | solution.py:39
  46.9 14.9 %collective-permute-start.18 = (bf16[8,32,512]{2,1,0:T(8,128)(2,1)S(1)}, bf16[8,32,512]{2,1,0:T(8,128)(2,1)S(1)}, u32[]{:S(2)}, u32[]{:S(2)}) collective-permute-start(bf16[8,32,512]{2,1,0:T(8,128)(2,1)S(1)} %get-tuple-element.64), channel_id=1, source_target_pairs={{0,1},{1,0},{2,3},{3,2},{4,5},{5,4},{6,7},{7,6},{8,9},{9,8},{10,11... | collective-permute-start | bytes 786440 | tf_op jit(solution)/shard_map/ppermute | solution.py:39
  52.5 7.4 %collective-permute-start.13 = (bf16[4,128,128]{2,1,0:T(8,128)(2,1)S(1)}, bf16[4,128,128]{2,1,0:T(8,128)(2,1)S(1)}, u32[]{:S(2)}, u32[]{:S(2)}) collective-permute-start(bf16[4,128,128]{2,1,0:T(8,128)(2,1)S(1)} %fusion.10), channel_id=1, source_target_pairs={{0,16},{4,20},{8,24},{12,28},{16,0},{20,4},{24,8},{28,12},{1,17},{... | collective-permute-start | bytes 393224 | tf_op jit(solution)/shard_map/ppermute | solution.py:39
  52.6 8.5 %collective-permute-start.7 = (bf16[1,128,1024]{2,1,0:T(8,128)(2,1)S(1)}, bf16[1,128,1024]{2,1,0:T(8,128)(2,1)S(1)}, u32[]{:S(2)}, u32[]{:S(2)}) collective-permute-start(bf16[1,128,1024]{2,1,0:T(8,128)(2,1)S(1)} %fusion.2), channel_id=1, source_target_pairs={{0,2},{1,3},{2,0},{3,1},{4,6},{5,7},{6,4},{7,5},{8,10},{9,11},{10,... | collective-permute-start | bytes 786440 | tf_op jit(solution)/shard_map/ppermute | solution.py:39
  54.2 7.7 %collective-permute-start.17 = (bf16[2,128,512]{2,1,0:T(8,128)(2,1)S(1)}, bf16[2,128,512]{2,1,0:T(8,128)(2,1)S(1)}, u32[]{:S(2)}, u32[]{:S(2)}) collective-permute-start(bf16[2,128,512]{2,1,0:T(8,128)(2,1)S(1)} %stack.55.refs_2_), channel_id=1, source_target_pairs={{0,4},{4,0},{8,12},{12,8},{16,20},{20,16},{24,28},{28,24},{1,5},{5... | collective-permute-start | bytes 786440 | tf_op jit(solution)/shard_map/ppermute | solution.py:39
  54.7 7.1 %collective-permute-start.20 = (bf16[8,32,512]{2,1,0:T(8,128)(2,1)S(1)}, bf16[8,32,512]{2,1,0:T(8,128)(2,1)S(1)}, u32[]{:S(2)}, u32[]{:S(2)}) collective-permute-start(bf16[8,32,512]{2,1,0:T(8,128)(2,1)S(1)} %collective-permute-done.19), channel_id=1, source_target_pairs={{0,1},{1,0},{2,3},{3,2},{4,5},{5,4},{6,7},{7,6},{8,9},{9,8},{10,11... | collective-permute-start | bytes 786440 | tf_op jit(solution)/shard_map/ppermute | solution.py:39

commit v4 on v0

--- a/solution.py
+++ b/solution.py
@@ -1,12 +1,506 @@
+import functools
+
 import jax
 import jax.numpy as jnp
 from jax import lax
+from jax.experimental import pallas as pl
+from jax.experimental.pallas import tpu as pltpu
 from jax.sharding import PartitionSpec as P
 
 HEAD_DIM = 128
-
-
-eps = 1e-06
+EPS = 1e-06
+LASTING = {
+    "kv": 3,
+    "near": 3,
+    "quarter": 0.2,
+    "far": 0.01,
+    "forward": 0.01,
+    "join_kv": 0.01,
+    "join_qg": 0.1,
+    "project": 0.2,
+    "inside": 5,
+    "stack": 0.1,
+    "last": 1,
+}
+WAITS = {
+    "kv4.s": ["quarter", "a1.s", "near"],
+    "h2.s": ["far", "a1.g"],
+    "rs2.s": ["a2.s"],
+    "a4.g": ["qg2.s", "qg1.g"],
+    "g1.g": ["hy.g"],
+    "qg4.g": ["h2.g", "rs2.g"],
+    "h6.g": ["qg2.s"],
+    "qg1.s": ["a2.g", "kv2.s"],
+    "away": ["c2.g"],
+    "qg4.s": ["rs2.s", "a4.s", "g1.s"],
+    "hy.s": ["c3.g"],
+    "forward": ["a1.g"],
+    "qg2.s": ["a2.g"],
+    "a2.s": ["c1.s"],
+    "quarter": ["kv1.s"],
+    "kv1.g": ["c1.s"],
+    "g3.g": ["qg4.g"],
+    "hz.g": ["qg4.g"],
+    "c1.s": ["c2.s"],
+    "c2.s": ["kv1.s"],
+    "hz.s": ["rs2.s", "h4.g"],
+    "qg2.g": ["g1.s"],
+    "g1.s": ["h6.g"],
+}
+
+NN = (((1,), (0,)), ((), ()))
+NT = (((1,), (1,)), ((), ()))
+TN = (((0,), (0,)), ((), ()))
+
+
+def mm(a, b, dims):
+    return lax.dot_general(a, b, dims, preferred_element_type=jnp.float32)
+
+
+def head_cols(i):
+    return slice(i * HEAD_DIM, (i + 1) * HEAD_DIM)
+
+
+def lower(length):
+    rows = lax.broadcasted_iota(jnp.int32, (length, length), 0)
+    cols = lax.broadcasted_iota(jnp.int32, (length, length), 1)
+    return rows >= cols
+
+
+def xor_permute(x, axis, bit):
+    count = lax.axis_size(axis)
+    return lax.ppermute(x, axis, [(i, i ^ bit) for i in range(count)])
+
+
+def whole(n):
+    return [pl.BlockSpec(memory_space=pltpu.VMEM)] * n
+
+
+def lasting(name):
+    return pl.CostEstimate(flops=int(LASTING[name] * 1.1e9), bytes_accessed=0, transcendentals=0)
+
+
+def kernel_call(name, body, outs, args, vmem=16 * 2**20):
+    return pl.pallas_call(
+        body,
+        out_shape=outs,
+        in_specs=whole(len(args)),
+        out_specs=whole(len(outs)),
+        compiler_params=pltpu.CompilerParams(vmem_limit_bytes=vmem),
+        cost_estimate=lasting(name),
+        name=name,
+    )(*args)
+
+
+def shaped(shape, dtype):
+    return jax.ShapeDtypeStruct(shape, dtype)
+
+
+def kv_body(k_hbm, v_hbm, own_ref, send_ref, k_ref, v_ref, sems):
+    loads = [
+        pltpu.make_async_copy(k_hbm, k_ref, sems.at[0]),
+        pltpu.make_async_copy(v_hbm, v_ref, sems.at[1]),
+    ]
+    for load in loads:
+        load.start()
+    for load in loads:
+        load.wait()
+    for i in range(k_ref.shape[2] // HEAD_DIM):
+        c = head_cols(i)
+        first = mm(k_ref[0, :, c], v_ref[0, :, c], TN)
+        second = mm(k_ref[1, :, c], v_ref[1, :, c], TN)
+        own_ref[i] = first
+        send_ref[0, i] = first.astype(jnp.bfloat16)
+        send_ref[1, i] = (first + second).astype(jnp.bfloat16)
+
+
+def in_hbm(x):
+    return pltpu.with_memory_space_constraint(x, pltpu.HBM)
+
+
+def kv_products(keys, values):
+    heads = keys.shape[2] // HEAD_DIM
+    square = (heads, HEAD_DIM, HEAD_DIM)
+    return pl.pallas_call(
+        kv_body,
+        out_shape=(shaped(square, jnp.float32), shaped((2,) + square, jnp.bfloat16)),
+        in_specs=[pl.BlockSpec(memory_space=pltpu.HBM)] * 2,
+        out_specs=whole(2),
+        scratch_shapes=[
+            pltpu.VMEM(keys.shape, keys.dtype),
+            pltpu.VMEM(values.shape, values.dtype),
+            pltpu.SemaphoreType.DMA((2,)),
+        ],
+        compiler_params=pltpu.CompilerParams(vmem_limit_bytes=16 * 2**20),
+    )(keys, values)
+
+
+def join_body(a_ref, b_ref, out_ref):
+    out_ref[...] = (a_ref[...].astype(jnp.float32) + b_ref[...].astype(jnp.float32)).astype(out_ref.dtype)
+
+
+def column_loads(spot_ref, w_hbm, w_ref, sems):
+    n, _, cols = w_ref.shape
+    loads = []
+    for slot in range(n):
+        at = pl.multiple_of((spot_ref[1] ^ slot) * cols, cols)
+        loads.append(pltpu.make_async_copy(w_hbm.at[:, pl.ds(at, cols)], w_ref.at[slot], sems.at[slot]))
+    return loads
+
+
+def near_body(spot_ref, w_hbm, up_hbm, out_ref, up_ref, w_ref, sems):
+    loads = [pltpu.make_async_copy(up_hbm, up_ref, sems.at[1])] + column_loads(spot_ref, w_hbm, w_ref, sems)
+    for load in loads:
+        load.start()
+    for load in loads:
+        load.wait()
+    out_ref[...] = mm(up_ref[...], w_ref[0], NT)
+
+
+def near_grad_of(up, weight, spot):
+    rows, cols = up.shape
+    features = weight.shape[0]
+    return pl.pallas_call(
+        near_body,
+        out_shape=(shaped((rows, features), jnp.float32), shaped(up.shape, up.dtype)),
+        in_specs=[pl.BlockSpec(memory_space=pltpu.SMEM)] + [pl.BlockSpec(memory_space=pltpu.HBM)] * 2,
+        out_specs=whole(2),
+        scratch_shapes=[pltpu.VMEM((1, features, cols), weight.dtype), pltpu.SemaphoreType.DMA((2,))],
+        compiler_params=pltpu.CompilerParams(vmem_limit_bytes=16 * 2**20),
+        cost_estimate=lasting("near"),
+        name="near",
+    )(spot, weight, up)
+
+
+def far_body(n, spot_ref, w_hbm, before_ref, *refs):
+    chunks, (out_ref, w_ref, sems) = refs[: n - 1], refs[n - 1 :]
+    loads = column_loads(spot_ref, w_hbm, w_ref, sems)
+    for load in loads[1:] + loads[:1]:
+        load.start()
+    total = before_ref[...]
+    for slot in range(1, n):
+        loads[slot].wait()
+        total += mm(chunks[slot - 1][...], w_ref[slot], NT)
+    out_ref[...] = total
+    loads[0].wait()
+
+
+def hidden_grad_of(before, chunks, weight, spot):
+    rows, cols = chunks[0].shape
+    features = weight.shape[0]
+    n = len(chunks) + 1
+    return pl.pallas_call(
+        functools.partial(far_body, n),
+        out_shape=(shaped((rows, features), jnp.float32), shaped((n, features, cols), weight.dtype)),
+        in_specs=[pl.BlockSpec(memory_space=pltpu.SMEM), pl.BlockSpec(memory_space=pltpu.HBM)] + whole(n),
+        out_specs=whole(2),
+        scratch_shapes=[pltpu.SemaphoreType.DMA((n,))],
+        compiler_params=pltpu.CompilerParams(vmem_limit_bytes=16 * 2**20),
+        cost_estimate=lasting("far"),
+        name="far",
+    )(spot, weight, before, *chunks)
+
+
+def forward_body(q_ref, k_ref, v_ref, hg_ref, own_ref, below_ref, above_ref,
+                 state_ref, hidden_ref, g_ref, qown_ref, qsend_ref):
+    length = q_ref.shape[1]
+    mask = lower(length)
+    for i in range(q_ref.shape[2] // HEAD_DIM):
+        c = head_cols(i)
+        below = below_ref[i]
+        states = (below, below + own_ref[i] + above_ref[i])
+        terms = []
+        for p in range(2):
+            r = slice(p * length, (p + 1) * length)
+            q, k, v = q_ref[p, :, c], k_ref[p, :, c], v_ref[p, :, c]
+            state = states[p].astype(jnp.bfloat16)
+            state_ref[p, i] = state
+            weights = jnp.where(mask, mm(q, k, NT), 0.0).astype(jnp.bfloat16)
+            attended = mm(weights, v, NN) + mm(q, state, NN)
+            scale = jnp.sqrt(jnp.mean(attended * attended, axis=-1, keepdims=True) + EPS)
+            normed = attended / scale
+            hidden_ref[r, c] = normed.astype(jnp.bfloat16)
+            hg = hg_ref[r, c]
+            inner = jnp.mean(hg * normed, axis=-1, keepdims=True)
+            g = ((hg - normed * inner) / scale).astype(jnp.bfloat16)
+            g_ref[p, :, c] = g
+            terms.append(mm(q, g, TN))
+        qown_ref[i] = terms[1]
+        qsend_ref[0, i] = terms[1].astype(jnp.bfloat16)
+        qsend_ref[1, i] = (terms[0] + terms[1]).astype(jnp.bfloat16)
+
+
+def inside_body(q_ref, k_ref, v_ref, g_ref, state_ref, dq_ref, dk_ref, dv_ref):
+    length = q_ref.shape[1]
+    mask = lower(length)
+    for i in range(q_ref.shape[2] // HEAD_DIM):
+        c = head_cols(i)
+        for p in range(2):
+            q, k, v, g = q_ref[p, :, c], k_ref[p, :, c], v_ref[p, :, c], g_ref[p, :, c]
+            weights = jnp.where(mask, mm(q, k, NT), 0.0).astype(jnp.bfloat16)
+            diffs = jnp.where(mask, mm(g, v, NT), 0.0).astype(jnp.bfloat16)
+            dq_ref[p, :, c] = (mm(diffs, k, NN) + mm(g, state_ref[p, i], NT)).astype(jnp.bfloat16)
+            dk_ref[p, :, c] = mm(diffs, q, TN)
+            dv_ref[p, :, c] = mm(weights, g, TN)
+
+
+def last_body(slots, spot_ref, k_ref, v_ref, dkp_ref, dvp_ref, own_ref, below_ref, above_ref, sum_ref, got_ref, *refs):
+    hiddens, ups = refs[: len(slots)], refs[len(slots)]
+    outs, sems = refs[len(slots) + 1 : len(slots) + 5], refs[-1]
+    dk_ref, dv_ref, out_ref, weight_ref = refs[len(slots) + 5 : -1]
+    features = weight_ref.shape[0]
+    tile = features // 2
+    copies = [pltpu.make_async_copy(x, y, sems.at[i]) for i, (x, y) in enumerate(zip((dk_ref, dv_ref, out_ref), outs))]
+    copies += [
+        pltpu.make_async_copy(weight_ref.at[pl.ds(t * tile, tile)], outs[3].at[pl.ds(t * tile, tile)], sems.at[3 + t])
+        for t in range(2)
+    ]
+    out_ref[...] = (sum_ref[...] + got_ref[...].astype(jnp.float32)).astype(out_ref.dtype)
+    copies[2].start()
+    for i in range(k_ref.shape[2] // HEAD_DIM):
+        c = head_cols(i)
+        below = below_ref[i]
+        laters = (below + own_ref[i] + above_ref[i], below)
+        for p in range(2):
+            later = laters[p].astype(jnp.bfloat16)
+            k, v = k_ref[p, :, c], v_ref[p, :, c]
+            dk_ref[p, :, c] = (dkp_ref[p, :, c] + mm(v, later, NT)).astype(jnp.bfloat16)
+            dv_ref[p, :, c] = (dvp_ref[p, :, c] + mm(k, later, NN)).astype(jnp.bfloat16)
+    copies[0].start()
+    copies[1].start()
+    head = spot_ref[1]
+    n, _, share, _ = ups.shape
+    rights = jnp.concatenate([ups[m, slot] for group in slots for slot in group for m in range(n)])
+    for t in range(2):
+        lefts = [
+            ref[i, pl.ds(pl.multiple_of((head ^ m) * share, share), share), t * tile : (t + 1) * tile]
+            for ref, group in zip(hiddens, slots)
+            for i in range(len(group))
+            for m in range(n)
+        ]
+        weight_ref[t * tile : (t + 1) * tile, :] = mm(jnp.concatenate(lefts), rights, TN)
+        copies[3 + t].start()
+    for copy in copies:
+        copy.wait()
+
+
+def last_call(slots, shapes, spot, args):
+    n = len(args)
+    return pl.pallas_call(
+        functools.partial(last_body, slots),
+        out_shape=shapes,
+        in_specs=[pl.BlockSpec(memory_space=pltpu.SMEM)] + whole(n),
+        out_specs=[pl.BlockSpec(memory_space=pl.ANY)] * len(shapes),
+        scratch_shapes=[pltpu.VMEM(x.shape, x.dtype) for x in shapes] + [pltpu.SemaphoreType.DMA((5,))],
+        compiler_params=pltpu.CompilerParams(vmem_limit_bytes=24 * 2**20),
+        cost_estimate=lasting("last"),
+        name="last",
+    )(spot, *args)
+
+
+def project_body(slots, w_ref, hidden_ref, out_ref):
+    for i, slot in enumerate(slots):
+        out_ref[i] = mm(hidden_ref[...], w_ref[slot], NN).astype(out_ref.dtype)
+
+
+def project(hidden, by_columns, slots, dtype):
+    shape = (len(slots), hidden.shape[0], by_columns.shape[2])
+    return kernel_call("project", functools.partial(project_body, slots), (shaped(shape, dtype),), (by_columns, hidden))[0]
+
+
+def quarter_body(n, spot_ref, *refs):
+    chunks, keep_ref, send_ref = refs[:n], refs[-2], refs[-1]
+    seq, head = spot_ref[0], spot_ref[1]
+    share, cols = keep_ref.shape[1:]
+    rows = pl.ds(pl.multiple_of(head * share, share), share)
+    odd = seq & 1
+    for m in range(n):
+        t = (seq // 2) ^ head ^ m
+        entry = (t & 1) * (n // 2) + t // 2
+        keep_ref[entry] = chunks[m][rows, pl.ds(pl.multiple_of(odd * cols, cols), cols)]
+        send_ref[entry] = chunks[m][rows, pl.ds(pl.multiple_of((1 - odd) * cols, cols), cols)]
+
+
+def share_out(chunks, spot):
+    n = len(chunks)
+    rows, cols = chunks[0].shape
+    part = shaped((n, rows // n, cols // 2), chunks[0].dtype)
+    return pl.pallas_call(
+        functools.partial(quarter_body, n),
+        out_shape=(part, part),
+        in_specs=[pl.BlockSpec(memory_space=pltpu.SMEM)] + whole(n),
+        out_specs=whole(2),
+        compiler_params=pltpu.CompilerParams(vmem_limit_bytes=16 * 2**20),
+        cost_estimate=lasting("quarter"),
+        name="quarter",
+    )(spot, *chunks)
+
+
+def stack_body(*refs):
+    for i, ref in enumerate(refs[:-1]):
+        refs[-1][i] = ref[...]
+
+
+def stacked(blocks):
+    shape = (len(blocks),) + blocks[0].shape
+    return kernel_call("stack", stack_body, (shaped(shape, blocks[0].dtype),), blocks)[0]
+
+
+def after(x, *others):
+    if not others:
+        return x
+    return lax.optimization_barrier((x,) + others)[0]
+
+
+def on_eight_by_four(queries, keys, values, out_weight, upstream):
+    pair, length, width = queries.shape
+    heads = width // HEAD_DIM
+    n_seq, n_head = lax.axis_size("seq"), lax.axis_size("head")
+    seq, head = lax.axis_index("seq"), lax.axis_index("head")
+    rows, own_cols = pair * length, upstream.shape[2]
+    f32, bf16 = jnp.float32, jnp.bfloat16
+    square = (heads, HEAD_DIM, HEAD_DIM)
+    flat_up = upstream.reshape(rows, own_cols)
+    spot = jnp.stack([seq, head]).astype(jnp.int32)
+    seen = {}
+
+    def node(name, x):
+        early = [seen[other] for other in WAITS.get(name, ()) if other in seen]
+        if early:
+            x = after(x, *early)
+        seen[name] = x
+        return x
+
+    class Scan:
+        def __init__(self, tag, near, send):
+            self.tag, self.send = tag, send
+            self.below = jnp.zeros_like(near)
+            self.above = jnp.zeros_like(near)
+
+        def put(self, bit):
+            self.upper = (seq & bit) != 0
+            if 2 * bit == n_seq:
+                self.send = jnp.where(self.upper, self.send[1], self.send[0])
+            self.name = self.tag + str(bit)
+            self.send = node(self.name + ".s", self.send)
+            self.raw = xor_permute(self.send, "seq", bit)
+
+        def take(self):
+            got = node(self.name + ".g", self.raw)
+            if got.ndim == 4:
+                self.send = kernel_call("join_" + self.tag, join_body, (shaped(got.shape, got.dtype),), (self.send, got))[0]
+            self.add(got.astype(jnp.float32))
+
+        def add(self, got):
+            near, both = (got[0], got[1]) if got.ndim == 4 else (got, got)
+            self.below = jnp.where(self.upper, self.below + near, self.below)
+            self.above = jnp.where(self.upper, self.above, self.above + both)
+
+    kv_own, kv_send = kv_products(in_hbm(keys), in_hbm(values))
+    kv = Scan("kv", kv_own, kv_send)
+    kv.put(1)
+    seen["kv"] = kv_send
+    flat_up = after(flat_up, kv_send)
+    c2_raw = xor_permute(node("c2.s", flat_up), "head", 2)
+    c1_raw = xor_permute(node("c1.s", flat_up), "head", 1)
+    weight_hbm = in_hbm(out_weight)
+    near_grad, c0 = near_grad_of(in_hbm(node("near", flat_up)), weight_hbm, spot)
+    near_grad = node("near_out", near_grad)
+    kv.take()
+    kv.put(2)
+    c2 = node("c2.g", c2_raw)
+    c3_raw = xor_permute(node("c3.s", c2), "head", 1)
+    c1 = node("c1.g", c1_raw)
+    c3 = node("c3.g", c3_raw)
+    chunks = [c0, c1, c2, c3]
+    keep, a1_send = share_out([node("quarter", c0)] + chunks[1:], spot)
+    a1_raw = xor_permute(node("a1.s", a1_send), "seq", 1)
+    kv.take()
+    kv.put(4)
+    a1 = node("a1.g", a1_raw)
+    held = jnp.stack([keep, a1], axis=1)
+    a2_raw = xor_permute(node("a2.s", held[2:]), "seq", 2)
+    hidden_grad, by_columns = hidden_grad_of(node("far", near_grad), chunks[1:], weight_hbm, spot)
+    a2 = node("a2.g", a2_raw)
+    held = jnp.concatenate([held[:2], a2], axis=1)
+    a4_raw = xor_permute(node("a4.s", held[1]), "seq", 4)
+    kv.take()
+    states, hidden, attn_grad, qg_own, qg_send = kernel_call(
+        "forward",
+        forward_body,
+        (
+            shaped((2,) + square, bf16),
+            shaped((rows, width), bf16),
+            shaped((pair, length, width), bf16),
+            shaped(square, f32),
+            shaped((2,) + square, bf16),
+        ),
+        (queries, keys, values, node("forward", hidden_grad), kv_own, kv.below, kv.above),
+    )
+    qg = Scan("qg", qg_own, qg_send)
+    qg.put(1)
+    h2_raw = xor_permute(node("h2.s", hidden), "seq", 2)
+    h4_raw = xor_permute(node("h4.s", hidden), "seq", 4)
+    away = project(node("away", hidden), by_columns, range(1, n_head, 2), bf16)
+    rs1_raw = xor_permute(node("rs1.s", away), "head", 1)
+    home = project(node("home", hidden), by_columns, range(0, n_head, 2), f32)
+    qg.take()
+    qg.put(2)
+    h2 = node("h2.g", h2_raw)
+    first_rows = stacked([hidden, h2])
+    hy_raw = xor_permute(node("hy.s", first_rows), "seq", 1)
+    rs1 = node("rs1.g", rs1_raw)
+    total = (home + rs1.astype(f32)).reshape(2, rows, own_cols)
+    rs2_raw = xor_permute(node("rs2.s", total[1].astype(bf16)), "head", 2)
+
+    query_grad, key_part, value_part = kernel_call(
+        "inside",
+        inside_body,
+        (
+            shaped((pair, length, width), bf16),
+            shaped((pair, length, width), f32),
+            shaped((pair, length, width), f32),
+        ),
+        (queries, keys, values, node("inside", attn_grad), states),
+    )
+    ups = jnp.concatenate([held[0], node("a4.g", a4_raw)])
+    h4 = node("h4.g", h4_raw)
+    g2_raw = xor_permute(node("g2.s", ups), "head", 2)
+    h6_raw = xor_permute(node("h6.s", h4), "seq", 2)
+    h6 = node("h6.g", h6_raw)
+    second_rows = stacked([h4, h6])
+    hz_raw = xor_permute(node("hz.s", second_rows), "seq", 1)
+    g1_raw = xor_permute(node("g1.s", ups), "head", 1)
+    qg.take()
+    qg.put(4)
+    g2 = node("g2.g", g2_raw)
+    g3_raw = xor_permute(node("g3.s", g2), "head", 1)
+    hy = node("hy.g", hy_raw)
+    g1 = node("g1.g", g1_raw)
+    rs2 = node("rs2.g", rs2_raw)
+    qg.take()
+    hz = node("hz.g", hz_raw)
+    g3 = node("g3.g", g3_raw)
+    ups = jnp.stack([ups, g1, g2, g3])
+    key_grad, value_grad, output, weight_grad = last_call(
+        [[0, 2], [1, 3], [4, 6], [5, 7]],
+        (
+            shaped((pair, length, width), bf16),
+            shaped((pair, length, width), bf16),
+            shaped((rows, own_cols), bf16),
+            shaped((width, own_cols // 2), f32),
+        ),
+        spot,
+        [keys, values, node("final", key_part), value_part, qg_own, qg.below, qg.above, total[0], rs2]
+        + [first_rows, hy, second_rows, hz, ups],
+    )
+    return (
+        output.reshape(pair, length, -1),
+        query_grad,
+        key_grad,
+        value_grad,
+        weight_grad,
+    )
 
 
 def carried_in(shard, axis, join, neutral, backward):
@@ -27,13 +521,7 @@
     return jax.tree.map(lambda left, right: left + right, earlier, later)
 
 
-def lower_mask(length):
-    rows = lax.broadcasted_iota(jnp.int32, (length, length), 0)
-    cols = lax.broadcasted_iota(jnp.int32, (length, length), 1)
-    return rows >= cols
-
-
-def on_device(queries, keys, values, out_weight, upstream):
+def on_any_mesh(queries, keys, values, out_weight, upstream):
     pair, length, width = queries.shape
     heads_here = width // HEAD_DIM
     shape_four = (pair, length, heads_here, HEAD_DIM)
@@ -49,14 +537,14 @@
     total_first = lax.psum(first_kv, "seq")
     state_second = total_first + after
     states = jnp.stack([before, state_second]).astype(jnp.bfloat16)
-    mask = lower_mask(length)
+    mask = lower(length)
     scores = jnp.einsum("pthd,pshd->phts", query4, key4, preferred_element_type=jnp.float32)
     weights = jnp.where(mask, scores, 0.0).astype(jnp.bfloat16)
     attended = jnp.einsum("phts,pshe->pthe", weights, value4, preferred_element_type=jnp.float32)
     attended = attended + jnp.einsum(
         "pthd,phde->pthe", query4, states, preferred_element_type=jnp.float32
     )
-    scale = jnp.sqrt(jnp.mean(attended * attended, axis=-1, keepdims=True) + eps)
+    scale = jnp.sqrt(jnp.mean(attended * attended, axis=-1, keepdims=True) + EPS)
     normed = attended / scale
     hidden = normed.astype(jnp.bfloat16).reshape(pair * length, width)
     partial_out = jnp.dot(hidden, out_weight, preferred_element_type=jnp.float32)
@@ -115,23 +603,17 @@
     )
 
 
+def on_device(*args):
+    plan = on_eight_by_four if (lax.axis_size("seq"), lax.axis_size("head")) == (8, 4) else on_any_mesh
+    return plan(*args)
+
+
 def solution(mesh):
+    rows = P(None, "seq", "head")
     return jax.shard_map(
         on_device,
         mesh=mesh,
-        in_specs=(
-            P(None, "seq", "head"),
-            P(None, "seq", "head"),
-            P(None, "seq", "head"),
-            P("head", None),
-            P(None, "seq", "head"),
-        ),
-        out_specs=(
-            P(None, "seq", "head"),
-            P(None, "seq", "head"),
-            P(None, "seq", "head"),
-            P(None, "seq", "head"),
-            P("head", "seq"),
-        ),
+        in_specs=(rows, rows, rows, P("head", None), rows),
+        out_specs=(rows, rows, rows, rows, P("head", "seq")),
         check_vma=False,
     )

time: 533 us -> 61.4 us (0.12)
  waiting for transfers between devices: 476 us -> 22.8 us
  starting transfers between devices: 0.37 us -> 21.5 us
  matrix products: 18.1 us -> 0 us
  other arithmetic: 16 us -> 0.84 us
  Pallas kernels: 0 us -> 15 us
  between operations: 14.1 us -> 0.97 us
  local copies, waits for them, and re-layouts: 6.57 us -> 0.11 us
    reduce_scatter x2 -> x0, waiting for transfers between devices: 179 us -> none  [the longest x1 154 us: on_device(): lax.psum_scatter(lax.dot_general(full_up, hidden, (((0,), (0,)), ((), ())...]
    all_gather x5 -> x0, waiting for transfers between devices: 150 us -> none  [the longest x4 135 us: carried_in(): gathered = lax.all_gather(shard.astype(jnp.bfloat16), axis)]
    psum x2 -> x0, waiting for transfers between devices: 146 us -> none  [the longest x1 73 us: on_device(): total_first = lax.psum(first_kv, 'seq')]
    ppermute x0 -> x22, waiting for transfers between devices: none -> 22.8 us  [xor_permute(): return lax.ppermute(x, axis, [(i, i ^ bit) for i in range(count)])]
    ppermute x0 -> x22, starting transfers between devices: none -> 21.5 us  [xor_permute(): return lax.ppermute(x, axis, [(i, i ^ bit) for i in range(count)])]
    dot_general x15 -> x0, matrix products: 18.1 us -> none  [the longest x1 4.53 us: on_device(): lax.dot_general(full_up, hidden, (((0,), (0,)), ((), ())), preferred_elem...]
    pallas_call x0 -> x15, Pallas kernels: none -> 15 us  [the longest x10 5.18 us: kernel_call(): pl.pallas_call(body, out_shape=outs, in_specs=whole(len(args)), out_specs...]
    add x14 -> x1, other arithmetic: 13.5 us -> 0.16 us  [on_eight_by_four(): total = (home + rs1.astype(f32)).reshape(2, rows, own_cols)]
  transfers between devices with their start and end apart: 9 -> 22, of which waited for: 9 -> 10; matrix products, arithmetic and copies ran while one was open for 7% -> 1% of each run, Pallas kernels for 0% -> 18%
where the time goes in v4:
time: 61.4 us; the launch traced here: 61.2 us
  waiting for transfers between devices  22.8 us (37%)
  starting transfers between devices  21.5 us (35%)
  Pallas kernels  15 us (24%)
  between operations  0.97 us (2%)
  other arithmetic  0.84 us (1%)
    ppermute x22, waiting for transfers between devices, xor_permute(): return lax.ppermute(x, axis, [(i, i ^ bit) for i in range(count)])  22.8 us
    ppermute x22, starting transfers between devices, xor_permute(): return lax.ppermute(x, axis, [(i, i ^ bit) for i in range(count)])  21.5 us
    pallas_call x10, Pallas kernels, kernel_call(): pl.pallas_call(body, out_shape=outs, in_specs=whole(len(args)), out_specs...  5.18 us
    pallas_call x1, Pallas kernels, hidden_grad_of(): pl.pallas_call(functools.partial(far_body, n), out_shape=(shaped((rows, f...  3.03 us
    pallas_call x1, Pallas kernels, last_call(): pl.pallas_call(functools.partial(last_body, slots), out_shape=shapes, in_...  2.59 us
    pallas_call x1, Pallas kernels, near_grad_of(): pl.pallas_call(near_body, out_shape=(shaped((rows, features), jnp.float32...  2.35 us
    pallas_call x1, Pallas kernels, kv_products(): pl.pallas_call(kv_body, out_shape=(shaped(square, jnp.float32), shaped((2...  1.25 us
  transfers between devices with their start and end apart: 22, of which 10 were waited for; matrix products, arithmetic and copies ran while one was open for 1% of the time, Pallas kernels for 18%

profile of v4, /device:TPU:0, one launch (start us, length us, event | category | flops | bytes accessed | tf_op | source)
XLA Modules:
  0.0 61.2 jit_solution(7929832381579329327)
XLA Ops:
  0.6 1.3 %shard_map.92 = (f32[4,128,128]{2,1,0:T(8,128)S(1)}, bf16[2,4,128,128]{3,2,1,0:T(8,128)(2,1)S(1)}) custom-call(bf16[2,64,512]{2,1,0:T(8,128)(2,1)} %k_ref.5, bf16[2,64,512]{2,1,0:T(8,128)(2,1)} %v_ref.5), custom_call_target="tpu_custom_call" | custom-call | tf_op jit(solution)/shard_map/pallas_call | solution.py:124
  1.9 3.0 %collective-permute-start.4 = (bf16[2,4,128,128]{3,2,1,0:T(8,128)(2,1)S(1)}, bf16[2,4,128,128]{3,2,1,0:T(8,128)(2,1)S(1)}, u32[]{:S(2)}, u32[]{:S(2)}) collective-permute-start(bf16[2,4,128,128]{3,2,1,0:T(8,128)(2,1)S(1)} %get-tuple-element.49.a_ref), channel_id=1, source_target_pairs={{0,4},{4,0},{8,12},{12,8},{16,20},{20,16},{24,28},{28,24},{1,5},{5... | collective-permute-start | bytes 786440 | tf_op jit(solution)/shard_map/ppermute | solution.py:72
  4.9 1.5 %collective-permute-start.1 = (bf16[128,1024]{1,0:T(8,128)(2,1)}, bf16[128,1024]{1,0:T(8,128)(2,1)S(1)}, u32[]{:S(2)}, u32[]{:S(2)}) collective-permute-start(bf16[128,1024]{1,0:T(8,128)(2,1)} %bitcast.62), channel_id=1, source_target_pairs={{0,2},{1,3},{2,0},{3,1},{4,6},{5,7},{6,4},{7,5},{8,10},{9,11},{10,... | collective-permute-start | bytes 786440 | tf_op jit(solution)/shard_map/ppermute | solution.py:72
  6.4 0.1 pad_add_fusion.spot_ref
  6.5 4.7 %collective-permute-done.4.b_ref = bf16[2,4,128,128]{3,2,1,0:T(8,128)(2,1)S(1)} collective-permute-done((bf16[2,4,128,128]{3,2,1,0:T(8,128)(2,1)S(1)}, bf16[2,4,128,128]{3,2,1,0:T(8,128)(2,1)S(1)}, u32[]{:S(2)}, u32[]{:S(2)}) %collective-permute-start.4) | collective-permute-done | bytes 262176 | tf_op jit(solution)/shard_map/ppermute | solution.py:72
  11.2 0.1 join_kv.2.a_ref
  11.3 1.9 %collective-permute-start.5 = (bf16[2,4,128,128]{3,2,1,0:T(8,128)(2,1)S(1)}, bf16[2,4,128,128]{3,2,1,0:T(8,128)(2,1)S(1)}, u32[]{:S(2)}, u32[]{:S(2)}) collective-permute-start(bf16[2,4,128,128]{3,2,1,0:T(8,128)(2,1)S(1)} %join_kv.2.a_ref), channel_id=1, source_target_pairs={{0,8},{4,12},{8,0},{12,4},{16,24},{20,28},{24,16},{28,20},{1,9},{5... | collective-permute-start | bytes 786440 | tf_op jit(solution)/shard_map/ppermute | solution.py:72
  13.2 2.4 %near.1 = (f32[128,512]{1,0:T(8,128)S(1)}, bf16[128,1024]{1,0:T(8,128)(2,1)S(1)}) custom-call(s32[2]{0:T(128)S(1)} %pad_add_fusion.spot_ref, bf16[512,4096]{1,0:T(8,128)(2,1)} %w_hbm.3, bf16[128,1024]{1,0:T(8,128)(2,1)} %bitcast.64), custom_call_target="tpu_custom_call" | custom-call | flops 3300000000 | tf_op jit(solution)/shard_map/near/pallas_call | solution.py:163
  15.5 0.6 quarter.1
  16.2 1.6 %collective-permute-start.3 = (bf16[4,32,512]{2,1,0:T(8,128)(2,1)S(1)}, bf16[4,32,512]{2,1,0:T(8,128)(2,1)S(1)}, u32[]{:S(2)}, u32[]{:S(2)}) collective-permute-start(bf16[4,32,512]{2,1,0:T(8,128)(2,1)S(1)} %get-tuple-element.57), channel_id=1, source_target_pairs={{0,4},{4,0},{8,12},{12,8},{16,20},{20,16},{24,28},{28,24},{1,5},{5... | collective-permute-start | bytes 393224 | tf_op jit(solution)/shard_map/ppermute | solution.py:72
  17.7 1.1 %collective-permute-done.5.b_ref = bf16[2,4,128,128]{3,2,1,0:T(8,128)(2,1)S(1)} collective-permute-done((bf16[2,4,128,128]{3,2,1,0:T(8,128)(2,1)S(1)}, bf16[2,4,128,128]{3,2,1,0:T(8,128)(2,1)S(1)}, u32[]{:S(2)}, u32[]{:S(2)}) %collective-permute-start.5) | collective-permute-done | bytes 262176 | tf_op jit(solution)/shard_map/ppermute | solution.py:72
  18.9 0.1 join_kv.3
  18.9 2.5 %collective-permute-start.6 = (bf16[4,128,128]{2,1,0:T(8,128)(2,1)S(1)}, bf16[4,128,128]{2,1,0:T(8,128)(2,1)S(1)}, u32[]{:S(2)}, u32[]{:S(2)}) collective-permute-start(bf16[4,128,128]{2,1,0:T(8,128)(2,1)S(1)} %fusion.8), channel_id=1, source_target_pairs={{0,16},{4,20},{8,24},{12,28},{16,0},{20,4},{24,8},{28,12},{1,17},{... | collective-permute-start | bytes 393224 | tf_op jit(solution)/shard_map/ppermute | solution.py:72
  21.5 0.0 copy-start
  21.5 0.0 copy-start.1
  21.6 0.0 copy-start.2
  21.6 3.0 %far.1 = (f32[128,512]{1,0:T(8,128)S(1)}, bf16[4,512,1024]{2,1,0:T(8,128)(2,1)S(1)}) custom-call(s32[2]{0:T(128)S(1)} %pad_add_fusion.spot_ref, bf16[512,4096]{1,0:T(8,128)(2,1)} %w_hbm.3, f32[128,512]{1,0:T(8,128)S(1)} %get-tuple-element.51.before_ref, bf16[128,1024]{1,0:T(8,128)(2,1)S(1)} %collective-permute-done.refs_0_.refs_1_, ...), custom_call_target="tpu_custom_call" | custom-call | flops 11000000 | tf_op jit(solution)/shard_map/far/pallas_call | solution.py:192
  24.7 1.7 %collective-permute-start.7 = (bf16[2,2,32,512]{3,2,1,0:T(8,128)(2,1)S(1)}, bf16[2,2,32,512]{3,2,1,0:T(8,128)(2,1)S(1)}, u32[]{:S(2)}, u32[]{:S(2)}) collective-permute-start(bf16[2,2,32,512]{3,2,1,0:T(8,128)(2,1)S(1)} %fusion.6), channel_id=1, source_target_pairs={{0,8},{4,12},{8,0},{12,4},{16,24},{20,28},{24,16},{28,20},{1,9},{5... | collective-permute-start | bytes 393224 | tf_op jit(solution)/shard_map/ppermute | solution.py:72
  26.3 0.9 %collective-permute-done.6 = bf16[4,128,128]{2,1,0:T(8,128)(2,1)S(1)} collective-permute-done((bf16[4,128,128]{2,1,0:T(8,128)(2,1)S(1)}, bf16[4,128,128]{2,1,0:T(8,128)(2,1)S(1)}, u32[]{:S(2)}, u32[]{:S(2)}) %collective-permute-start.6) | collective-permute-done | bytes 131104 | tf_op jit(solution)/shard_map/ppermute | solution.py:72
  27.2 0.1 add_select_fusion.4
  27.3 1.8 %forward.1 = (bf16[2,4,128,128]{3,2,1,0:T(8,128)(2,1)S(1)}, bf16[128,512]{1,0:T(8,128)(2,1)S(1)}, bf16[2,64,512]{2,1,0:T(8,128)(2,1)S(1)}, f32[4,128,128]{2,1,0:T(8,128)S(1)}, bf16[2,4,128,128]{3,2,1,0:T(8,128)(2,1)S(1)}) custom-call(bf16[2,64,512]{2,1,0:T(8,128)(2,1)S(1)} %copy-done.2, bf16[2,64,512]{2,1,0:T(8,128)(2,1)S(1)} %copy-done, ...), custom_call_target="tpu_custom_call" | custom-call | flops 11000000 | tf_op jit(solution)/shard_map/forward/pallas_call | solution.py:84
  29.1 0.2 collective-permute-start.11
  29.3 3.0 %collective-permute-start.15 = (bf16[128,512]{1,0:T(8,128)(2,1)S(1)}, bf16[128,512]{1,0:T(8,128)(2,1)S(1)}, u32[]{:S(2)}, u32[]{:S(2)}) collective-permute-start(bf16[128,512]{1,0:T(8,128)(2,1)S(1)} %get-tuple-element.81.hidden_ref.refs_0_), channel_id=1, source_target_pairs={{0,8},{4,12},{8,0},{12,4},{16,24},{20,28},{24,16},{28,20},{1,9},{5... | collective-permute-start | bytes 393224 | tf_op jit(solution)/shard_map/ppermute | solution.py:72
  32.4 0.4 project.3
  32.8 0.1 collective-permute-start.13
  32.9 1.5 %collective-permute-start.8 = (bf16[2,4,128,128]{3,2,1,0:T(8,128)(2,1)S(1)}, bf16[2,4,128,128]{3,2,1,0:T(8,128)(2,1)S(1)}, u32[]{:S(2)}, u32[]{:S(2)}) collective-permute-start(bf16[2,4,128,128]{3,2,1,0:T(8,128)(2,1)S(1)} %get-tuple-element.70.a_ref), channel_id=1, source_target_pairs={{0,4},{4,0},{8,12},{12,8},{16,20},{20,16},{24,28},{28,24},{1,5},{5... | collective-permute-start | bytes 786440 | tf_op jit(solution)/shard_map/ppermute | solution.py:72
  34.5 0.1 collective-permute-start.10
  34.6 2.1 %collective-permute-done.11.refs_0_ = bf16[128,512]{1,0:T(8,128)(2,1)S(1)} collective-permute-done((bf16[128,512]{1,0:T(8,128)(2,1)S(1)}, bf16[128,512]{1,0:T(8,128)(2,1)S(1)}, u32[]{:S(2)}, u32[]{:S(2)}) %collective-permute-start.11) | collective-permute-done | bytes 131104 | tf_op jit(solution)/shard_map/ppermute | solution.py:72
  36.7 2.2 %inside.1 = (bf16[2,64,512]{2,1,0:T(8,128)(2,1)}, f32[2,64,512]{2,1,0:T(8,128)S(1)}, f32[2,64,512]{2,1,0:T(8,128)S(1)}) custom-call(bf16[2,64,512]{2,1,0:T(8,128)(2,1)S(1)} %copy-done.2, bf16[2,64,512]{2,1,0:T(8,128)(2,1)S(1)} %copy-done, bf16[2,64,512]{2,1,0:T(8,128)(2,1)S(1)} %copy-done.1, bf16[2,64,512]{2,1,0:T(8,128)(2,1)S(1)} %get-tuple-element.62.g_ref, ...), custom_call_target="tpu_custom_call" | custom-call | flops 5500000256 | tf_op jit(solution)/shard_map/inside/pallas_call | solution.py:84
  39.0 0.4 project.2
  39.4 0.5 collective-permute-start.17
  40.0 2.1 %collective-permute-done.8.b_ref = bf16[2,4,128,128]{3,2,1,0:T(8,128)(2,1)S(1)} collective-permute-done((bf16[2,4,128,128]{3,2,1,0:T(8,128)(2,1)S(1)}, bf16[2,4,128,128]{3,2,1,0:T(8,128)(2,1)S(1)}, u32[]{:S(2)}, u32[]{:S(2)}) %collective-permute-start.8) | collective-permute-done | bytes 262176 | tf_op jit(solution)/shard_map/ppermute | solution.py:72
  42.1 0.1 join_qg.2.a_ref
  42.1 0.1 collective-permute-start.9
  42.2 2.1 %collective-permute-done.12.refs_1_ = bf16[128,512]{1,0:T(8,128)(2,1)S(1)} collective-permute-done((bf16[128,512]{1,0:T(8,128)(2,1)S(1)}, bf16[128,512]{1,0:T(8,128)(2,1)S(1)}, u32[]{:S(2)}, u32[]{:S(2)}) %collective-permute-start.12) | collective-permute-done | bytes 131104 | tf_op jit(solution)/shard_map/ppermute | solution.py:72
  44.4 1.6 %collective-permute-start.20 = (bf16[8,32,512]{2,1,0:T(8,128)(2,1)S(1)}, bf16[8,32,512]{2,1,0:T(8,128)(2,1)S(1)}, u32[]{:S(2)}, u32[]{:S(2)}) collective-permute-start(bf16[8,32,512]{2,1,0:T(8,128)(2,1)S(1)} %get-tuple-element.75), channel_id=1, source_target_pairs={{0,2},{1,3},{2,0},{3,1},{4,6},{5,7},{6,4},{7,5},{8,10},{9,11},{10,... | collective-permute-start | bytes 786440 | tf_op jit(solution)/shard_map/ppermute | solution.py:72
  46.0 0.2 convert_add_fusion
  46.2 0.6 collective-permute-start.16
  46.8 3.0 %collective-permute-done.9.b_ref = bf16[2,4,128,128]{3,2,1,0:T(8,128)(2,1)S(1)} collective-permute-done((bf16[2,4,128,128]{3,2,1,0:T(8,128)(2,1)S(1)}, bf16[2,4,128,128]{3,2,1,0:T(8,128)(2,1)S(1)}, u32[]{:S(2)}, u32[]{:S(2)}) %collective-permute-start.9) | collective-permute-done | bytes 262176 | tf_op jit(solution)/shard_map/ppermute | solution.py:72
  49.8 1.3 %collective-permute-start.18 = (bf16[2,128,512]{2,1,0:T(8,128)(2,1)S(1)}, bf16[2,128,512]{2,1,0:T(8,128)(2,1)S(1)}, u32[]{:S(2)}, u32[]{:S(2)}) collective-permute-start(bf16[2,128,512]{2,1,0:T(8,128)(2,1)S(1)} %stack.47.refs_2_), channel_id=1, source_target_pairs={{0,4},{4,0},{8,12},{12,8},{16,20},{20,16},{24,28},{28,24},{1,5},{5... | collective-permute-start | bytes 786440 | tf_op jit(solution)/shard_map/ppermute | solution.py:72
  51.1 0.1 join_qg.3
  51.2 0.3 collective-permute-start.14
  51.5 2.2 %collective-permute-done.20 = bf16[8,32,512]{2,1,0:T(8,128)(2,1)S(1)} collective-permute-done((bf16[8,32,512]{2,1,0:T(8,128)(2,1)S(1)}, bf16[8,32,512]{2,1,0:T(8,128)(2,1)S(1)}, u32[]{:S(2)}, u32[]{:S(2)}) %collective-permute-start.20) | collective-permute-done | bytes 262176 | tf_op jit(solution)/shard_map/ppermute | solution.py:72
  53.8 3.5 %collective-permute-done.16.got_ref = bf16[128,1024]{1,0:T(8,128)(2,1)S(1)} collective-permute-done((bf16[128,1024]{1,0:T(8,128)(2,1)S(1)}, bf16[128,1024]{1,0:T(8,128)(2,1)S(1)}, u32[]{:S(2)}, u32[]{:S(2)}) %collective-permute-start.16) | collective-permute-done | bytes 262176 | tf_op jit(solution)/shard_map/ppermute | solution.py:72
  57.3 1.1 %collective-permute-done.14 = bf16[4,128,128]{2,1,0:T(8,128)(2,1)S(1)} collective-permute-done((bf16[4,128,128]{2,1,0:T(8,128)(2,1)S(1)}, bf16[4,128,128]{2,1,0:T(8,128)(2,1)S(1)}, u32[]{:S(2)}, u32[]{:S(2)}) %collective-permute-start.14) | collective-permute-done | bytes 131104 | tf_op jit(solution)/shard_map/ppermute | solution.py:72
  58.3 0.1 add_select_fusion
  58.5 0.1 pad_maximum_fusion.refs_4_
  58.6 2.6 %last.1 = (bf16[2,64,512]{2,1,0:T(8,128)(2,1)}, bf16[2,64,512]{2,1,0:T(8,128)(2,1)}, bf16[128,1024]{1,0:T(8,128)(2,1)}, f32[512,512]{1,0:T(8,128)}) custom-call(s32[2]{0:T(128)S(1)} %pad_add_fusion.spot_ref, bf16[2,64,512]{2,1,0:T(8,128)(2,1)S(1)} %copy-done, bf16[2,64,512]{2,1,0:T(8,128)(2,1)S(1)} %copy-done.1, ...), custom_call_target="tpu_custom_call" | custom-call | flops 1100000000 | tf_op jit(solution)/shard_map/last/pallas_call | solution.py:289
  (34 shorter events, 0.4 us)
Async XLA Ops:
  1.9 9.3 %collective-permute-start.4 = (bf16[2,4,128,128]{3,2,1,0:T(8,128)(2,1)S(1)}, bf16[2,4,128,128]{3,2,1,0:T(8,128)(2,1)S(1)}, u32[]{:S(2)}, u32[]{:S(2)}) collective-permute-start(bf16[2,4,128,128]{3,2,1,0:T(8,128)(2,1)S(1)} %get-tuple-element.49.a_ref), channel_id=1, source_target_pairs={{0,4},{4,0},{8,12},{12,8},{16,20},{20,16},{24,28},{28,24},{1,5},{5... | collective-permute-start | bytes 786440 | tf_op jit(solution)/shard_map/ppermute | solution.py:72
  4.9 8.2 %collective-permute-start.1 = (bf16[128,1024]{1,0:T(8,128)(2,1)}, bf16[128,1024]{1,0:T(8,128)(2,1)S(1)}, u32[]{:S(2)}, u32[]{:S(2)}) collective-permute-start(bf16[128,1024]{1,0:T(8,128)(2,1)} %bitcast.62), channel_id=1, source_target_pairs={{0,2},{1,3},{2,0},{3,1},{4,6},{5,7},{6,4},{7,5},{8,10},{9,11},{10,... | collective-permute-start | bytes 786440 | tf_op jit(solution)/shard_map/ppermute | solution.py:72
  6.4 9.1 %collective-permute-start = (bf16[128,1024]{1,0:T(8,128)(2,1)}, bf16[128,1024]{1,0:T(8,128)(2,1)S(1)}, u32[]{:S(2)}, u32[]{:S(2)}) collective-permute-start(bf16[128,1024]{1,0:T(8,128)(2,1)} %bitcast.63), channel_id=1, source_target_pairs={{0,1},{1,0},{2,3},{3,2},{4,5},{5,4},{6,7},{7,6},{8,9},{9,8},{10,11... | collective-permute-start | bytes 786440 | tf_op jit(solution)/shard_map/ppermute | solution.py:72
  11.3 7.6 %collective-permute-start.5 = (bf16[2,4,128,128]{3,2,1,0:T(8,128)(2,1)S(1)}, bf16[2,4,128,128]{3,2,1,0:T(8,128)(2,1)S(1)}, u32[]{:S(2)}, u32[]{:S(2)}) collective-permute-start(bf16[2,4,128,128]{3,2,1,0:T(8,128)(2,1)S(1)} %join_kv.2.a_ref), channel_id=1, source_target_pairs={{0,8},{4,12},{8,0},{12,4},{16,24},{20,28},{24,16},{28,20},{1,9},{5... | collective-permute-start | bytes 786440 | tf_op jit(solution)/shard_map/ppermute | solution.py:72
  13.2 2.4 %collective-permute-start.2 = (bf16[128,1024]{1,0:T(8,128)(2,1)S(1)}, bf16[128,1024]{1,0:T(8,128)(2,1)S(1)}, u32[]{:S(2)}, u32[]{:S(2)}) collective-permute-start(bf16[128,1024]{1,0:T(8,128)(2,1)S(1)} %collective-permute-done.1.refs_1_.refs_2_), channel_id=1, source_target_pairs={{0,1},{1,0},{2,3},{3,2},{4,5},{5,4},{6,7},{7,6},{8,9},{9,8},{10,11... | collective-permute-start | bytes 786440 | tf_op jit(solution)/shard_map/ppermute | solution.py:72
  16.2 8.5 %collective-permute-start.3 = (bf16[4,32,512]{2,1,0:T(8,128)(2,1)S(1)}, bf16[4,32,512]{2,1,0:T(8,128)(2,1)S(1)}, u32[]{:S(2)}, u32[]{:S(2)}) collective-permute-start(bf16[4,32,512]{2,1,0:T(8,128)(2,1)S(1)} %get-tuple-element.57), channel_id=1, source_target_pairs={{0,4},{4,0},{8,12},{12,8},{16,20},{20,16},{24,28},{28,24},{1,5},{5... | collective-permute-start | bytes 393224 | tf_op jit(solution)/shard_map/ppermute | solution.py:72
  18.9 8.3 %collective-permute-start.6 = (bf16[4,128,128]{2,1,0:T(8,128)(2,1)S(1)}, bf16[4,128,128]{2,1,0:T(8,128)(2,1)S(1)}, u32[]{:S(2)}, u32[]{:S(2)}) collective-permute-start(bf16[4,128,128]{2,1,0:T(8,128)(2,1)S(1)} %fusion.8), channel_id=1, source_target_pairs={{0,16},{4,20},{8,24},{12,28},{16,0},{20,4},{24,8},{28,12},{1,17},{... | collective-permute-start | bytes 393224 | tf_op jit(solution)/shard_map/ppermute | solution.py:72
  21.5 5.8 %copy-start = (bf16[2,64,512]{2,1,0:T(8,128)(2,1)S(1)}, bf16[2,64,512]{2,1,0:T(8,128)(2,1)}, u32[]{:S(2)}) copy-start(bf16[2,64,512]{2,1,0:T(8,128)(2,1)} %k_ref.5) | copy-start | bytes 393220
  21.5 5.8 %copy-start.1 = (bf16[2,64,512]{2,1,0:T(8,128)(2,1)S(1)}, bf16[2,64,512]{2,1,0:T(8,128)(2,1)}, u32[]{:S(2)}) copy-start(bf16[2,64,512]{2,1,0:T(8,128)(2,1)} %v_ref.5) | copy-start | bytes 393220
  21.6 5.8 %copy-start.2 = (bf16[2,64,512]{2,1,0:T(8,128)(2,1)S(1)}, bf16[2,64,512]{2,1,0:T(8,128)(2,1)}, u32[]{:S(2)}) copy-start(bf16[2,64,512]{2,1,0:T(8,128)(2,1)} %q_ref.3) | copy-start | bytes 393220
  24.7 8.2 %collective-permute-start.7 = (bf16[2,2,32,512]{3,2,1,0:T(8,128)(2,1)S(1)}, bf16[2,2,32,512]{3,2,1,0:T(8,128)(2,1)S(1)}, u32[]{:S(2)}, u32[]{:S(2)}) collective-permute-start(bf16[2,2,32,512]{3,2,1,0:T(8,128)(2,1)S(1)} %fusion.6), channel_id=1, source_target_pairs={{0,8},{4,12},{8,0},{12,4},{16,24},{20,28},{24,16},{28,20},{1,9},{5... | collective-permute-start | bytes 393224 | tf_op jit(solution)/shard_map/ppermute | solution.py:72
  29.1 7.6 %collective-permute-start.11 = (bf16[128,512]{1,0:T(8,128)(2,1)S(1)}, bf16[128,512]{1,0:T(8,128)(2,1)S(1)}, u32[]{:S(2)}, u32[]{:S(2)}) collective-permute-start(bf16[128,512]{1,0:T(8,128)(2,1)S(1)} %get-tuple-element.81.hidden_ref.refs_0_), channel_id=1, source_target_pairs={{0,16},{4,20},{8,24},{12,28},{16,0},{20,4},{24,8},{28,12},{1,17},{... | collective-permute-start | bytes 393224 | tf_op jit(solution)/shard_map/ppermute | solution.py:72
  29.3 10.1 %collective-permute-start.15 = (bf16[128,512]{1,0:T(8,128)(2,1)S(1)}, bf16[128,512]{1,0:T(8,128)(2,1)S(1)}, u32[]{:S(2)}, u32[]{:S(2)}) collective-permute-start(bf16[128,512]{1,0:T(8,128)(2,1)S(1)} %get-tuple-element.81.hidden_ref.refs_0_), channel_id=1, source_target_pairs={{0,8},{4,12},{8,0},{12,4},{16,24},{20,28},{24,16},{28,20},{1,9},{5... | collective-permute-start | bytes 393224 | tf_op jit(solution)/shard_map/ppermute | solution.py:72
  32.8 13.2 %collective-permute-start.13 = (bf16[2,128,1024]{2,1,0:T(8,128)(2,1)S(1)}, bf16[2,128,1024]{2,1,0:T(8,128)(2,1)S(1)}, u32[]{:S(2)}, u32[]{:S(2)}) collective-permute-start(bf16[2,128,1024]{2,1,0:T(8,128)(2,1)S(1)} %project.3), channel_id=1, source_target_pairs={{0,1},{1,0},{2,3},{3,2},{4,5},{5,4},{6,7},{7,6},{8,9},{9,8},{10,11... | collective-permute-start | bytes 1572872 | tf_op jit(solution)/shard_map/ppermute | solution.py:72
  32.9 9.2 %collective-permute-start.8 = (bf16[2,4,128,128]{3,2,1,0:T(8,128)(2,1)S(1)}, bf16[2,4,128,128]{3,2,1,0:T(8,128)(2,1)S(1)}, u32[]{:S(2)}, u32[]{:S(2)}) collective-permute-start(bf16[2,4,128,128]{3,2,1,0:T(8,128)(2,1)S(1)} %get-tuple-element.70.a_ref), channel_id=1, source_target_pairs={{0,4},{4,0},{8,12},{12,8},{16,20},{20,16},{24,28},{28,24},{1,5},{5... | collective-permute-start | bytes 786440 | tf_op jit(solution)/shard_map/ppermute | solution.py:72
  34.5 9.8 %collective-permute-start.10 = (bf16[4,32,512]{2,1,0:T(8,128)(2,1)S(1)}, bf16[4,32,512]{2,1,0:T(8,128)(2,1)S(1)}, u32[]{:S(2)}, u32[]{:S(2)}) collective-permute-start(bf16[4,32,512]{2,1,0:T(8,128)(2,1)S(1)} %get-tuple-element.100), channel_id=1, source_target_pairs={{0,16},{4,20},{8,24},{12,28},{16,0},{20,4},{24,8},{28,12},{1,17},{... | collective-permute-start | bytes 393224 | tf_op jit(solution)/shard_map/ppermute | solution.py:72
  36.7 7.6 %collective-permute-start.12 = (bf16[128,512]{1,0:T(8,128)(2,1)S(1)}, bf16[128,512]{1,0:T(8,128)(2,1)S(1)}, u32[]{:S(2)}, u32[]{:S(2)}) collective-permute-start(bf16[128,512]{1,0:T(8,128)(2,1)S(1)} %collective-permute-done.11.refs_0_), channel_id=1, source_target_pairs={{0,8},{4,12},{8,0},{12,4},{16,24},{20,28},{24,16},{28,20},{1,9},{5... | collective-permute-start | bytes 393224 | tf_op jit(solution)/shard_map/ppermute | solution.py:72
  39.4 11.7 %collective-permute-start.17 = (bf16[2,128,512]{2,1,0:T(8,128)(2,1)S(1)}, bf16[2,128,512]{2,1,0:T(8,128)(2,1)S(1)}, u32[]{:S(2)}, u32[]{:S(2)}) collective-permute-start(bf16[2,128,512]{2,1,0:T(8,128)(2,1)S(1)} %stack.46.refs_0_), channel_id=1, source_target_pairs={{0,4},{4,0},{8,12},{12,8},{16,20},{20,16},{24,28},{28,24},{1,5},{5... | collective-permute-start | bytes 786440 | tf_op jit(solution)/shard_map/ppermute | solution.py:72
  42.1 7.7 %collective-permute-start.9 = (bf16[2,4,128,128]{3,2,1,0:T(8,128)(2,1)S(1)}, bf16[2,4,128,128]{3,2,1,0:T(8,128)(2,1)S(1)}, u32[]{:S(2)}, u32[]{:S(2)}) collective-permute-start(bf16[2,4,128,128]{3,2,1,0:T(8,128)(2,1)S(1)} %join_qg.2.a_ref), channel_id=1, source_target_pairs={{0,8},{4,12},{8,0},{12,4},{16,24},{20,28},{24,16},{28,20},{1,9},{5... | collective-permute-start | bytes 786440 | tf_op jit(solution)/shard_map/ppermute | solution.py:72
  44.4 9.3 %collective-permute-start.20 = (bf16[8,32,512]{2,1,0:T(8,128)(2,1)S(1)}, bf16[8,32,512]{2,1,0:T(8,128)(2,1)S(1)}, u32[]{:S(2)}, u32[]{:S(2)}) collective-permute-start(bf16[8,32,512]{2,1,0:T(8,128)(2,1)S(1)} %get-tuple-element.75), channel_id=1, source_target_pairs={{0,2},{1,3},{2,0},{3,1},{4,6},{5,7},{6,4},{7,5},{8,10},{9,11},{10,... | collective-permute-start | bytes 786440 | tf_op jit(solution)/shard_map/ppermute | solution.py:72
  46.0 7.8 %collective-permute-start.19 = (bf16[8,32,512]{2,1,0:T(8,128)(2,1)S(1)}, bf16[8,32,512]{2,1,0:T(8,128)(2,1)S(1)}, u32[]{:S(2)}, u32[]{:S(2)}) collective-permute-start(bf16[8,32,512]{2,1,0:T(8,128)(2,1)S(1)} %get-tuple-element.75), channel_id=1, source_target_pairs={{0,1},{1,0},{2,3},{3,2},{4,5},{5,4},{6,7},{7,6},{8,9},{9,8},{10,11... | collective-permute-start | bytes 786440 | tf_op jit(solution)/shard_map/ppermute | solution.py:72
  46.2 11.0 %collective-permute-start.16 = (bf16[128,1024]{1,0:T(8,128)(2,1)S(1)}, bf16[128,1024]{1,0:T(8,128)(2,1)S(1)}, u32[]{:S(2)}, u32[]{:S(2)}) collective-permute-start(bf16[128,1024]{1,0:T(8,128)(2,1)S(1)} %fusion), channel_id=1, source_target_pairs={{0,2},{1,3},{2,0},{3,1},{4,6},{5,7},{6,4},{7,5},{8,10},{9,11},{10,... | collective-permute-start | bytes 786440 | tf_op jit(solution)/shard_map/ppermute | solution.py:72
  49.8 8.5 %collective-permute-start.18 = (bf16[2,128,512]{2,1,0:T(8,128)(2,1)S(1)}, bf16[2,128,512]{2,1,0:T(8,128)(2,1)S(1)}, u32[]{:S(2)}, u32[]{:S(2)}) collective-permute-start(bf16[2,128,512]{2,1,0:T(8,128)(2,1)S(1)} %stack.47.refs_2_), channel_id=1, source_target_pairs={{0,4},{4,0},{8,12},{12,8},{16,20},{20,16},{24,28},{28,24},{1,5},{5... | collective-permute-start | bytes 786440 | tf_op jit(solution)/shard_map/ppermute | solution.py:72
  51.2 7.2 %collective-permute-start.14 = (bf16[4,128,128]{2,1,0:T(8,128)(2,1)S(1)}, bf16[4,128,128]{2,1,0:T(8,128)(2,1)S(1)}, u32[]{:S(2)}, u32[]{:S(2)}) collective-permute-start(bf16[4,128,128]{2,1,0:T(8,128)(2,1)S(1)} %fusion.7), channel_id=1, source_target_pairs={{0,16},{4,20},{8,24},{12,28},{16,0},{20,4},{24,8},{28,12},{1,17},{... | collective-permute-start | bytes 393224 | tf_op jit(solution)/shard_map/ppermute | solution.py:72
  53.7 4.8 %collective-permute-start.21 = (bf16[8,32,512]{2,1,0:T(8,128)(2,1)S(1)}, bf16[8,32,512]{2,1,0:T(8,128)(2,1)S(1)}, u32[]{:S(2)}, u32[]{:S(2)}) collective-permute-start(bf16[8,32,512]{2,1,0:T(8,128)(2,1)S(1)} %collective-permute-done.20), channel_id=1, source_target_pairs={{0,1},{1,0},{2,3},{3,2},{4,5},{5,4},{6,7},{7,6},{8,9},{9,8},{10,11... | collective-permute-start | bytes 786440 | tf_op jit(solution)/shard_map/ppermute | solution.py:72

commit v5 on v4

--- a/solution.py
+++ b/solution.py
@@ -205,29 +205,34 @@
                  state_ref, hidden_ref, g_ref, qown_ref, qsend_ref):
     length = q_ref.shape[1]
     mask = lower(length)
-    for i in range(q_ref.shape[2] // HEAD_DIM):
-        c = head_cols(i)
+    heads = q_ref.shape[2] // HEAD_DIM
+    blocks = [(i, p) for i in range(heads) for p in range(2)]
+    rows = [slice(p * length, (p + 1) * length) for p in range(2)]
+    queries = {(i, p): q_ref[p, :, head_cols(i)] for i, p in blocks}
+    scores = {(i, p): mm(queries[i, p], k_ref[p, :, head_cols(i)], NT) for i, p in blocks}
+    states = {}
+    for i in range(heads):
         below = below_ref[i]
-        states = (below, below + own_ref[i] + above_ref[i])
-        terms = []
-        for p in range(2):
-            r = slice(p * length, (p + 1) * length)
-            q, k, v = q_ref[p, :, c], k_ref[p, :, c], v_ref[p, :, c]
-            state = states[p].astype(jnp.bfloat16)
-            state_ref[p, i] = state
-            weights = jnp.where(mask, mm(q, k, NT), 0.0).astype(jnp.bfloat16)
-            attended = mm(weights, v, NN) + mm(q, state, NN)
-            scale = jnp.sqrt(jnp.mean(attended * attended, axis=-1, keepdims=True) + EPS)
-            normed = attended / scale
-            hidden_ref[r, c] = normed.astype(jnp.bfloat16)
-            hg = hg_ref[r, c]
-            inner = jnp.mean(hg * normed, axis=-1, keepdims=True)
-            g = ((hg - normed * inner) / scale).astype(jnp.bfloat16)
-            g_ref[p, :, c] = g
-            terms.append(mm(q, g, TN))
-        qown_ref[i] = terms[1]
-        qsend_ref[0, i] = terms[1].astype(jnp.bfloat16)
-        qsend_ref[1, i] = (terms[0] + terms[1]).astype(jnp.bfloat16)
+        states[i, 0] = below.astype(jnp.bfloat16)
+        states[i, 1] = (below + own_ref[i] + above_ref[i]).astype(jnp.bfloat16)
+    carried = {b: mm(queries[b], states[b], NN) for b in blocks}
+    weights = {b: jnp.where(mask, scores[b], 0.0).astype(jnp.bfloat16) for b in blocks}
+    attended = {(i, p): mm(weights[i, p], v_ref[p, :, head_cols(i)], NN) + carried[i, p] for i, p in blocks}
+    squares = {b: jnp.mean(attended[b] * attended[b], axis=-1, keepdims=True) for b in blocks}
+    inverse = {b: lax.rsqrt(squares[b] + EPS) for b in blocks}
+    normed = {b: attended[b] * inverse[b] for b in blocks}
+    grads = {(i, p): hg_ref[rows[p], head_cols(i)] for i, p in blocks}
+    inner = {b: jnp.mean(grads[b] * normed[b], axis=-1, keepdims=True) for b in blocks}
+    g = {b: ((grads[b] - normed[b] * inner[b]) * inverse[b]).astype(jnp.bfloat16) for b in blocks}
+    terms = {b: mm(queries[b], g[b], TN) for b in blocks}
+    for i, p in blocks:
+        state_ref[p, i] = states[i, p]
+        hidden_ref[rows[p], head_cols(i)] = normed[i, p].astype(jnp.bfloat16)
+        g_ref[p, :, head_cols(i)] = g[i, p]
+    for i in range(heads):
+        qown_ref[i] = terms[i, 1]
+        qsend_ref[0, i] = terms[i, 1].astype(jnp.bfloat16)
+        qsend_ref[1, i] = (terms[i, 0] + terms[i, 1]).astype(jnp.bfloat16)
 
 
 def inside_body(q_ref, k_ref, v_ref, g_ref, state_ref, dq_ref, dk_ref, dv_ref):

time: 61.4 us -> 59.6 us (0.971)
  waiting for transfers between devices: 22.8 us -> 20.8 us
  starting transfers between devices: 21.5 us -> 22.7 us
  Pallas kernels: 15 us -> 14 us
    ppermute x22, waiting for transfers between devices: 22.8 us -> 20.8 us  [xor_permute(): return lax.ppermute(x, axis, [(i, i ^ bit) for i in range(count)])]
    ppermute x22, starting transfers between devices: 21.5 us -> 22.7 us  [xor_permute(): return lax.ppermute(x, axis, [(i, i ^ bit) for i in range(count)])]
    pallas_call x10, Pallas kernels: 5.18 us -> 4.19 us  [kernel_call(): pl.pallas_call(body, out_shape=outs, in_specs=whole(len(args)), out_specs...]
  transfers between devices with their start and end apart: 22 -> 22, of which waited for: 10 -> 10; matrix products, arithmetic and copies ran while one was open for 1% -> 1% of each run, Pallas kernels for 18% -> 17%
where the time goes in v5:
time: 59.6 us; the launch traced here: 59.5 us
  starting transfers between devices  22.7 us (38%)
  waiting for transfers between devices  20.8 us (35%)
  Pallas kernels  14 us (23%)
  between operations  0.97 us (2%)
  other arithmetic  0.84 us (1%)
    ppermute x22, starting transfers between devices, xor_permute(): return lax.ppermute(x, axis, [(i, i ^ bit) for i in range(count)])  22.7 us
    ppermute x22, waiting for transfers between devices, xor_permute(): return lax.ppermute(x, axis, [(i, i ^ bit) for i in range(count)])  20.8 us
    pallas_call x10, Pallas kernels, kernel_call(): pl.pallas_call(body, out_shape=outs, in_specs=whole(len(args)), out_specs...  4.19 us
    pallas_call x1, Pallas kernels, hidden_grad_of(): pl.pallas_call(functools.partial(far_body, n), out_shape=(shaped((rows, f...  3.03 us
    pallas_call x1, Pallas kernels, last_call(): pl.pallas_call(functools.partial(last_body, slots), out_shape=shapes, in_...  2.59 us
    pallas_call x1, Pallas kernels, near_grad_of(): pl.pallas_call(near_body, out_shape=(shaped((rows, features), jnp.float32...  2.35 us
    pallas_call x1, Pallas kernels, kv_products(): pl.pallas_call(kv_body, out_shape=(shaped(square, jnp.float32), shaped((2...  1.25 us
  transfers between devices with their start and end apart: 22, of which 10 were waited for; matrix products, arithmetic and copies ran while one was open for 1% of the time, Pallas kernels for 17%

profile of v5, /device:TPU:0, one launch (start us, length us, event | category | flops | bytes accessed | tf_op | source)
XLA Modules:
  0.0 59.5 jit_solution(7487800831041079745)
XLA Ops:
  0.6 1.3 %shard_map.92 = (f32[4,128,128]{2,1,0:T(8,128)S(1)}, bf16[2,4,128,128]{3,2,1,0:T(8,128)(2,1)S(1)}) custom-call(bf16[2,64,512]{2,1,0:T(8,128)(2,1)} %k_ref.5, bf16[2,64,512]{2,1,0:T(8,128)(2,1)} %v_ref.5), custom_call_target="tpu_custom_call" | custom-call | tf_op jit(solution)/shard_map/pallas_call | solution.py:124
  1.9 3.0 %collective-permute-start.4 = (bf16[2,4,128,128]{3,2,1,0:T(8,128)(2,1)S(1)}, bf16[2,4,128,128]{3,2,1,0:T(8,128)(2,1)S(1)}, u32[]{:S(2)}, u32[]{:S(2)}) collective-permute-start(bf16[2,4,128,128]{3,2,1,0:T(8,128)(2,1)S(1)} %get-tuple-element.49.a_ref), channel_id=1, source_target_pairs={{0,4},{4,0},{8,12},{12,8},{16,20},{20,16},{24,28},{28,24},{1,5},{5... | collective-permute-start | bytes 786440 | tf_op jit(solution)/shard_map/ppermute | solution.py:72
  4.9 1.5 %collective-permute-start.1 = (bf16[128,1024]{1,0:T(8,128)(2,1)}, bf16[128,1024]{1,0:T(8,128)(2,1)S(1)}, u32[]{:S(2)}, u32[]{:S(2)}) collective-permute-start(bf16[128,1024]{1,0:T(8,128)(2,1)} %bitcast.62), channel_id=1, source_target_pairs={{0,2},{1,3},{2,0},{3,1},{4,6},{5,7},{6,4},{7,5},{8,10},{9,11},{10,... | collective-permute-start | bytes 786440 | tf_op jit(solution)/shard_map/ppermute | solution.py:72
  6.4 0.1 pad_add_fusion.spot_ref
  6.5 4.7 %collective-permute-done.4.b_ref = bf16[2,4,128,128]{3,2,1,0:T(8,128)(2,1)S(1)} collective-permute-done((bf16[2,4,128,128]{3,2,1,0:T(8,128)(2,1)S(1)}, bf16[2,4,128,128]{3,2,1,0:T(8,128)(2,1)S(1)}, u32[]{:S(2)}, u32[]{:S(2)}) %collective-permute-start.4) | collective-permute-done | bytes 262176 | tf_op jit(solution)/shard_map/ppermute | solution.py:72
  11.2 0.1 join_kv.2.a_ref
  11.3 1.9 %collective-permute-start.5 = (bf16[2,4,128,128]{3,2,1,0:T(8,128)(2,1)S(1)}, bf16[2,4,128,128]{3,2,1,0:T(8,128)(2,1)S(1)}, u32[]{:S(2)}, u32[]{:S(2)}) collective-permute-start(bf16[2,4,128,128]{3,2,1,0:T(8,128)(2,1)S(1)} %join_kv.2.a_ref), channel_id=1, source_target_pairs={{0,8},{4,12},{8,0},{12,4},{16,24},{20,28},{24,16},{28,20},{1,9},{5... | collective-permute-start | bytes 786440 | tf_op jit(solution)/shard_map/ppermute | solution.py:72
  13.2 2.4 %near.1 = (f32[128,512]{1,0:T(8,128)S(1)}, bf16[128,1024]{1,0:T(8,128)(2,1)S(1)}) custom-call(s32[2]{0:T(128)S(1)} %pad_add_fusion.spot_ref, bf16[512,4096]{1,0:T(8,128)(2,1)} %w_hbm.3, bf16[128,1024]{1,0:T(8,128)(2,1)} %bitcast.64), custom_call_target="tpu_custom_call" | custom-call | flops 3300000000 | tf_op jit(solution)/shard_map/near/pallas_call | solution.py:163
  15.5 0.6 quarter.1
  16.2 1.6 %collective-permute-start.3 = (bf16[4,32,512]{2,1,0:T(8,128)(2,1)S(1)}, bf16[4,32,512]{2,1,0:T(8,128)(2,1)S(1)}, u32[]{:S(2)}, u32[]{:S(2)}) collective-permute-start(bf16[4,32,512]{2,1,0:T(8,128)(2,1)S(1)} %get-tuple-element.57), channel_id=1, source_target_pairs={{0,4},{4,0},{8,12},{12,8},{16,20},{20,16},{24,28},{28,24},{1,5},{5... | collective-permute-start | bytes 393224 | tf_op jit(solution)/shard_map/ppermute | solution.py:72
  17.7 1.1 %collective-permute-done.5.b_ref = bf16[2,4,128,128]{3,2,1,0:T(8,128)(2,1)S(1)} collective-permute-done((bf16[2,4,128,128]{3,2,1,0:T(8,128)(2,1)S(1)}, bf16[2,4,128,128]{3,2,1,0:T(8,128)(2,1)S(1)}, u32[]{:S(2)}, u32[]{:S(2)}) %collective-permute-start.5) | collective-permute-done | bytes 262176 | tf_op jit(solution)/shard_map/ppermute | solution.py:72
  18.9 0.1 join_kv.3
  18.9 2.5 %collective-permute-start.6 = (bf16[4,128,128]{2,1,0:T(8,128)(2,1)S(1)}, bf16[4,128,128]{2,1,0:T(8,128)(2,1)S(1)}, u32[]{:S(2)}, u32[]{:S(2)}) collective-permute-start(bf16[4,128,128]{2,1,0:T(8,128)(2,1)S(1)} %fusion.8), channel_id=1, source_target_pairs={{0,16},{4,20},{8,24},{12,28},{16,0},{20,4},{24,8},{28,12},{1,17},{... | collective-permute-start | bytes 393224 | tf_op jit(solution)/shard_map/ppermute | solution.py:72
  21.5 0.0 copy-start.1
  21.6 0.0 copy-start.2
  21.6 3.0 %far.1 = (f32[128,512]{1,0:T(8,128)S(1)}, bf16[4,512,1024]{2,1,0:T(8,128)(2,1)S(1)}) custom-call(s32[2]{0:T(128)S(1)} %pad_add_fusion.spot_ref, bf16[512,4096]{1,0:T(8,128)(2,1)} %w_hbm.3, f32[128,512]{1,0:T(8,128)S(1)} %get-tuple-element.51.before_ref, bf16[128,1024]{1,0:T(8,128)(2,1)S(1)} %collective-permute-done.refs_0_.refs_1_, ...), custom_call_target="tpu_custom_call" | custom-call | flops 11000000 | tf_op jit(solution)/shard_map/far/pallas_call | solution.py:192
  24.7 1.7 %collective-permute-start.7 = (bf16[2,2,32,512]{3,2,1,0:T(8,128)(2,1)S(1)}, bf16[2,2,32,512]{3,2,1,0:T(8,128)(2,1)S(1)}, u32[]{:S(2)}, u32[]{:S(2)}) collective-permute-start(bf16[2,2,32,512]{3,2,1,0:T(8,128)(2,1)S(1)} %fusion.6), channel_id=1, source_target_pairs={{0,8},{4,12},{8,0},{12,4},{16,24},{20,28},{24,16},{28,20},{1,9},{5... | collective-permute-start | bytes 393224 | tf_op jit(solution)/shard_map/ppermute | solution.py:72
  26.3 0.9 %collective-permute-done.6 = bf16[4,128,128]{2,1,0:T(8,128)(2,1)S(1)} collective-permute-done((bf16[4,128,128]{2,1,0:T(8,128)(2,1)S(1)}, bf16[4,128,128]{2,1,0:T(8,128)(2,1)S(1)}, u32[]{:S(2)}, u32[]{:S(2)}) %collective-permute-start.6) | collective-permute-done | bytes 131104 | tf_op jit(solution)/shard_map/ppermute | solution.py:72
  27.2 0.1 add_select_fusion.4
  27.3 0.8 %forward.1 = (bf16[2,4,128,128]{3,2,1,0:T(8,128)(2,1)S(1)}, bf16[128,512]{1,0:T(8,128)(2,1)S(1)}, bf16[2,64,512]{2,1,0:T(8,128)(2,1)S(1)}, f32[4,128,128]{2,1,0:T(8,128)S(1)}, bf16[2,4,128,128]{3,2,1,0:T(8,128)(2,1)S(1)}) custom-call(bf16[2,64,512]{2,1,0:T(8,128)(2,1)S(1)} %copy-done.2, bf16[2,64,512]{2,1,0:T(8,128)(2,1)S(1)} %copy-done, ...), custom_call_target="tpu_custom_call" | custom-call | flops 11000000 | tf_op jit(solution)/shard_map/forward/pallas_call | solution.py:84
  28.1 0.2 collective-permute-start.11
  28.4 3.0 %collective-permute-start.15 = (bf16[128,512]{1,0:T(8,128)(2,1)S(1)}, bf16[128,512]{1,0:T(8,128)(2,1)S(1)}, u32[]{:S(2)}, u32[]{:S(2)}) collective-permute-start(bf16[128,512]{1,0:T(8,128)(2,1)S(1)} %get-tuple-element.81.hidden_ref.refs_0_), channel_id=1, source_target_pairs={{0,8},{4,12},{8,0},{12,4},{16,24},{20,28},{24,16},{28,20},{1,9},{5... | collective-permute-start | bytes 393224 | tf_op jit(solution)/shard_map/ppermute | solution.py:72
  31.4 0.4 project.3
  31.8 0.1 collective-permute-start.13
  31.9 2.6 %collective-permute-start.8 = (bf16[2,4,128,128]{3,2,1,0:T(8,128)(2,1)S(1)}, bf16[2,4,128,128]{3,2,1,0:T(8,128)(2,1)S(1)}, u32[]{:S(2)}, u32[]{:S(2)}) collective-permute-start(bf16[2,4,128,128]{3,2,1,0:T(8,128)(2,1)S(1)} %get-tuple-element.70.a_ref), channel_id=1, source_target_pairs={{0,4},{4,0},{8,12},{12,8},{16,20},{20,16},{24,28},{28,24},{1,5},{5... | collective-permute-start | bytes 786440 | tf_op jit(solution)/shard_map/ppermute | solution.py:72
  34.5 0.1 collective-permute-start.10
  34.6 1.1 %collective-permute-done.11.refs_0_ = bf16[128,512]{1,0:T(8,128)(2,1)S(1)} collective-permute-done((bf16[128,512]{1,0:T(8,128)(2,1)S(1)}, bf16[128,512]{1,0:T(8,128)(2,1)S(1)}, u32[]{:S(2)}, u32[]{:S(2)}) %collective-permute-start.11) | collective-permute-done | bytes 131104 | tf_op jit(solution)/shard_map/ppermute | solution.py:72
  35.7 0.0 collective-permute-start.12
  35.8 2.2 %inside.1 = (bf16[2,64,512]{2,1,0:T(8,128)(2,1)}, f32[2,64,512]{2,1,0:T(8,128)S(1)}, f32[2,64,512]{2,1,0:T(8,128)S(1)}) custom-call(bf16[2,64,512]{2,1,0:T(8,128)(2,1)S(1)} %copy-done.2, bf16[2,64,512]{2,1,0:T(8,128)(2,1)S(1)} %copy-done, bf16[2,64,512]{2,1,0:T(8,128)(2,1)S(1)} %copy-done.1, bf16[2,64,512]{2,1,0:T(8,128)(2,1)S(1)} %get-tuple-element.62.g_ref, ...), custom_call_target="tpu_custom_call" | custom-call | flops 5500000256 | tf_op jit(solution)/shard_map/inside/pallas_call | solution.py:84
  38.0 0.4 project.2
  38.5 0.5 collective-permute-start.17
  39.0 2.6 %collective-permute-done.8.b_ref = bf16[2,4,128,128]{3,2,1,0:T(8,128)(2,1)S(1)} collective-permute-done((bf16[2,4,128,128]{3,2,1,0:T(8,128)(2,1)S(1)}, bf16[2,4,128,128]{3,2,1,0:T(8,128)(2,1)S(1)}, u32[]{:S(2)}, u32[]{:S(2)}) %collective-permute-start.8) | collective-permute-done | bytes 262176 | tf_op jit(solution)/shard_map/ppermute | solution.py:72
  41.6 0.1 join_qg.2.a_ref
  41.7 0.1 collective-permute-start.9
  41.8 1.8 %collective-permute-done.12.refs_1_ = bf16[128,512]{1,0:T(8,128)(2,1)S(1)} collective-permute-done((bf16[128,512]{1,0:T(8,128)(2,1)S(1)}, bf16[128,512]{1,0:T(8,128)(2,1)S(1)}, u32[]{:S(2)}, u32[]{:S(2)}) %collective-permute-start.12) | collective-permute-done | bytes 131104 | tf_op jit(solution)/shard_map/ppermute | solution.py:72
  43.6 1.6 %collective-permute-start.20 = (bf16[8,32,512]{2,1,0:T(8,128)(2,1)S(1)}, bf16[8,32,512]{2,1,0:T(8,128)(2,1)S(1)}, u32[]{:S(2)}, u32[]{:S(2)}) collective-permute-start(bf16[8,32,512]{2,1,0:T(8,128)(2,1)S(1)} %get-tuple-element.75), channel_id=1, source_target_pairs={{0,2},{1,3},{2,0},{3,1},{4,6},{5,7},{6,4},{7,5},{8,10},{9,11},{10,... | collective-permute-start | bytes 786440 | tf_op jit(solution)/shard_map/ppermute | solution.py:72
  45.3 0.2 convert_add_fusion
  45.5 0.6 collective-permute-start.16
  46.1 2.6 %collective-permute-done.9.b_ref = bf16[2,4,128,128]{3,2,1,0:T(8,128)(2,1)S(1)} collective-permute-done((bf16[2,4,128,128]{3,2,1,0:T(8,128)(2,1)S(1)}, bf16[2,4,128,128]{3,2,1,0:T(8,128)(2,1)S(1)}, u32[]{:S(2)}, u32[]{:S(2)}) %collective-permute-start.9) | collective-permute-done | bytes 262176 | tf_op jit(solution)/shard_map/ppermute | solution.py:72
  48.7 1.0 %collective-permute-start.18 = (bf16[2,128,512]{2,1,0:T(8,128)(2,1)S(1)}, bf16[2,128,512]{2,1,0:T(8,128)(2,1)S(1)}, u32[]{:S(2)}, u32[]{:S(2)}) collective-permute-start(bf16[2,128,512]{2,1,0:T(8,128)(2,1)S(1)} %stack.47.refs_2_), channel_id=1, source_target_pairs={{0,4},{4,0},{8,12},{12,8},{16,20},{20,16},{24,28},{28,24},{1,5},{5... | collective-permute-start | bytes 786440 | tf_op jit(solution)/shard_map/ppermute | solution.py:72
  49.7 0.1 join_qg.3
  49.8 0.8 %collective-permute-start.14 = (bf16[4,128,128]{2,1,0:T(8,128)(2,1)S(1)}, bf16[4,128,128]{2,1,0:T(8,128)(2,1)S(1)}, u32[]{:S(2)}, u32[]{:S(2)}) collective-permute-start(bf16[4,128,128]{2,1,0:T(8,128)(2,1)S(1)} %fusion.7), channel_id=1, source_target_pairs={{0,16},{4,20},{8,24},{12,28},{16,0},{20,4},{24,8},{28,12},{1,17},{... | collective-permute-start | bytes 393224 | tf_op jit(solution)/shard_map/ppermute | solution.py:72
  50.6 1.5 %collective-permute-done.20 = bf16[8,32,512]{2,1,0:T(8,128)(2,1)S(1)} collective-permute-done((bf16[8,32,512]{2,1,0:T(8,128)(2,1)S(1)}, bf16[8,32,512]{2,1,0:T(8,128)(2,1)S(1)}, u32[]{:S(2)}, u32[]{:S(2)}) %collective-permute-start.20) | collective-permute-done | bytes 262176 | tf_op jit(solution)/shard_map/ppermute | solution.py:72
  52.2 3.8 %collective-permute-done.16.got_ref = bf16[128,1024]{1,0:T(8,128)(2,1)S(1)} collective-permute-done((bf16[128,1024]{1,0:T(8,128)(2,1)S(1)}, bf16[128,1024]{1,0:T(8,128)(2,1)S(1)}, u32[]{:S(2)}, u32[]{:S(2)}) %collective-permute-start.16) | collective-permute-done | bytes 262176 | tf_op jit(solution)/shard_map/ppermute | solution.py:72
  56.0 0.6 collective-permute-done.14
  56.6 0.1 add_select_fusion
  56.7 0.1 pad_maximum_fusion.refs_4_
  56.9 2.6 %last.1 = (bf16[2,64,512]{2,1,0:T(8,128)(2,1)}, bf16[2,64,512]{2,1,0:T(8,128)(2,1)}, bf16[128,1024]{1,0:T(8,128)(2,1)}, f32[512,512]{1,0:T(8,128)}) custom-call(s32[2]{0:T(128)S(1)} %pad_add_fusion.spot_ref, bf16[2,64,512]{2,1,0:T(8,128)(2,1)S(1)} %copy-done, bf16[2,64,512]{2,1,0:T(8,128)(2,1)S(1)} %copy-done.1, ...), custom_call_target="tpu_custom_call" | custom-call | flops 1100000000 | tf_op jit(solution)/shard_map/last/pallas_call | solution.py:294
  (34 shorter events, 0.4 us)
Async XLA Ops:
  1.9 9.3 %collective-permute-start.4 = (bf16[2,4,128,128]{3,2,1,0:T(8,128)(2,1)S(1)}, bf16[2,4,128,128]{3,2,1,0:T(8,128)(2,1)S(1)}, u32[]{:S(2)}, u32[]{:S(2)}) collective-permute-start(bf16[2,4,128,128]{3,2,1,0:T(8,128)(2,1)S(1)} %get-tuple-element.49.a_ref), channel_id=1, source_target_pairs={{0,4},{4,0},{8,12},{12,8},{16,20},{20,16},{24,28},{28,24},{1,5},{5... | collective-permute-start | bytes 786440 | tf_op jit(solution)/shard_map/ppermute | solution.py:72
  4.9 8.2 %collective-permute-start.1 = (bf16[128,1024]{1,0:T(8,128)(2,1)}, bf16[128,1024]{1,0:T(8,128)(2,1)S(1)}, u32[]{:S(2)}, u32[]{:S(2)}) collective-permute-start(bf16[128,1024]{1,0:T(8,128)(2,1)} %bitcast.62), channel_id=1, source_target_pairs={{0,2},{1,3},{2,0},{3,1},{4,6},{5,7},{6,4},{7,5},{8,10},{9,11},{10,... | collective-permute-start | bytes 786440 | tf_op jit(solution)/shard_map/ppermute | solution.py:72
  6.4 9.1 %collective-permute-start = (bf16[128,1024]{1,0:T(8,128)(2,1)}, bf16[128,1024]{1,0:T(8,128)(2,1)S(1)}, u32[]{:S(2)}, u32[]{:S(2)}) collective-permute-start(bf16[128,1024]{1,0:T(8,128)(2,1)} %bitcast.63), channel_id=1, source_target_pairs={{0,1},{1,0},{2,3},{3,2},{4,5},{5,4},{6,7},{7,6},{8,9},{9,8},{10,11... | collective-permute-start | bytes 786440 | tf_op jit(solution)/shard_map/ppermute | solution.py:72
  11.3 7.6 %collective-permute-start.5 = (bf16[2,4,128,128]{3,2,1,0:T(8,128)(2,1)S(1)}, bf16[2,4,128,128]{3,2,1,0:T(8,128)(2,1)S(1)}, u32[]{:S(2)}, u32[]{:S(2)}) collective-permute-start(bf16[2,4,128,128]{3,2,1,0:T(8,128)(2,1)S(1)} %join_kv.2.a_ref), channel_id=1, source_target_pairs={{0,8},{4,12},{8,0},{12,4},{16,24},{20,28},{24,16},{28,20},{1,9},{5... | collective-permute-start | bytes 786440 | tf_op jit(solution)/shard_map/ppermute | solution.py:72
  13.2 2.4 %collective-permute-start.2 = (bf16[128,1024]{1,0:T(8,128)(2,1)S(1)}, bf16[128,1024]{1,0:T(8,128)(2,1)S(1)}, u32[]{:S(2)}, u32[]{:S(2)}) collective-permute-start(bf16[128,1024]{1,0:T(8,128)(2,1)S(1)} %collective-permute-done.1.refs_1_.refs_2_), channel_id=1, source_target_pairs={{0,1},{1,0},{2,3},{3,2},{4,5},{5,4},{6,7},{7,6},{8,9},{9,8},{10,11... | collective-permute-start | bytes 786440 | tf_op jit(solution)/shard_map/ppermute | solution.py:72
  16.2 8.5 %collective-permute-start.3 = (bf16[4,32,512]{2,1,0:T(8,128)(2,1)S(1)}, bf16[4,32,512]{2,1,0:T(8,128)(2,1)S(1)}, u32[]{:S(2)}, u32[]{:S(2)}) collective-permute-start(bf16[4,32,512]{2,1,0:T(8,128)(2,1)S(1)} %get-tuple-element.57), channel_id=1, source_target_pairs={{0,4},{4,0},{8,12},{12,8},{16,20},{20,16},{24,28},{28,24},{1,5},{5... | collective-permute-start | bytes 393224 | tf_op jit(solution)/shard_map/ppermute | solution.py:72
  18.9 8.3 %collective-permute-start.6 = (bf16[4,128,128]{2,1,0:T(8,128)(2,1)S(1)}, bf16[4,128,128]{2,1,0:T(8,128)(2,1)S(1)}, u32[]{:S(2)}, u32[]{:S(2)}) collective-permute-start(bf16[4,128,128]{2,1,0:T(8,128)(2,1)S(1)} %fusion.8), channel_id=1, source_target_pairs={{0,16},{4,20},{8,24},{12,28},{16,0},{20,4},{24,8},{28,12},{1,17},{... | collective-permute-start | bytes 393224 | tf_op jit(solution)/shard_map/ppermute | solution.py:72
  21.5 5.8 %copy-start = (bf16[2,64,512]{2,1,0:T(8,128)(2,1)S(1)}, bf16[2,64,512]{2,1,0:T(8,128)(2,1)}, u32[]{:S(2)}) copy-start(bf16[2,64,512]{2,1,0:T(8,128)(2,1)} %k_ref.5) | copy-start | bytes 393220
  21.5 5.8 %copy-start.1 = (bf16[2,64,512]{2,1,0:T(8,128)(2,1)S(1)}, bf16[2,64,512]{2,1,0:T(8,128)(2,1)}, u32[]{:S(2)}) copy-start(bf16[2,64,512]{2,1,0:T(8,128)(2,1)} %v_ref.5) | copy-start | bytes 393220
  21.6 5.8 %copy-start.2 = (bf16[2,64,512]{2,1,0:T(8,128)(2,1)S(1)}, bf16[2,64,512]{2,1,0:T(8,128)(2,1)}, u32[]{:S(2)}) copy-start(bf16[2,64,512]{2,1,0:T(8,128)(2,1)} %q_ref.3) | copy-start | bytes 393220
  24.7 7.2 %collective-permute-start.7 = (bf16[2,2,32,512]{3,2,1,0:T(8,128)(2,1)S(1)}, bf16[2,2,32,512]{3,2,1,0:T(8,128)(2,1)S(1)}, u32[]{:S(2)}, u32[]{:S(2)}) collective-permute-start(bf16[2,2,32,512]{3,2,1,0:T(8,128)(2,1)S(1)} %fusion.6), channel_id=1, source_target_pairs={{0,8},{4,12},{8,0},{12,4},{16,24},{20,28},{24,16},{28,20},{1,9},{5... | collective-permute-start | bytes 393224 | tf_op jit(solution)/shard_map/ppermute | solution.py:72
  28.1 7.6 %collective-permute-start.11 = (bf16[128,512]{1,0:T(8,128)(2,1)S(1)}, bf16[128,512]{1,0:T(8,128)(2,1)S(1)}, u32[]{:S(2)}, u32[]{:S(2)}) collective-permute-start(bf16[128,512]{1,0:T(8,128)(2,1)S(1)} %get-tuple-element.81.hidden_ref.refs_0_), channel_id=1, source_target_pairs={{0,16},{4,20},{8,24},{12,28},{16,0},{20,4},{24,8},{28,12},{1,17},{... | collective-permute-start | bytes 393224 | tf_op jit(solution)/shard_map/ppermute | solution.py:72
  28.4 10.1 %collective-permute-start.15 = (bf16[128,512]{1,0:T(8,128)(2,1)S(1)}, bf16[128,512]{1,0:T(8,128)(2,1)S(1)}, u32[]{:S(2)}, u32[]{:S(2)}) collective-permute-start(bf16[128,512]{1,0:T(8,128)(2,1)S(1)} %get-tuple-element.81.hidden_ref.refs_0_), channel_id=1, source_target_pairs={{0,8},{4,12},{8,0},{12,4},{16,24},{20,28},{24,16},{28,20},{1,9},{5... | collective-permute-start | bytes 393224 | tf_op jit(solution)/shard_map/ppermute | solution.py:72
  31.8 13.5 %collective-permute-start.13 = (bf16[2,128,1024]{2,1,0:T(8,128)(2,1)S(1)}, bf16[2,128,1024]{2,1,0:T(8,128)(2,1)S(1)}, u32[]{:S(2)}, u32[]{:S(2)}) collective-permute-start(bf16[2,128,1024]{2,1,0:T(8,128)(2,1)S(1)} %project.3), channel_id=1, source_target_pairs={{0,1},{1,0},{2,3},{3,2},{4,5},{5,4},{6,7},{7,6},{8,9},{9,8},{10,11... | collective-permute-start | bytes 1572872 | tf_op jit(solution)/shard_map/ppermute | solution.py:72
  31.9 9.7 %collective-permute-start.8 = (bf16[2,4,128,128]{3,2,1,0:T(8,128)(2,1)S(1)}, bf16[2,4,128,128]{3,2,1,0:T(8,128)(2,1)S(1)}, u32[]{:S(2)}, u32[]{:S(2)}) collective-permute-start(bf16[2,4,128,128]{3,2,1,0:T(8,128)(2,1)S(1)} %get-tuple-element.70.a_ref), channel_id=1, source_target_pairs={{0,4},{4,0},{8,12},{12,8},{16,20},{20,16},{24,28},{28,24},{1,5},{5... | collective-permute-start | bytes 786440 | tf_op jit(solution)/shard_map/ppermute | solution.py:72
  34.5 9.1 %collective-permute-start.10 = (bf16[4,32,512]{2,1,0:T(8,128)(2,1)S(1)}, bf16[4,32,512]{2,1,0:T(8,128)(2,1)S(1)}, u32[]{:S(2)}, u32[]{:S(2)}) collective-permute-start(bf16[4,32,512]{2,1,0:T(8,128)(2,1)S(1)} %get-tuple-element.100), channel_id=1, source_target_pairs={{0,16},{4,20},{8,24},{12,28},{16,0},{20,4},{24,8},{28,12},{1,17},{... | collective-permute-start | bytes 393224 | tf_op jit(solution)/shard_map/ppermute | solution.py:72
  35.7 7.9 %collective-permute-start.12 = (bf16[128,512]{1,0:T(8,128)(2,1)S(1)}, bf16[128,512]{1,0:T(8,128)(2,1)S(1)}, u32[]{:S(2)}, u32[]{:S(2)}) collective-permute-start(bf16[128,512]{1,0:T(8,128)(2,1)S(1)} %collective-permute-done.11.refs_0_), channel_id=1, source_target_pairs={{0,8},{4,12},{8,0},{12,4},{16,24},{20,28},{24,16},{28,20},{1,9},{5... | collective-permute-start | bytes 393224 | tf_op jit(solution)/shard_map/ppermute | solution.py:72
  38.5 11.3 %collective-permute-start.17 = (bf16[2,128,512]{2,1,0:T(8,128)(2,1)S(1)}, bf16[2,128,512]{2,1,0:T(8,128)(2,1)S(1)}, u32[]{:S(2)}, u32[]{:S(2)}) collective-permute-start(bf16[2,128,512]{2,1,0:T(8,128)(2,1)S(1)} %stack.46.refs_0_), channel_id=1, source_target_pairs={{0,4},{4,0},{8,12},{12,8},{16,20},{20,16},{24,28},{28,24},{1,5},{5... | collective-permute-start | bytes 786440 | tf_op jit(solution)/shard_map/ppermute | solution.py:72
  41.7 7.0 %collective-permute-start.9 = (bf16[2,4,128,128]{3,2,1,0:T(8,128)(2,1)S(1)}, bf16[2,4,128,128]{3,2,1,0:T(8,128)(2,1)S(1)}, u32[]{:S(2)}, u32[]{:S(2)}) collective-permute-start(bf16[2,4,128,128]{3,2,1,0:T(8,128)(2,1)S(1)} %join_qg.2.a_ref), channel_id=1, source_target_pairs={{0,8},{4,12},{8,0},{12,4},{16,24},{20,28},{24,16},{28,20},{1,9},{5... | collective-permute-start | bytes 786440 | tf_op jit(solution)/shard_map/ppermute | solution.py:72
  43.6 8.4 %collective-permute-start.20 = (bf16[8,32,512]{2,1,0:T(8,128)(2,1)S(1)}, bf16[8,32,512]{2,1,0:T(8,128)(2,1)S(1)}, u32[]{:S(2)}, u32[]{:S(2)}) collective-permute-start(bf16[8,32,512]{2,1,0:T(8,128)(2,1)S(1)} %get-tuple-element.75), channel_id=1, source_target_pairs={{0,2},{1,3},{2,0},{3,1},{4,6},{5,7},{6,4},{7,5},{8,10},{9,11},{10,... | collective-permute-start | bytes 786440 | tf_op jit(solution)/shard_map/ppermute | solution.py:72
  45.2 7.0 %collective-permute-start.19 = (bf16[8,32,512]{2,1,0:T(8,128)(2,1)S(1)}, bf16[8,32,512]{2,1,0:T(8,128)(2,1)S(1)}, u32[]{:S(2)}, u32[]{:S(2)}) collective-permute-start(bf16[8,32,512]{2,1,0:T(8,128)(2,1)S(1)} %get-tuple-element.75), channel_id=1, source_target_pairs={{0,1},{1,0},{2,3},{3,2},{4,5},{5,4},{6,7},{7,6},{8,9},{9,8},{10,11... | collective-permute-start | bytes 786440 | tf_op jit(solution)/shard_map/ppermute | solution.py:72
  45.5 10.5 %collective-permute-start.16 = (bf16[128,1024]{1,0:T(8,128)(2,1)S(1)}, bf16[128,1024]{1,0:T(8,128)(2,1)S(1)}, u32[]{:S(2)}, u32[]{:S(2)}) collective-permute-start(bf16[128,1024]{1,0:T(8,128)(2,1)S(1)} %fusion), channel_id=1, source_target_pairs={{0,2},{1,3},{2,0},{3,1},{4,6},{5,7},{6,4},{7,5},{8,10},{9,11},{10,... | collective-permute-start | bytes 786440 | tf_op jit(solution)/shard_map/ppermute | solution.py:72
  48.7 7.9 %collective-permute-start.18 = (bf16[2,128,512]{2,1,0:T(8,128)(2,1)S(1)}, bf16[2,128,512]{2,1,0:T(8,128)(2,1)S(1)}, u32[]{:S(2)}, u32[]{:S(2)}) collective-permute-start(bf16[2,128,512]{2,1,0:T(8,128)(2,1)S(1)} %stack.47.refs_2_), channel_id=1, source_target_pairs={{0,4},{4,0},{8,12},{12,8},{16,20},{20,16},{24,28},{28,24},{1,5},{5... | collective-permute-start | bytes 786440 | tf_op jit(solution)/shard_map/ppermute | solution.py:72
  49.8 6.8 %collective-permute-start.14 = (bf16[4,128,128]{2,1,0:T(8,128)(2,1)S(1)}, bf16[4,128,128]{2,1,0:T(8,128)(2,1)S(1)}, u32[]{:S(2)}, u32[]{:S(2)}) collective-permute-start(bf16[4,128,128]{2,1,0:T(8,128)(2,1)S(1)} %fusion.7), channel_id=1, source_target_pairs={{0,16},{4,20},{8,24},{12,28},{16,0},{20,4},{24,8},{28,12},{1,17},{... | collective-permute-start | bytes 393224 | tf_op jit(solution)/shard_map/ppermute | solution.py:72
  52.1 4.6 %collective-permute-start.21 = (bf16[8,32,512]{2,1,0:T(8,128)(2,1)S(1)}, bf16[8,32,512]{2,1,0:T(8,128)(2,1)S(1)}, u32[]{:S(2)}, u32[]{:S(2)}) collective-permute-start(bf16[8,32,512]{2,1,0:T(8,128)(2,1)S(1)} %collective-permute-done.20), channel_id=1, source_target_pairs={{0,1},{1,0},{2,3},{3,2},{4,5},{5,4},{6,7},{7,6},{8,9},{9,8},{10,11... | collective-permute-start | bytes 786440 | tf_op jit(solution)/shard_map/ppermute | solution.py:72

commit v6 on v5

--- a/solution.py
+++ b/solution.py
@@ -105,10 +105,9 @@
         load.start()
     for load in loads:
         load.wait()
-    for i in range(k_ref.shape[2] // HEAD_DIM):
-        c = head_cols(i)
-        first = mm(k_ref[0, :, c], v_ref[0, :, c], TN)
-        second = mm(k_ref[1, :, c], v_ref[1, :, c], TN)
+    heads = k_ref.shape[2] // HEAD_DIM
+    products = [[mm(k_ref[p, :, head_cols(i)], v_ref[p, :, head_cols(i)], TN) for p in range(2)] for i in range(heads)]
+    for i, (first, second) in enumerate(products):
         own_ref[i] = first
         send_ref[0, i] = first.astype(jnp.bfloat16)
         send_ref[1, i] = (first + second).astype(jnp.bfloat16)
@@ -262,15 +261,18 @@
     ]
     out_ref[...] = (sum_ref[...] + got_ref[...].astype(jnp.float32)).astype(out_ref.dtype)
     copies[2].start()
-    for i in range(k_ref.shape[2] // HEAD_DIM):
+    blocks = [(i, p) for i in range(k_ref.shape[2] // HEAD_DIM) for p in range(2)]
+    laters = {}
+    for i, _ in blocks:
+        below = below_ref[i]
+        laters[i, 0] = (below + own_ref[i] + above_ref[i]).astype(jnp.bfloat16)
+        laters[i, 1] = below.astype(jnp.bfloat16)
+    dk = {(i, p): mm(v_ref[p, :, head_cols(i)], laters[i, p], NT) for i, p in blocks}
+    dv = {(i, p): mm(k_ref[p, :, head_cols(i)], laters[i, p], NN) for i, p in blocks}
+    for i, p in blocks:
         c = head_cols(i)
-        below = below_ref[i]
-        laters = (below + own_ref[i] + above_ref[i], below)
-        for p in range(2):
-            later = laters[p].astype(jnp.bfloat16)
-            k, v = k_ref[p, :, c], v_ref[p, :, c]
-            dk_ref[p, :, c] = (dkp_ref[p, :, c] + mm(v, later, NT)).astype(jnp.bfloat16)
-            dv_ref[p, :, c] = (dvp_ref[p, :, c] + mm(k, later, NN)).astype(jnp.bfloat16)
+        dk_ref[p, :, c] = (dkp_ref[p, :, c] + dk[i, p]).astype(jnp.bfloat16)
+        dv_ref[p, :, c] = (dvp_ref[p, :, c] + dv[i, p]).astype(jnp.bfloat16)
     copies[0].start()
     copies[1].start()
     head = spot_ref[1]

time: 59.6 us -> 59.7 us (level)
  no operation moved by 1% of the time
where the time goes in v6:
time: 59.7 us; the launch traced here: 59.5 us
  starting transfers between devices  22.7 us (38%)
  waiting for transfers between devices  20.8 us (35%)
  Pallas kernels  14 us (23%)
  between operations  0.97 us (2%)
  other arithmetic  0.84 us (1%)
    ppermute x22, starting transfers between devices, xor_permute(): return lax.ppermute(x, axis, [(i, i ^ bit) for i in range(count)])  22.7 us
    ppermute x22, waiting for transfers between devices, xor_permute(): return lax.ppermute(x, axis, [(i, i ^ bit) for i in range(count)])  20.8 us
    pallas_call x10, Pallas kernels, kernel_call(): pl.pallas_call(body, out_shape=outs, in_specs=whole(len(args)), out_specs...  4.19 us
    pallas_call x1, Pallas kernels, hidden_grad_of(): pl.pallas_call(functools.partial(far_body, n), out_shape=(shaped((rows, f...  3.03 us
    pallas_call x1, Pallas kernels, last_call(): pl.pallas_call(functools.partial(last_body, slots), out_shape=shapes, in_...  2.62 us
    pallas_call x1, Pallas kernels, near_grad_of(): pl.pallas_call(near_body, out_shape=(shaped((rows, features), jnp.float32...  2.35 us
    pallas_call x1, Pallas kernels, kv_products(): pl.pallas_call(kv_body, out_shape=(shaped(square, jnp.float32), shaped((2...  1.25 us
  transfers between devices with their start and end apart: 22, of which 10 were waited for; matrix products, arithmetic and copies ran while one was open for 1% of the time, Pallas kernels for 17%

profile of v6, /device:TPU:0, one launch (start us, length us, event | category | flops | bytes accessed | tf_op | source)
XLA Modules:
  0.0 59.5 jit_solution(12421625432821577372)
XLA Ops:
  0.6 1.3 %shard_map.92 = (f32[4,128,128]{2,1,0:T(8,128)S(1)}, bf16[2,4,128,128]{3,2,1,0:T(8,128)(2,1)S(1)}) custom-call(bf16[2,64,512]{2,1,0:T(8,128)(2,1)} %k_ref.5, bf16[2,64,512]{2,1,0:T(8,128)(2,1)} %v_ref.5), custom_call_target="tpu_custom_call" | custom-call | tf_op jit(solution)/shard_map/pallas_call | solution.py:123
  1.9 3.0 %collective-permute-start.4 = (bf16[2,4,128,128]{3,2,1,0:T(8,128)(2,1)S(1)}, bf16[2,4,128,128]{3,2,1,0:T(8,128)(2,1)S(1)}, u32[]{:S(2)}, u32[]{:S(2)}) collective-permute-start(bf16[2,4,128,128]{3,2,1,0:T(8,128)(2,1)S(1)} %get-tuple-element.49.a_ref), channel_id=1, source_target_pairs={{0,4},{4,0},{8,12},{12,8},{16,20},{20,16},{24,28},{28,24},{1,5},{5... | collective-permute-start | bytes 786440 | tf_op jit(solution)/shard_map/ppermute | solution.py:72
  4.9 1.5 %collective-permute-start.1 = (bf16[128,1024]{1,0:T(8,128)(2,1)}, bf16[128,1024]{1,0:T(8,128)(2,1)S(1)}, u32[]{:S(2)}, u32[]{:S(2)}) collective-permute-start(bf16[128,1024]{1,0:T(8,128)(2,1)} %bitcast.62), channel_id=1, source_target_pairs={{0,2},{1,3},{2,0},{3,1},{4,6},{5,7},{6,4},{7,5},{8,10},{9,11},{10,... | collective-permute-start | bytes 786440 | tf_op jit(solution)/shard_map/ppermute | solution.py:72
  6.4 0.1 pad_add_fusion.spot_ref
  6.5 4.7 %collective-permute-done.4.b_ref = bf16[2,4,128,128]{3,2,1,0:T(8,128)(2,1)S(1)} collective-permute-done((bf16[2,4,128,128]{3,2,1,0:T(8,128)(2,1)S(1)}, bf16[2,4,128,128]{3,2,1,0:T(8,128)(2,1)S(1)}, u32[]{:S(2)}, u32[]{:S(2)}) %collective-permute-start.4) | collective-permute-done | bytes 262176 | tf_op jit(solution)/shard_map/ppermute | solution.py:72
  11.2 0.1 join_kv.2.a_ref
  11.3 1.9 %collective-permute-start.5 = (bf16[2,4,128,128]{3,2,1,0:T(8,128)(2,1)S(1)}, bf16[2,4,128,128]{3,2,1,0:T(8,128)(2,1)S(1)}, u32[]{:S(2)}, u32[]{:S(2)}) collective-permute-start(bf16[2,4,128,128]{3,2,1,0:T(8,128)(2,1)S(1)} %join_kv.2.a_ref), channel_id=1, source_target_pairs={{0,8},{4,12},{8,0},{12,4},{16,24},{20,28},{24,16},{28,20},{1,9},{5... | collective-permute-start | bytes 786440 | tf_op jit(solution)/shard_map/ppermute | solution.py:72
  13.2 2.4 %near.1 = (f32[128,512]{1,0:T(8,128)S(1)}, bf16[128,1024]{1,0:T(8,128)(2,1)S(1)}) custom-call(s32[2]{0:T(128)S(1)} %pad_add_fusion.spot_ref, bf16[512,4096]{1,0:T(8,128)(2,1)} %w_hbm.3, bf16[128,1024]{1,0:T(8,128)(2,1)} %bitcast.64), custom_call_target="tpu_custom_call" | custom-call | flops 3300000000 | tf_op jit(solution)/shard_map/near/pallas_call | solution.py:162
  15.5 0.6 quarter.1
  16.2 1.6 %collective-permute-start.3 = (bf16[4,32,512]{2,1,0:T(8,128)(2,1)S(1)}, bf16[4,32,512]{2,1,0:T(8,128)(2,1)S(1)}, u32[]{:S(2)}, u32[]{:S(2)}) collective-permute-start(bf16[4,32,512]{2,1,0:T(8,128)(2,1)S(1)} %get-tuple-element.57), channel_id=1, source_target_pairs={{0,4},{4,0},{8,12},{12,8},{16,20},{20,16},{24,28},{28,24},{1,5},{5... | collective-permute-start | bytes 393224 | tf_op jit(solution)/shard_map/ppermute | solution.py:72
  17.7 1.1 %collective-permute-done.5.b_ref = bf16[2,4,128,128]{3,2,1,0:T(8,128)(2,1)S(1)} collective-permute-done((bf16[2,4,128,128]{3,2,1,0:T(8,128)(2,1)S(1)}, bf16[2,4,128,128]{3,2,1,0:T(8,128)(2,1)S(1)}, u32[]{:S(2)}, u32[]{:S(2)}) %collective-permute-start.5) | collective-permute-done | bytes 262176 | tf_op jit(solution)/shard_map/ppermute | solution.py:72
  18.9 0.1 join_kv.3
  18.9 2.5 %collective-permute-start.6 = (bf16[4,128,128]{2,1,0:T(8,128)(2,1)S(1)}, bf16[4,128,128]{2,1,0:T(8,128)(2,1)S(1)}, u32[]{:S(2)}, u32[]{:S(2)}) collective-permute-start(bf16[4,128,128]{2,1,0:T(8,128)(2,1)S(1)} %fusion.8), channel_id=1, source_target_pairs={{0,16},{4,20},{8,24},{12,28},{16,0},{20,4},{24,8},{28,12},{1,17},{... | collective-permute-start | bytes 393224 | tf_op jit(solution)/shard_map/ppermute | solution.py:72
  21.5 0.0 copy-start
  21.5 0.0 copy-start.1
  21.6 3.0 %far.1 = (f32[128,512]{1,0:T(8,128)S(1)}, bf16[4,512,1024]{2,1,0:T(8,128)(2,1)S(1)}) custom-call(s32[2]{0:T(128)S(1)} %pad_add_fusion.spot_ref, bf16[512,4096]{1,0:T(8,128)(2,1)} %w_hbm.3, f32[128,512]{1,0:T(8,128)S(1)} %get-tuple-element.51.before_ref, bf16[128,1024]{1,0:T(8,128)(2,1)S(1)} %collective-permute-done.refs_0_.refs_1_, ...), custom_call_target="tpu_custom_call" | custom-call | flops 11000000 | tf_op jit(solution)/shard_map/far/pallas_call | solution.py:191
  24.7 1.7 %collective-permute-start.7 = (bf16[2,2,32,512]{3,2,1,0:T(8,128)(2,1)S(1)}, bf16[2,2,32,512]{3,2,1,0:T(8,128)(2,1)S(1)}, u32[]{:S(2)}, u32[]{:S(2)}) collective-permute-start(bf16[2,2,32,512]{3,2,1,0:T(8,128)(2,1)S(1)} %fusion.6), channel_id=1, source_target_pairs={{0,8},{4,12},{8,0},{12,4},{16,24},{20,28},{24,16},{28,20},{1,9},{5... | collective-permute-start | bytes 393224 | tf_op jit(solution)/shard_map/ppermute | solution.py:72
  26.3 0.9 %collective-permute-done.6 = bf16[4,128,128]{2,1,0:T(8,128)(2,1)S(1)} collective-permute-done((bf16[4,128,128]{2,1,0:T(8,128)(2,1)S(1)}, bf16[4,128,128]{2,1,0:T(8,128)(2,1)S(1)}, u32[]{:S(2)}, u32[]{:S(2)}) %collective-permute-start.6) | collective-permute-done | bytes 131104 | tf_op jit(solution)/shard_map/ppermute | solution.py:72
  27.2 0.1 add_select_fusion.4
  27.3 0.8 %forward.1 = (bf16[2,4,128,128]{3,2,1,0:T(8,128)(2,1)S(1)}, bf16[128,512]{1,0:T(8,128)(2,1)S(1)}, bf16[2,64,512]{2,1,0:T(8,128)(2,1)S(1)}, f32[4,128,128]{2,1,0:T(8,128)S(1)}, bf16[2,4,128,128]{3,2,1,0:T(8,128)(2,1)S(1)}) custom-call(bf16[2,64,512]{2,1,0:T(8,128)(2,1)S(1)} %copy-done.2, bf16[2,64,512]{2,1,0:T(8,128)(2,1)S(1)} %copy-done, ...), custom_call_target="tpu_custom_call" | custom-call | flops 11000000 | tf_op jit(solution)/shard_map/forward/pallas_call | solution.py:84
  28.1 0.2 collective-permute-start.11
  28.4 3.0 %collective-permute-start.15 = (bf16[128,512]{1,0:T(8,128)(2,1)S(1)}, bf16[128,512]{1,0:T(8,128)(2,1)S(1)}, u32[]{:S(2)}, u32[]{:S(2)}) collective-permute-start(bf16[128,512]{1,0:T(8,128)(2,1)S(1)} %get-tuple-element.81.hidden_ref.refs_0_), channel_id=1, source_target_pairs={{0,8},{4,12},{8,0},{12,4},{16,24},{20,28},{24,16},{28,20},{1,9},{5... | collective-permute-start | bytes 393224 | tf_op jit(solution)/shard_map/ppermute | solution.py:72
  31.4 0.4 project.3
  31.8 0.1 collective-permute-start.13
  31.9 2.6 %collective-permute-start.8 = (bf16[2,4,128,128]{3,2,1,0:T(8,128)(2,1)S(1)}, bf16[2,4,128,128]{3,2,1,0:T(8,128)(2,1)S(1)}, u32[]{:S(2)}, u32[]{:S(2)}) collective-permute-start(bf16[2,4,128,128]{3,2,1,0:T(8,128)(2,1)S(1)} %get-tuple-element.70.a_ref), channel_id=1, source_target_pairs={{0,4},{4,0},{8,12},{12,8},{16,20},{20,16},{24,28},{28,24},{1,5},{5... | collective-permute-start | bytes 786440 | tf_op jit(solution)/shard_map/ppermute | solution.py:72
  34.5 0.1 collective-permute-start.10
  34.6 1.1 %collective-permute-done.11.refs_0_ = bf16[128,512]{1,0:T(8,128)(2,1)S(1)} collective-permute-done((bf16[128,512]{1,0:T(8,128)(2,1)S(1)}, bf16[128,512]{1,0:T(8,128)(2,1)S(1)}, u32[]{:S(2)}, u32[]{:S(2)}) %collective-permute-start.11) | collective-permute-done | bytes 131104 | tf_op jit(solution)/shard_map/ppermute | solution.py:72
  35.7 0.0 collective-permute-start.12
  35.8 2.2 %inside.1 = (bf16[2,64,512]{2,1,0:T(8,128)(2,1)}, f32[2,64,512]{2,1,0:T(8,128)S(1)}, f32[2,64,512]{2,1,0:T(8,128)S(1)}) custom-call(bf16[2,64,512]{2,1,0:T(8,128)(2,1)S(1)} %copy-done.2, bf16[2,64,512]{2,1,0:T(8,128)(2,1)S(1)} %copy-done, bf16[2,64,512]{2,1,0:T(8,128)(2,1)S(1)} %copy-done.1, bf16[2,64,512]{2,1,0:T(8,128)(2,1)S(1)} %get-tuple-element.62.g_ref, ...), custom_call_target="tpu_custom_call" | custom-call | flops 5500000256 | tf_op jit(solution)/shard_map/inside/pallas_call | solution.py:84
  38.0 0.4 project.2
  38.5 0.5 collective-permute-start.17
  39.0 2.6 %collective-permute-done.8.b_ref = bf16[2,4,128,128]{3,2,1,0:T(8,128)(2,1)S(1)} collective-permute-done((bf16[2,4,128,128]{3,2,1,0:T(8,128)(2,1)S(1)}, bf16[2,4,128,128]{3,2,1,0:T(8,128)(2,1)S(1)}, u32[]{:S(2)}, u32[]{:S(2)}) %collective-permute-start.8) | collective-permute-done | bytes 262176 | tf_op jit(solution)/shard_map/ppermute | solution.py:72
  41.6 0.1 join_qg.2.a_ref
  41.7 0.1 collective-permute-start.9
  41.8 1.8 %collective-permute-done.12.refs_1_ = bf16[128,512]{1,0:T(8,128)(2,1)S(1)} collective-permute-done((bf16[128,512]{1,0:T(8,128)(2,1)S(1)}, bf16[128,512]{1,0:T(8,128)(2,1)S(1)}, u32[]{:S(2)}, u32[]{:S(2)}) %collective-permute-start.12) | collective-permute-done | bytes 131104 | tf_op jit(solution)/shard_map/ppermute | solution.py:72
  43.6 1.6 %collective-permute-start.20 = (bf16[8,32,512]{2,1,0:T(8,128)(2,1)S(1)}, bf16[8,32,512]{2,1,0:T(8,128)(2,1)S(1)}, u32[]{:S(2)}, u32[]{:S(2)}) collective-permute-start(bf16[8,32,512]{2,1,0:T(8,128)(2,1)S(1)} %get-tuple-element.75), channel_id=1, source_target_pairs={{0,2},{1,3},{2,0},{3,1},{4,6},{5,7},{6,4},{7,5},{8,10},{9,11},{10,... | collective-permute-start | bytes 786440 | tf_op jit(solution)/shard_map/ppermute | solution.py:72
  45.3 0.2 convert_add_fusion
  45.5 0.6 collective-permute-start.16
  46.1 2.6 %collective-permute-done.9.b_ref = bf16[2,4,128,128]{3,2,1,0:T(8,128)(2,1)S(1)} collective-permute-done((bf16[2,4,128,128]{3,2,1,0:T(8,128)(2,1)S(1)}, bf16[2,4,128,128]{3,2,1,0:T(8,128)(2,1)S(1)}, u32[]{:S(2)}, u32[]{:S(2)}) %collective-permute-start.9) | collective-permute-done | bytes 262176 | tf_op jit(solution)/shard_map/ppermute | solution.py:72
  48.7 1.0 %collective-permute-start.18 = (bf16[2,128,512]{2,1,0:T(8,128)(2,1)S(1)}, bf16[2,128,512]{2,1,0:T(8,128)(2,1)S(1)}, u32[]{:S(2)}, u32[]{:S(2)}) collective-permute-start(bf16[2,128,512]{2,1,0:T(8,128)(2,1)S(1)} %stack.47.refs_2_), channel_id=1, source_target_pairs={{0,4},{4,0},{8,12},{12,8},{16,20},{20,16},{24,28},{28,24},{1,5},{5... | collective-permute-start | bytes 786440 | tf_op jit(solution)/shard_map/ppermute | solution.py:72
  49.7 0.1 join_qg.3
  49.8 0.8 %collective-permute-start.14 = (bf16[4,128,128]{2,1,0:T(8,128)(2,1)S(1)}, bf16[4,128,128]{2,1,0:T(8,128)(2,1)S(1)}, u32[]{:S(2)}, u32[]{:S(2)}) collective-permute-start(bf16[4,128,128]{2,1,0:T(8,128)(2,1)S(1)} %fusion.7), channel_id=1, source_target_pairs={{0,16},{4,20},{8,24},{12,28},{16,0},{20,4},{24,8},{28,12},{1,17},{... | collective-permute-start | bytes 393224 | tf_op jit(solution)/shard_map/ppermute | solution.py:72
  50.6 1.5 %collective-permute-done.20 = bf16[8,32,512]{2,1,0:T(8,128)(2,1)S(1)} collective-permute-done((bf16[8,32,512]{2,1,0:T(8,128)(2,1)S(1)}, bf16[8,32,512]{2,1,0:T(8,128)(2,1)S(1)}, u32[]{:S(2)}, u32[]{:S(2)}) %collective-permute-start.20) | collective-permute-done | bytes 262176 | tf_op jit(solution)/shard_map/ppermute | solution.py:72
  52.2 3.8 %collective-permute-done.16.got_ref = bf16[128,1024]{1,0:T(8,128)(2,1)S(1)} collective-permute-done((bf16[128,1024]{1,0:T(8,128)(2,1)S(1)}, bf16[128,1024]{1,0:T(8,128)(2,1)S(1)}, u32[]{:S(2)}, u32[]{:S(2)}) %collective-permute-start.16) | collective-permute-done | bytes 262176 | tf_op jit(solution)/shard_map/ppermute | solution.py:72
  56.0 0.6 collective-permute-done.14
  56.6 0.1 add_select_fusion
  56.7 0.1 pad_maximum_fusion.refs_4_
  56.9 2.6 %last.1 = (bf16[2,64,512]{2,1,0:T(8,128)(2,1)}, bf16[2,64,512]{2,1,0:T(8,128)(2,1)}, bf16[128,1024]{1,0:T(8,128)(2,1)}, f32[512,512]{1,0:T(8,128)}) custom-call(s32[2]{0:T(128)S(1)} %pad_add_fusion.spot_ref, bf16[2,64,512]{2,1,0:T(8,128)(2,1)S(1)} %copy-done, bf16[2,64,512]{2,1,0:T(8,128)(2,1)S(1)} %copy-done.1, ...), custom_call_target="tpu_custom_call" | custom-call | flops 1100000000 | tf_op jit(solution)/shard_map/last/pallas_call | solution.py:296
  (34 shorter events, 0.4 us)
Async XLA Ops:
  1.9 9.3 %collective-permute-start.4 = (bf16[2,4,128,128]{3,2,1,0:T(8,128)(2,1)S(1)}, bf16[2,4,128,128]{3,2,1,0:T(8,128)(2,1)S(1)}, u32[]{:S(2)}, u32[]{:S(2)}) collective-permute-start(bf16[2,4,128,128]{3,2,1,0:T(8,128)(2,1)S(1)} %get-tuple-element.49.a_ref), channel_id=1, source_target_pairs={{0,4},{4,0},{8,12},{12,8},{16,20},{20,16},{24,28},{28,24},{1,5},{5... | collective-permute-start | bytes 786440 | tf_op jit(solution)/shard_map/ppermute | solution.py:72
  4.9 8.2 %collective-permute-start.1 = (bf16[128,1024]{1,0:T(8,128)(2,1)}, bf16[128,1024]{1,0:T(8,128)(2,1)S(1)}, u32[]{:S(2)}, u32[]{:S(2)}) collective-permute-start(bf16[128,1024]{1,0:T(8,128)(2,1)} %bitcast.62), channel_id=1, source_target_pairs={{0,2},{1,3},{2,0},{3,1},{4,6},{5,7},{6,4},{7,5},{8,10},{9,11},{10,... | collective-permute-start | bytes 786440 | tf_op jit(solution)/shard_map/ppermute | solution.py:72
  6.4 9.1 %collective-permute-start = (bf16[128,1024]{1,0:T(8,128)(2,1)}, bf16[128,1024]{1,0:T(8,128)(2,1)S(1)}, u32[]{:S(2)}, u32[]{:S(2)}) collective-permute-start(bf16[128,1024]{1,0:T(8,128)(2,1)} %bitcast.63), channel_id=1, source_target_pairs={{0,1},{1,0},{2,3},{3,2},{4,5},{5,4},{6,7},{7,6},{8,9},{9,8},{10,11... | collective-permute-start | bytes 786440 | tf_op jit(solution)/shard_map/ppermute | solution.py:72
  11.3 7.6 %collective-permute-start.5 = (bf16[2,4,128,128]{3,2,1,0:T(8,128)(2,1)S(1)}, bf16[2,4,128,128]{3,2,1,0:T(8,128)(2,1)S(1)}, u32[]{:S(2)}, u32[]{:S(2)}) collective-permute-start(bf16[2,4,128,128]{3,2,1,0:T(8,128)(2,1)S(1)} %join_kv.2.a_ref), channel_id=1, source_target_pairs={{0,8},{4,12},{8,0},{12,4},{16,24},{20,28},{24,16},{28,20},{1,9},{5... | collective-permute-start | bytes 786440 | tf_op jit(solution)/shard_map/ppermute | solution.py:72
  13.2 2.4 %collective-permute-start.2 = (bf16[128,1024]{1,0:T(8,128)(2,1)S(1)}, bf16[128,1024]{1,0:T(8,128)(2,1)S(1)}, u32[]{:S(2)}, u32[]{:S(2)}) collective-permute-start(bf16[128,1024]{1,0:T(8,128)(2,1)S(1)} %collective-permute-done.1.refs_1_.refs_2_), channel_id=1, source_target_pairs={{0,1},{1,0},{2,3},{3,2},{4,5},{5,4},{6,7},{7,6},{8,9},{9,8},{10,11... | collective-permute-start | bytes 786440 | tf_op jit(solution)/shard_map/ppermute | solution.py:72
  16.2 8.5 %collective-permute-start.3 = (bf16[4,32,512]{2,1,0:T(8,128)(2,1)S(1)}, bf16[4,32,512]{2,1,0:T(8,128)(2,1)S(1)}, u32[]{:S(2)}, u32[]{:S(2)}) collective-permute-start(bf16[4,32,512]{2,1,0:T(8,128)(2,1)S(1)} %get-tuple-element.57), channel_id=1, source_target_pairs={{0,4},{4,0},{8,12},{12,8},{16,20},{20,16},{24,28},{28,24},{1,5},{5... | collective-permute-start | bytes 393224 | tf_op jit(solution)/shard_map/ppermute | solution.py:72
  18.9 8.3 %collective-permute-start.6 = (bf16[4,128,128]{2,1,0:T(8,128)(2,1)S(1)}, bf16[4,128,128]{2,1,0:T(8,128)(2,1)S(1)}, u32[]{:S(2)}, u32[]{:S(2)}) collective-permute-start(bf16[4,128,128]{2,1,0:T(8,128)(2,1)S(1)} %fusion.8), channel_id=1, source_target_pairs={{0,16},{4,20},{8,24},{12,28},{16,0},{20,4},{24,8},{28,12},{1,17},{... | collective-permute-start | bytes 393224 | tf_op jit(solution)/shard_map/ppermute | solution.py:72
  21.5 5.8 %copy-start = (bf16[2,64,512]{2,1,0:T(8,128)(2,1)S(1)}, bf16[2,64,512]{2,1,0:T(8,128)(2,1)}, u32[]{:S(2)}) copy-start(bf16[2,64,512]{2,1,0:T(8,128)(2,1)} %k_ref.5) | copy-start | bytes 393220
  21.5 5.8 %copy-start.1 = (bf16[2,64,512]{2,1,0:T(8,128)(2,1)S(1)}, bf16[2,64,512]{2,1,0:T(8,128)(2,1)}, u32[]{:S(2)}) copy-start(bf16[2,64,512]{2,1,0:T(8,128)(2,1)} %v_ref.5) | copy-start | bytes 393220
  21.6 5.8 %copy-start.2 = (bf16[2,64,512]{2,1,0:T(8,128)(2,1)S(1)}, bf16[2,64,512]{2,1,0:T(8,128)(2,1)}, u32[]{:S(2)}) copy-start(bf16[2,64,512]{2,1,0:T(8,128)(2,1)} %q_ref.3) | copy-start | bytes 393220
  24.7 7.2 %collective-permute-start.7 = (bf16[2,2,32,512]{3,2,1,0:T(8,128)(2,1)S(1)}, bf16[2,2,32,512]{3,2,1,0:T(8,128)(2,1)S(1)}, u32[]{:S(2)}, u32[]{:S(2)}) collective-permute-start(bf16[2,2,32,512]{3,2,1,0:T(8,128)(2,1)S(1)} %fusion.6), channel_id=1, source_target_pairs={{0,8},{4,12},{8,0},{12,4},{16,24},{20,28},{24,16},{28,20},{1,9},{5... | collective-permute-start | bytes 393224 | tf_op jit(solution)/shard_map/ppermute | solution.py:72
  28.1 7.6 %collective-permute-start.11 = (bf16[128,512]{1,0:T(8,128)(2,1)S(1)}, bf16[128,512]{1,0:T(8,128)(2,1)S(1)}, u32[]{:S(2)}, u32[]{:S(2)}) collective-permute-start(bf16[128,512]{1,0:T(8,128)(2,1)S(1)} %get-tuple-element.81.hidden_ref.refs_0_), channel_id=1, source_target_pairs={{0,16},{4,20},{8,24},{12,28},{16,0},{20,4},{24,8},{28,12},{1,17},{... | collective-permute-start | bytes 393224 | tf_op jit(solution)/shard_map/ppermute | solution.py:72
  28.4 10.1 %collective-permute-start.15 = (bf16[128,512]{1,0:T(8,128)(2,1)S(1)}, bf16[128,512]{1,0:T(8,128)(2,1)S(1)}, u32[]{:S(2)}, u32[]{:S(2)}) collective-permute-start(bf16[128,512]{1,0:T(8,128)(2,1)S(1)} %get-tuple-element.81.hidden_ref.refs_0_), channel_id=1, source_target_pairs={{0,8},{4,12},{8,0},{12,4},{16,24},{20,28},{24,16},{28,20},{1,9},{5... | collective-permute-start | bytes 393224 | tf_op jit(solution)/shard_map/ppermute | solution.py:72
  31.8 13.5 %collective-permute-start.13 = (bf16[2,128,1024]{2,1,0:T(8,128)(2,1)S(1)}, bf16[2,128,1024]{2,1,0:T(8,128)(2,1)S(1)}, u32[]{:S(2)}, u32[]{:S(2)}) collective-permute-start(bf16[2,128,1024]{2,1,0:T(8,128)(2,1)S(1)} %project.3), channel_id=1, source_target_pairs={{0,1},{1,0},{2,3},{3,2},{4,5},{5,4},{6,7},{7,6},{8,9},{9,8},{10,11... | collective-permute-start | bytes 1572872 | tf_op jit(solution)/shard_map/ppermute | solution.py:72
  31.9 9.7 %collective-permute-start.8 = (bf16[2,4,128,128]{3,2,1,0:T(8,128)(2,1)S(1)}, bf16[2,4,128,128]{3,2,1,0:T(8,128)(2,1)S(1)}, u32[]{:S(2)}, u32[]{:S(2)}) collective-permute-start(bf16[2,4,128,128]{3,2,1,0:T(8,128)(2,1)S(1)} %get-tuple-element.70.a_ref), channel_id=1, source_target_pairs={{0,4},{4,0},{8,12},{12,8},{16,20},{20,16},{24,28},{28,24},{1,5},{5... | collective-permute-start | bytes 786440 | tf_op jit(solution)/shard_map/ppermute | solution.py:72
  34.5 9.1 %collective-permute-start.10 = (bf16[4,32,512]{2,1,0:T(8,128)(2,1)S(1)}, bf16[4,32,512]{2,1,0:T(8,128)(2,1)S(1)}, u32[]{:S(2)}, u32[]{:S(2)}) collective-permute-start(bf16[4,32,512]{2,1,0:T(8,128)(2,1)S(1)} %get-tuple-element.100), channel_id=1, source_target_pairs={{0,16},{4,20},{8,24},{12,28},{16,0},{20,4},{24,8},{28,12},{1,17},{... | collective-permute-start | bytes 393224 | tf_op jit(solution)/shard_map/ppermute | solution.py:72
  35.7 7.9 %collective-permute-start.12 = (bf16[128,512]{1,0:T(8,128)(2,1)S(1)}, bf16[128,512]{1,0:T(8,128)(2,1)S(1)}, u32[]{:S(2)}, u32[]{:S(2)}) collective-permute-start(bf16[128,512]{1,0:T(8,128)(2,1)S(1)} %collective-permute-done.11.refs_0_), channel_id=1, source_target_pairs={{0,8},{4,12},{8,0},{12,4},{16,24},{20,28},{24,16},{28,20},{1,9},{5... | collective-permute-start | bytes 393224 | tf_op jit(solution)/shard_map/ppermute | solution.py:72
  38.5 11.3 %collective-permute-start.17 = (bf16[2,128,512]{2,1,0:T(8,128)(2,1)S(1)}, bf16[2,128,512]{2,1,0:T(8,128)(2,1)S(1)}, u32[]{:S(2)}, u32[]{:S(2)}) collective-permute-start(bf16[2,128,512]{2,1,0:T(8,128)(2,1)S(1)} %stack.46.refs_0_), channel_id=1, source_target_pairs={{0,4},{4,0},{8,12},{12,8},{16,20},{20,16},{24,28},{28,24},{1,5},{5... | collective-permute-start | bytes 786440 | tf_op jit(solution)/shard_map/ppermute | solution.py:72
  41.7 7.0 %collective-permute-start.9 = (bf16[2,4,128,128]{3,2,1,0:T(8,128)(2,1)S(1)}, bf16[2,4,128,128]{3,2,1,0:T(8,128)(2,1)S(1)}, u32[]{:S(2)}, u32[]{:S(2)}) collective-permute-start(bf16[2,4,128,128]{3,2,1,0:T(8,128)(2,1)S(1)} %join_qg.2.a_ref), channel_id=1, source_target_pairs={{0,8},{4,12},{8,0},{12,4},{16,24},{20,28},{24,16},{28,20},{1,9},{5... | collective-permute-start | bytes 786440 | tf_op jit(solution)/shard_map/ppermute | solution.py:72
  43.6 8.4 %collective-permute-start.20 = (bf16[8,32,512]{2,1,0:T(8,128)(2,1)S(1)}, bf16[8,32,512]{2,1,0:T(8,128)(2,1)S(1)}, u32[]{:S(2)}, u32[]{:S(2)}) collective-permute-start(bf16[8,32,512]{2,1,0:T(8,128)(2,1)S(1)} %get-tuple-element.75), channel_id=1, source_target_pairs={{0,2},{1,3},{2,0},{3,1},{4,6},{5,7},{6,4},{7,5},{8,10},{9,11},{10,... | collective-permute-start | bytes 786440 | tf_op jit(solution)/shard_map/ppermute | solution.py:72
  45.2 7.0 %collective-permute-start.19 = (bf16[8,32,512]{2,1,0:T(8,128)(2,1)S(1)}, bf16[8,32,512]{2,1,0:T(8,128)(2,1)S(1)}, u32[]{:S(2)}, u32[]{:S(2)}) collective-permute-start(bf16[8,32,512]{2,1,0:T(8,128)(2,1)S(1)} %get-tuple-element.75), channel_id=1, source_target_pairs={{0,1},{1,0},{2,3},{3,2},{4,5},{5,4},{6,7},{7,6},{8,9},{9,8},{10,11... | collective-permute-start | bytes 786440 | tf_op jit(solution)/shard_map/ppermute | solution.py:72
  45.5 10.5 %collective-permute-start.16 = (bf16[128,1024]{1,0:T(8,128)(2,1)S(1)}, bf16[128,1024]{1,0:T(8,128)(2,1)S(1)}, u32[]{:S(2)}, u32[]{:S(2)}) collective-permute-start(bf16[128,1024]{1,0:T(8,128)(2,1)S(1)} %fusion), channel_id=1, source_target_pairs={{0,2},{1,3},{2,0},{3,1},{4,6},{5,7},{6,4},{7,5},{8,10},{9,11},{10,... | collective-permute-start | bytes 786440 | tf_op jit(solution)/shard_map/ppermute | solution.py:72
  48.7 7.9 %collective-permute-start.18 = (bf16[2,128,512]{2,1,0:T(8,128)(2,1)S(1)}, bf16[2,128,512]{2,1,0:T(8,128)(2,1)S(1)}, u32[]{:S(2)}, u32[]{:S(2)}) collective-permute-start(bf16[2,128,512]{2,1,0:T(8,128)(2,1)S(1)} %stack.47.refs_2_), channel_id=1, source_target_pairs={{0,4},{4,0},{8,12},{12,8},{16,20},{20,16},{24,28},{28,24},{1,5},{5... | collective-permute-start | bytes 786440 | tf_op jit(solution)/shard_map/ppermute | solution.py:72
  49.8 6.8 %collective-permute-start.14 = (bf16[4,128,128]{2,1,0:T(8,128)(2,1)S(1)}, bf16[4,128,128]{2,1,0:T(8,128)(2,1)S(1)}, u32[]{:S(2)}, u32[]{:S(2)}) collective-permute-start(bf16[4,128,128]{2,1,0:T(8,128)(2,1)S(1)} %fusion.7), channel_id=1, source_target_pairs={{0,16},{4,20},{8,24},{12,28},{16,0},{20,4},{24,8},{28,12},{1,17},{... | collective-permute-start | bytes 393224 | tf_op jit(solution)/shard_map/ppermute | solution.py:72
  52.1 4.6 %collective-permute-start.21 = (bf16[8,32,512]{2,1,0:T(8,128)(2,1)S(1)}, bf16[8,32,512]{2,1,0:T(8,128)(2,1)S(1)}, u32[]{:S(2)}, u32[]{:S(2)}) collective-permute-start(bf16[8,32,512]{2,1,0:T(8,128)(2,1)S(1)} %collective-permute-done.20), channel_id=1, source_target_pairs={{0,1},{1,0},{2,3},{3,2},{4,5},{5,4},{6,7},{7,6},{8,9},{9,8},{10,11... | collective-permute-start | bytes 786440 | tf_op jit(solution)/shard_map/ppermute | solution.py:72
